TPU v7x, 128 devices: a whole 4x4x4 slice. The times are simulated.
128 devices in a mesh: gx: 8 (over z_lo, y), gy: 4 (over z_hi, core), gz: 4 (over x).
Axes of the slice: x: 4, y: 4, z: 4 (z_hi: 2, z_lo: 2; z = z_hi * 2 + z_lo), core: 2. Of those that a mesh axis runs over, the one named last changes fastest.
Arguments:
- positions: float32 [16, 4, 4, 3, 32], P('gx', 'gy', 'gz'), may hold values from 0 to 5, as said below
- counts: int32 [16, 4, 4], P('gx', 'gy', 'gz'), may hold values from 1 to 32, as said below
- scalars: bfloat16 [16, 4, 4, 32, 128], P('gx', 'gy', 'gz'), may hold values from -6 to 6
- vectors: bfloat16 [16, 4, 4, 32, 3, 128], P('gx', 'gy', 'gz'), may hold values from -6 to 6
- radial_in: bfloat16 [2, 8, 64], replicated, may hold values from -2 to 2
- radial_bias: float32 [2, 64], replicated, may hold values from -3 to 3
- radial_out: bfloat16 [2, 64, 512], replicated, may hold values from -0.75 to 0.75
- atom_in: bfloat16 [2, 128, 128], replicated, may hold values from -0.5 to 0.5
- atom_bias: float32 [2, 128], replicated, may hold values from -3 to 3
- atom_out: bfloat16 [2, 128, 512], replicated, may hold values from -0.5 to 0.5
- readout_in: bfloat16 [128, 64], replicated, may hold values from -0.5 to 0.5
- readout_out: float32 [64], replicated, may hold values from -0.75 to 0.75
Outputs:
- scalars_out: bfloat16 [16, 4, 4, 32, 128], P('gx', 'gy', 'gz')
- vectors_out: bfloat16 [16, 4, 4, 32, 3, 128], P('gx', 'gy', 'gz')
- energy: float32 [1], replicated
Inputs may be any that keep to these rules, and one draw needn't show every extreme that they name: `counts`: some cell of every draw holds 32 atoms and some other cell one atom. `positions`: the slots of a cell sit on distinct sites of a jittered lattice, so that any two slots, also of neighbouring cells, lie at least 0.5 apart.
All inputs are finite; a program needn't handle non-finite values.
Results may differ from a plain program's by a relative error of at most 0.0075.
Values may be sent and summed in bfloat16 or wider, within the bound.
No kernel may reach another device: no remote copies, remote signals or barrier semaphores. Data moves between devices by JAX's collectives and lax.ppermute only.
A program may use at most 64 MiB of HBM per device.

v0:
```python
import functools
import math

import jax
import jax.numpy as jnp
import numpy as np
from jax import lax
from jax.experimental import pallas as pl
from jax.experimental.pallas import tpu as pltpu
from jax.sharding import PartitionSpec as P

cutoff = 5.0
message_scale = 0.5
slots = 32
chan = 128
hidden = 64
block = 8
room = 2 * slots + block
depth = 80
own_atoms, own_main, own_span = 576, 512, 640
side_atoms, side_main, side_span = 288, 256, 384
f32 = jnp.float32
bf16 = jnp.bfloat16
across = (((1,), (1,)), ((), ()))


def pieces(value):
    high = lax.reduce_precision(value, 8, 7)
    rest = value - high
    middle = lax.reduce_precision(rest, 8, 7)
    low = lax.reduce_precision(rest - middle, 8, 7)
    return high.astype(bf16), middle.astype(bf16), low.astype(bf16)


def dot(a, b):
    return jnp.dot(a, b, preferred_element_type=f32)


def half_silu(y):
    return y + y * jnp.tanh(y)


def iotas(shape):
    return lax.broadcasted_iota(jnp.int32, shape, 0), lax.broadcasted_iota(jnp.int32, shape, 1)


def flag(condition):
    return jnp.where(condition, 1.0, 0.0)


def rows_of(geo):
    row, lane = iotas((8, chan))
    pick = flag((lane == row) | (lane == row + 8) | (lane == row + 16)).astype(bf16)
    return lax.dot_general(pick, geo, across, preferred_element_type=f32)


def columns_of(geo):
    row, lane = iotas((chan, chan))
    pick = flag((lane == row) | (lane + 8 == row) | (lane + 16 == row)).astype(bf16)
    return dot(geo, pick)


def own_table(y):
    row, lane = iotas((own_atoms // 3, chan))
    plane = flag(row >= 3 * slots)
    row = jnp.where(row >= 3 * slots, row - 3 * slots, row)
    z = flag(row >= slots) + flag(row >= 2 * slots) - 1.0
    table = jnp.where(lane == 4, plane * cutoff, 0.0) + jnp.where(lane == 6, z * cutoff, 0.0)
    table += jnp.where(lane == 5, (y - 1) * cutoff, 0.0)
    if y == 1:
        name = (row - slots + 1).astype(f32) + plane * slots
        table += jnp.where((lane == 7) & (z == 0.0), name, 0.0)
    return table.astype(bf16)


def side_table():
    row, lane = iotas((side_atoms, chan))
    y = flag(row >= 3 * slots) + flag(row >= 6 * slots) - 1.0
    row = row.astype(f32) - (y + 1.0) * (3 * slots)
    z = flag(row >= slots) + flag(row >= 2 * slots) - 1.0
    table = jnp.where(lane == 5, y * cutoff, 0.0) + jnp.where(lane == 6, z * cutoff, 0.0)
    return table.astype(bf16)


def compaction(live, span):
    atoms = live.shape[0]
    ranks = []
    total = jnp.zeros((1, 1), f32)
    for at in range(0, atoms, chan):
        part = live[at : at + chan]
        row, lane = iotas((part.shape[0], part.shape[0]))
        before = jnp.sum(jnp.where(row < lane, part, 0.0), axis=0, keepdims=True)
        own = jnp.sum(jnp.where(row == lane, part, 0.0), axis=0, keepdims=True)
        ranks.append(jnp.where(own > 0.5, before + total, -1.0))
        total = total + jnp.sum(part, axis=0, keepdims=True)
    rank = jnp.concatenate(ranks, axis=1)
    row = lax.broadcasted_iota(jnp.int32, (span, atoms), 0).astype(f32)
    return flag(row == rank).astype(bf16), total


def geometry(row, mine, number, shift, pairs_ref, at):
    dist2 = None
    disp = []
    for k in range(3):
        offset = row[4 + k : 5 + k] + shift if k == 0 else row[4 + k : 5 + k]
        d = (row[k : k + 1] + offset) - mine[:, k : k + 1]
        disp.append(d)
        dist2 = d * d if k == 0 else dist2 + d * d
    live = row[3:4]
    itself = flag(row[7:8] == number.astype(f32))
    dist = jnp.sqrt(dist2 + itself + (1.0 - live))
    smooth = jnp.where(dist < cutoff, 0.5 * (jnp.cos(math.pi * dist / cutoff) + 1.0), 0.0)
    weight = smooth * live * (1.0 - itself)
    scaled = weight / dist
    pairs_ref[8, at, :] = weight
    for k in range(3):
        pairs_ref[9 + k, at, :] = scaled * disp[k]
    sharp = 0.5 * (7.0 / cutoff) ** 2
    for k in range(8):
        away = dist - k * (cutoff / 7.0)
        pairs_ref[k, at, :] = jnp.exp(-sharp * (away * away))


def features(layer, x, part, weights, feats):
    _, _, ain_ref, abias_ref, aout_ref = weights
    s = x[:, :chan]
    bias = abias_ref[layer : layer + 1, :]
    hid = half_silu(0.5 * (dot(s, ain_ref[layer]) + bias)).astype(bf16)
    gates = dot(hid, aout_ref[layer]).astype(bf16)
    ga, gb = gates[:, :chan], gates[:, chan : 2 * chan]
    gc, gg = gates[:, 2 * chan : 3 * chan], gates[:, 3 * chan :]
    vec = [x[:, (k + 1) * chan : (k + 2) * chan] for k in range(3)]
    feats[0][part, :] = jnp.concatenate([ga] + [gb * v for v in vec], axis=1)
    for k in range(3):
        feats[1 + k][part, :] = jnp.concatenate([gc, gg * vec[k]], axis=1)


def messages(layer, count, place, window, weights, pairs_ref, feats, edges, delta):
    rin_ref, rout_ref = weights[:2]
    width = window.stop - window.start
    even, odd = edges[:4], edges[4:]

    def rows_at(b):
        return pl.ds(pl.multiple_of(place(b)[0], block), block)

    def hidden_of(b):
        slab = pairs_ref[0:8, rows_at(b), window].reshape(8 * block, width)
        slab = jnp.concatenate([slab, jnp.ones((depth - 8 * block, width), f32)], axis=0)
        return dot(rin_ref[layer], slab.astype(bf16)), pairs_ref[8:12, rows_at(b), window]

    def edge(r, y, w, out):
        part = slice(r * hidden, (r + 1) * hidden)
        s = half_silu(y[part]).astype(bf16).reshape(4, 16, width)
        for g in range(4):
            line = jnp.broadcast_to(w[g][r : r + 1, :], (16, width)).astype(bf16)
            out[g][part, :width] = (s * line[None]).reshape(hidden, width)

    def product(n, used, atoms):
        if n < 2:
            return dot(used[0][:, :width], feats[0][atoms, 2 * n * chan : 2 * (n + 1) * chan])
        return dot(used[n - 1][:, :width], feats[n - 1][atoms, :])

    def gather(n, result, radial, sums):
        groups = ((0, 1), (1, 1), (2, 3), (2, 3), (2, 3))[n]
        targets = ((0, 1), (2, 3), (1, 0), (2, 0), (3, 0))[n]
        for half in range(2):
            value = result[:, half * chan : (half + 1) * chan].reshape(block, hidden, chan)
            value = jnp.sum(value * radial[groups[half]], axis=1)
            t = targets[half]
            sums[t] = value if sums[t] is None else sums[t] + value

    def step(b, used, following):
        radial = [rout_ref[layer, :, g * chan : (g + 1) * chan].astype(f32)[None] for g in range(4)]
        sums = [None] * 4
        atoms = pl.ds(pl.multiple_of(place(b)[1], chan), width)
        if following is not None:
            y, w = hidden_of(b + 1)
        made, previous = 0, None
        for n in range(5):
            result = product(n, used, atoms)
            while following is not None and made < block and made * 5 < (n + 1) * block:
                edge(made, y, w, following)
                made += 1
            if n > 0:
                gather(n - 1, previous, radial, sums)
            previous = result
        gather(4, previous, radial, sums)
        for g in range(4):
            delta[rows_at(b), g * chan : (g + 1) * chan] += sums[g]

    y, w = hidden_of(0)
    for r in range(block):
        edge(r, y, w, even)

    def two_steps(t, carry):
        step(2 * t, even, odd)
        step(2 * t + 1, odd, even)
        return carry

    lax.fori_loop(0, count // 2, two_steps, 0)

    @pl.when(count % 2 == 1)
    def _():
        step(count - 1, even, None)


def own_kernel(layer, *refs):
    counts_ref, low, middle, high = refs[:4]
    weights = refs[4:9]
    refs = refs[9:]
    if layer == 0:
        delta, pairs_out, order_out, more = refs[:4]
        refs = refs[4:]
        pairs, order, done = refs[12:]
    else:
        pairs, order, more, delta = refs[:4]
        refs = refs[4:]
    feats, edges = refs[:4], refs[4:12]
    parts = [ref[...].reshape(own_atoms // 3, -1) for ref in (low, middle, high)]
    third = own_atoms // 3
    if layer == 0:
        geo = [p[:, 4 * chan :] + own_table(n) for n, p in enumerate(parts)]
        geo = jnp.concatenate(geo, axis=0)
        order[...], total = compaction(geo[:, 3:4].astype(f32), own_span)
        row = rows_of(dot(order[...], geo).astype(bf16))
        more[0] = jnp.where(jnp.sum(total) > own_main + 0.5, 1, 0)
        first = counts_ref[0]
        mine = columns_of(
            jnp.concatenate([middle[q, 1][:, 4 * chan :] for q in range(2)], axis=0)
        )
        place = lax.broadcasted_iota(jnp.int32, (2 * slots, 1), 0)
        moved = pltpu.roll(mine, lax.rem(first + slots, 2 * slots), 0)
        mine = jnp.where(place < first, mine, moved)
        number = jnp.where(place < first, place + 1, place - first + (slots + 1))
        shift = jnp.where(place < first, 0.0, -cutoff)
        geometry(row, mine, number, shift, pairs, slice(0, 2 * slots))
        keep = [
            pltpu.make_async_copy(pairs, pairs_out, done.at[0]),
            pltpu.make_async_copy(order, order_out, done.at[1]),
        ]
        for copy in keep:
            copy.start()

    def gathered(part):
        x = None
        for n in range(3):
            y = dot(order[part, n * third : (n + 1) * third], parts[n][:, : 4 * chan])
            x = y if n == 0 else x + y
        features(layer, x.astype(bf16), part, weights, feats)

    delta[...] = jnp.zeros_like(delta)
    main, rest = slice(0, own_main), slice(own_main, own_span)
    count = (counts_ref[0] + counts_ref[1] + block - 1) // block

    def add(part):
        gathered(part)
        messages(
            layer,
            count,
            lambda b: (b * block, part.start),
            part,
            weights,
            pairs,
            feats,
            edges,
            delta,
        )

    add(main)

    @pl.when(more[0] > 0)
    def _():
        add(rest)

    if layer == 0:
        for copy in keep:
            copy.wait()


def side_kernel(layer, last, *refs):
    counts_ref, low, high, own_ref, before = refs[:5]
    weights = refs[5:10]
    refs = refs[10:]
    if last:
        read_in_ref, read_out_ref = refs[:2]
        refs = refs[2:]
    if layer > 0:
        (pairs, order, more), refs = refs[:3], refs[3:]
    if last:
        (scalar_ref, vector_ref, energy_ref), refs = refs[:3], refs[3:]
    else:
        state_ref, refs = refs[0], refs[1:]
    if layer == 0:
        (pairs, order, more), refs = refs[:3], refs[3:]
    feats, edges, delta = refs[:4], refs[4:12], refs[12]
    delta[...] = jnp.zeros_like(delta)
    main, rest = slice(0, side_main), slice(side_main, side_span)
    atoms = [ref[...].reshape(side_atoms, -1) for ref in (low, high)]
    if layer == 0:
        total = []
        for q in range(2):
            geo = atoms[q][:, 4 * chan :] + side_table()
            order[q], number = compaction(geo[:, 3:4].astype(f32), side_span)
            total.append(jnp.sum(number))
            row = rows_of(dot(order[q], geo).astype(bf16))
            mine = columns_of(own_ref[q][:, 4 * chan :])
            at = slice(q * slots, (q + 1) * slots)
            number = lax.broadcasted_iota(jnp.int32, (slots, 1), 0) + (q * slots + 1)
            geometry(row, mine, number, (-cutoff, cutoff)[q], pairs, at)
        more[0] = jnp.where(jnp.maximum(total[0], total[1]) > side_main + 0.5, 1, 0)
    below = (counts_ref[0] + block - 1) // block
    above = (counts_ref[1] + block - 1) // block

    def add(part):
        for q in range(2):
            x = dot(order[q, part, :], atoms[q][:, : 4 * chan])
            rows = slice(q * side_span + part.start, q * side_span + part.stop)
            features(layer, x.astype(bf16), rows, weights, feats)

        def place(b):
            q = jnp.where(b >= below, 1, 0)
            return b * block + q * (slots - below * block), q * side_span + part.start

        messages(layer, below + above, place, part, weights, pairs, feats, edges, delta)

    add(main)

    @pl.when(more[0] > 0)
    def _():
        add(rest)

    slot = lax.broadcasted_iota(jnp.int32, (2 * slots, 1), 0)
    limit = jnp.where(slot < slots, counts_ref[0], counts_ref[1] + slots)
    live = flag(slot < limit)
    mine = own_ref[...].reshape(2 * slots, -1)[:, : 4 * chan].astype(f32)
    packed = before[0 : 2 * slots, :]
    moved = pltpu.roll(packed, slots - counts_ref[0], 0)
    change = delta[0 : 2 * slots, :] + jnp.where(slot < slots, packed, moved)
    state = ((mine + message_scale * change) * live).astype(bf16)
    if not last:
        state_ref[...] = state
    else:
        for q in range(2):
            at = slice(q * slots, (q + 1) * slots)
            scalar_ref[q] = state[at, :chan]
            for k in range(3):
                vector_ref[q, k] = state[at, (k + 1) * chan : (k + 2) * chan]
        x = dot(state[:, :chan], read_in_ref[...])
        each = half_silu(0.5 * x) * read_out_ref[...] * live
        energy_ref[...] = jnp.broadcast_to(jnp.sum(each, keepdims=True), energy_ref.shape)


vmem = pl.BlockSpec(memory_space=pltpu.VMEM)
smem = pl.BlockSpec(memory_space=pltpu.SMEM)
hbm = pl.BlockSpec(memory_space=pltpu.HBM)


def scratch(rows, main):
    return [
        pltpu.VMEM((rows, 4 * chan), bf16),
        *[pltpu.VMEM((rows, 2 * chan), bf16)] * 3,
        *[pltpu.VMEM((block * hidden, main), bf16)] * 8,
    ]


def cost(atoms):
    return pl.CostEstimate(
        flops=2 * 2 * slots * atoms * 81920, bytes_accessed=4000000, transcendentals=4000000
    )


params = pltpu.CompilerParams(vmem_limit_bytes=24 * 1024 * 1024)
delta_shape = jax.ShapeDtypeStruct((room, 4 * chan), f32)


def kept_shapes(span, order):
    return (
        jax.ShapeDtypeStruct((12, room, span), f32),
        jax.ShapeDtypeStruct(order, bf16),
        jax.ShapeDtypeStruct((2,), jnp.int32),
    )


kept_specs = (vmem, vmem, smem)


def own_call(layer, counts, ys, weights, kept):
    operands = [counts, *ys, *weights]
    specs = [smem] + [vmem] * (len(operands) - 1)
    shapes, outs = (delta_shape,), (vmem,)
    held = scratch(own_span, own_main)
    if layer == 0:
        kept_out = kept_shapes(own_span, (own_span, own_atoms))
        shapes += tuple(pltpu.HBM(k.shape, k.dtype) for k in kept_out[:2]) + kept_out[2:]
        outs += (hbm, hbm, smem)
        held += [pltpu.VMEM(k.shape, k.dtype) for k in kept_out[:2]]
        held += [pltpu.SemaphoreType.DMA((2,))]
    else:
        operands += kept
        specs += kept_specs
    return pl.pallas_call(
        functools.partial(own_kernel, layer),
        out_shape=shapes,
        in_specs=specs,
        out_specs=outs,
        scratch_shapes=held,
        compiler_params=params,
        cost_estimate=cost(own_atoms),
        name=f"own_part_{layer}",
    )(*operands)


def side_call(layer, last, counts, low, high, own, delta, weights, readout, kept):
    operands = [counts, low, high, own, delta, *weights]
    specs = [smem] + [vmem] * (len(operands) - 1)
    shapes, outs = (jax.ShapeDtypeStruct((2 * slots, 4 * chan), bf16),), (vmem,)
    if last:
        operands += readout
        specs += [vmem] * 2
        shapes = (
            jax.ShapeDtypeStruct((2, slots, chan), bf16),
            jax.ShapeDtypeStruct((2, 3, slots, chan), bf16),
            jax.ShapeDtypeStruct((chan, chan), f32),
        )
        outs = (vmem,) * 3
    if layer == 0:
        shapes += kept_shapes(side_span, (2, side_span, side_atoms))
        outs += kept_specs
    else:
        operands += kept
        specs += kept_specs
    return pl.pallas_call(
        functools.partial(side_kernel, layer, last),
        out_shape=shapes,
        in_specs=specs,
        out_specs=outs,
        scratch_shapes=scratch(2 * side_span, side_main) + [pltpu.VMEM(delta_shape.shape, f32)],
        compiler_params=params,
        cost_estimate=cost(side_atoms),
        name=f"side_part_{layer}",
    )(*operands)


def pack_kernel(counts_in, position_in, scalar_in, vector_in, out_ref, counts_ref, place, done):
    copies = [(counts_in, counts_ref), (position_in, place)]
    for q in range(2):
        copies.append((scalar_in.at[q], out_ref.at[q, :, pl.ds(0, chan)]))
        for k in range(3):
            at = pl.ds((k + 1) * chan, chan)
            copies.append((vector_in.at[q, k], out_ref.at[q, :, at]))
    copies = [pltpu.make_async_copy(*c, done.at[n]) for n, c in enumerate(copies)]
    for copy in copies:
        copy.start()
    for copy in copies:
        copy.wait()
    row, lane = iotas((2, slots))
    live = flag(lane < jnp.where(row == 0, counts_ref[0], counts_ref[1]))
    rest = jnp.concatenate([place[q, k] for k in range(3) for q in range(2)] + [live], axis=0)
    addends = []
    for _ in range(3):
        addends.append(rest.astype(bf16).astype(f32))
        rest = rest - addends[-1]
    addends = jnp.concatenate(addends, axis=0).astype(bf16)
    row, lane = iotas((24, chan))
    target = (row // 8) * 8 + (row % 8) // 2
    for q in range(2):
        spread = flag((lane == target) & (row % 2 == q)).astype(bf16)
        geo = lax.dot_general(
            addends, spread, (((0,), (0,)), ((), ())), preferred_element_type=f32
        )
        out_ref[q, :, 4 * chan :] = geo.astype(bf16)


def pack_call(*operands):
    operands = [pltpu.with_memory_space_constraint(x, pltpu.HBM) for x in operands]
    return pl.pallas_call(
        pack_kernel,
        out_shape=jax.ShapeDtypeStruct((2, slots, 5 * chan), bf16),
        in_specs=[hbm] * 4,
        out_specs=vmem,
        scratch_shapes=[
            pltpu.SMEM((2,), jnp.int32),
            pltpu.VMEM((2, 3, 1, slots), f32),
            pltpu.SemaphoreType.DMA((10,)),
        ],
        compiler_params=pltpu.CompilerParams(vmem_limit_bytes=4 * 1024 * 1024),
        name="pack",
    )(*operands)


def shifted(value, axis, step):
    count = lax.axis_size(axis)
    return lax.ppermute(value, axis, [((i + step) % count, i) for i in range(count)])


def radial_rows(radial_in, radial_bias):
    layers = radial_in.shape[0]
    eye = jnp.asarray(np.eye(block) * 0.5, bf16)
    spread = radial_in.transpose(0, 2, 1)[:, None, :, :, None] * eye[:, None, None, :]
    spread = spread.reshape(layers, block * hidden, 8 * block)
    bias = jnp.stack([p * jnp.asarray(0.5, bf16) for p in pieces(radial_bias)], axis=2)
    bias = jnp.broadcast_to(bias[:, None], (layers, block, hidden, 3))
    bias = bias.reshape(layers, block * hidden, 3)
    return jnp.pad(
        jnp.concatenate([spread, bias], axis=2), ((0, 0), (0, 0), (0, depth - 8 * block - 3))
    )


def on_device(
    positions,
    counts,
    scalars,
    vectors,
    radial_in,
    radial_bias,
    radial_out,
    atom_in,
    atom_bias,
    atom_out,
    readout_in,
    readout_out,
):
    counts = counts.reshape(2)
    own = pack_call(
        counts,
        positions.reshape(2, 3, 1, slots),
        scalars.reshape(2, slots, chan),
        vectors.reshape(2, slots, 3, chan).transpose(0, 2, 1, 3),
    )
    layers = radial_in.shape[0]
    own_kept = side_kept = ()
    for layer in range(layers):
        last = layer == layers - 1
        y = jnp.stack([shifted(own, "gz", -1), own, shifted(own, "gz", 1)], axis=1)
        if layer == 0:
            y, radial_in, radial_bias = lax.optimization_barrier((y, radial_in, radial_bias))
            rin = radial_rows(radial_in, radial_bias)
            weights = [rin, radial_out, atom_in, atom_bias, atom_out]
        ys = [shifted(y, "gy", -1), y, shifted(y, "gy", 1)]
        low = shifted(jnp.stack([v[1] for v in ys]), "gx", -1)
        high = shifted(jnp.stack([v[0] for v in ys]), "gx", 1)
        delta, *kept = own_call(layer, counts, ys, weights, own_kept)
        own_kept = own_kept or kept
        readout = [readout_in, readout_out[None, :]]
        state, *kept = side_call(
            layer, last, counts, low, high, own, delta, weights, readout, side_kept
        )
        if last:
            vector_state, energy = kept
        else:
            side_kept = side_kept or kept
            own = state.reshape(2, slots, 4 * chan)
    scalar_state = state.reshape(scalars.shape)
    vector_state = vector_state.transpose(0, 2, 1, 3).reshape(vectors.shape)
    every = lax.all_to_all(energy, ("gx", "gy", "gz"), 0, 0, tiled=True)
    energy = jnp.sum(every, axis=0)[:1]
    return scalar_state, vector_state, energy


def solution(mesh):
    in_specs = (
        P("gx", "gy", "gz", None, None),
        P("gx", "gy", "gz"),
        P("gx", "gy", "gz", None, None),
        P("gx", "gy", "gz", None, None, None),
        P(),
        P(),
        P(),
        P(),
        P(),
        P(),
        P(),
        P(),
    )
    out_specs = (P("gx", "gy", "gz", None, None), P("gx", "gy", "gz", None, None, None), P())
    return jax.shard_map(
        on_device, mesh=mesh, in_specs=in_specs, out_specs=out_specs, check_vma=False
    )
```

profile of v0, /device:TPU:1, one launch (start us, length us, event | category | flops | bytes accessed | tf_op | source)
XLA Modules:
  0.0 94.8 jit_solution(8165546418218459428)
XLA Ops:
  0.6 1.1 %pack.1.refs_3_ = bf16[2,32,640]{2,1,0:T(8,128)(2,1)S(1)} custom-call(s32[2]{0:T(128)} %bitcast.48, f32[2,3,1,32]{3,2,1,0:T(1,128)} %bitcast.62, bf16[2,32,128]{2,1,0:T(8,128)(2,1)} %bitcast.60, bf16[2,3,32,128]{3,2,1,0:T(8,128)(2,1)} %bitcast.59), custom_call_target="tpu_custom_call" | custom-call | tf_op jit(solution)/shard_map/pack/pallas_call | solution.py:476
  1.7 2.1 %collective-permute-start = (bf16[2,32,640]{2,1,0:T(8,128)(2,1)S(1)}, bf16[2,32,640]{2,1,0:T(8,128)(2,1)S(1)}, u32[]{:S(2)}, u32[]{:S(2)}) collective-permute-start(bf16[2,32,640]{2,1,0:T(8,128)(2,1)S(1)} %pack.1.refs_3_), channel_id=1, source_target_pairs={{3,0},{0,1},{1,2},{2,3},{7,4},{4,5},{5,6},{6,7},{11,8},{8,9},{9,10... | collective-permute-start | bytes 245768 | tf_op jit(solution)/shard_map/ppermute | solution.py:493
  3.9 1.3 %collective-permute-start.1 = (bf16[2,32,640]{2,1,0:T(8,128)(2,1)S(1)}, bf16[2,32,640]{2,1,0:T(8,128)(2,1)S(1)}, u32[]{:S(2)}, u32[]{:S(2)}) collective-permute-start(bf16[2,32,640]{2,1,0:T(8,128)(2,1)S(1)} %pack.1.refs_3_), channel_id=1, source_target_pairs={{1,0},{2,1},{3,2},{0,3},{5,4},{6,5},{7,6},{4,7},{9,8},{10,9},{11,1... | collective-permute-start | bytes 245768 | tf_op jit(solution)/shard_map/ppermute | solution.py:493
  5.2 0.8 mul.31
  6.0 0.1 mul.32
  6.1 0.1 copy.37
  6.2 0.7 collective-permute-done
  7.0 0.2 collective-permute-done.1
  7.2 5.7 %collective-permute-start.2 = (bf16[2,3,32,640]{3,2,1,0:T(8,128)(2,1)S(1)}, bf16[2,3,32,640]{3,2,1,0:T(8,128)(2,1)S(1)}, u32[]{:S(2)}, u32[]{:S(2)}) collective-permute-start(bf16[2,3,32,640]{3,2,1,0:T(8,128)(2,1)S(1)} %pad_maximum_fusion.4.refs_2_), channel_id=1, source_target_pairs={{12,0},{0,4},{4,8},{8,12},{13,1},{1,5},{5,9},{9,13},{14,2},{2,6},{... | collective-permute-start | bytes 737288 | tf_op jit(solution)/shard_map/ppermute | solution.py:493
  12.8 0.0 collective-permute-start.3
  12.8 0.7 fusion.6
  13.5 0.1 copy.39
  13.7 0.7 mul.29
  14.4 0.2 mul.30
  14.6 0.2 copy.38
  14.8 0.0 copy-start
  14.8 0.0 copy-start.1
  14.8 0.0 copy-start.2
  14.8 0.0 copy-start.3
  14.8 0.0 copy-start.4
  15.0 0.2 fusion.2.refs_4_.refs_5_
  15.1 3.5 %collective-permute-done.2.refs_1_ = bf16[2,3,32,640]{3,2,1,0:T(8,128)(2,1)S(1)} collective-permute-done((bf16[2,3,32,640]{3,2,1,0:T(8,128)(2,1)S(1)}, bf16[2,3,32,640]{3,2,1,0:T(8,128)(2,1)S(1)}, u32[]{:S(2)}, u32[]{:S(2)}) %collective-permute-start.2) | collective-permute-done | bytes 245792 | tf_op jit(solution)/shard_map/ppermute | solution.py:493
  18.6 1.3 %collective-permute-done.3.refs_3_ = bf16[2,3,32,640]{3,2,1,0:T(8,128)(2,1)S(1)} collective-permute-done((bf16[2,3,32,640]{3,2,1,0:T(8,128)(2,1)S(1)}, bf16[2,3,32,640]{3,2,1,0:T(8,128)(2,1)S(1)}, u32[]{:S(2)}, u32[]{:S(2)}) %collective-permute-start.3) | collective-permute-done | bytes 245792 | tf_op jit(solution)/shard_map/ppermute | solution.py:493
  20.0 0.1 pad_maximum_fusion.1
  20.1 3.3 %collective-permute-start.5 = (bf16[3,3,32,640]{3,2,1,0:T(8,128)(2,1)S(1)}, bf16[3,3,32,640]{3,2,1,0:T(8,128)(2,1)S(1)}, u32[]{:S(2)}, u32[]{:S(2)}) collective-permute-start(bf16[3,3,32,640]{3,2,1,0:T(8,128)(2,1)S(1)} %pad_maximum_fusion.1), channel_id=1, source_target_pairs={{16,0},{32,16},{48,32},{64,48},{80,64},{96,80},{112,96},{0,112},{1... | collective-permute-start | bytes 1105928 | tf_op jit(solution)/shard_map/ppermute | solution.py:493
  23.3 0.1 pad_maximum_fusion
  23.4 0.1 collective-permute-start.4
  23.5 6.5 %own_part_0.1 = (f32[72,512]{1,0:T(8,128)S(1)}, f32[12,72,640]{2,1,0:T(8,128)}, bf16[640,576]{1,0:T(8,128)(2,1)}, s32[2]{0:T(128)S(1)}) custom-call(s32[2]{0:T(128)S(1)} %bitcast.49, bf16[2,3,32,640]{3,2,1,0:T(8,128)(2,1)S(1)} %collective-permute-done.2.refs_1_, bf16[2,3,32,640]{3,2,1,0:T(8,128)(2,1)S(1)} %pad_maximum_fusion.4.refs_2_, ...), custom_call_target="tpu_custom_call" | custom-call | flops 6039797760 | bytes 4000000 | tf_op jit(solution)/shard_map/own_part_0/pallas_call | solution.py:401
  30.0 1.2 %collective-permute-done.5.refs_2_ = bf16[3,3,32,640]{3,2,1,0:T(8,128)(2,1)S(1)} collective-permute-done((bf16[3,3,32,640]{3,2,1,0:T(8,128)(2,1)S(1)}, bf16[3,3,32,640]{3,2,1,0:T(8,128)(2,1)S(1)}, u32[]{:S(2)}, u32[]{:S(2)}) %collective-permute-start.5) | collective-permute-done | bytes 368672 | tf_op jit(solution)/shard_map/ppermute | solution.py:493
  31.2 4.5 %collective-permute-done.4.refs_1_ = bf16[3,3,32,640]{3,2,1,0:T(8,128)(2,1)S(1)} collective-permute-done((bf16[3,3,32,640]{3,2,1,0:T(8,128)(2,1)S(1)}, bf16[3,3,32,640]{3,2,1,0:T(8,128)(2,1)S(1)}, u32[]{:S(2)}, u32[]{:S(2)}) %collective-permute-start.4) | collective-permute-done | bytes 368672 | tf_op jit(solution)/shard_map/ppermute | solution.py:493
  35.7 4.2 %side_part_0.1 = (bf16[64,512]{1,0:T(8,128)(2,1)S(1)}, f32[12,72,384]{2,1,0:T(8,128)S(1)}, bf16[2,384,288]{2,1,0:T(8,128)(2,1)S(1)}, s32[2]{0:T(128)S(1)}) custom-call(s32[2]{0:T(128)S(1)} %bitcast.50, bf16[3,3,32,640]{3,2,1,0:T(8,128)(2,1)S(1)} %collective-permute-done.4.refs_1_, bf16[3,3,32,640]{3,2,1,0:T(8,128)(2,1)S(1)} %collective-permute-done.5.refs_2_, ...), custom_call_target="tpu_custom_call" | custom-call | flops 3019898880 | bytes 4000000 | tf_op jit(solution)/shard_map/side_part_0/pallas_call | solution.py:432
  39.9 1.3 %collective-permute-start.6 = (bf16[2,32,512]{2,1,0:T(8,128)(2,1)S(1)}, bf16[2,32,512]{2,1,0:T(8,128)(2,1)S(1)}, u32[]{:S(2)}, u32[]{:S(2)}) collective-permute-start(bf16[2,32,512]{2,1,0:T(8,128)(2,1)S(1)} %bitcast.44), channel_id=1, source_target_pairs={{3,0},{0,1},{1,2},{2,3},{7,4},{4,5},{5,6},{6,7},{11,8},{8,9},{9,10... | collective-permute-start | bytes 196616 | tf_op jit(solution)/shard_map/ppermute | solution.py:493
  41.2 1.5 %collective-permute-start.7 = (bf16[2,32,512]{2,1,0:T(8,128)(2,1)S(1)}, bf16[2,32,512]{2,1,0:T(8,128)(2,1)S(1)}, u32[]{:S(2)}, u32[]{:S(2)}) collective-permute-start(bf16[2,32,512]{2,1,0:T(8,128)(2,1)S(1)} %bitcast.45), channel_id=1, source_target_pairs={{1,0},{2,1},{3,2},{0,3},{5,4},{6,5},{7,6},{4,7},{9,8},{10,9},{11,1... | collective-permute-start | bytes 196616 | tf_op jit(solution)/shard_map/ppermute | solution.py:493
  42.8 0.1 copy.45.refs_10_
  42.9 1.4 %collective-permute-done.6 = bf16[2,32,512]{2,1,0:T(8,128)(2,1)S(1)} collective-permute-done((bf16[2,32,512]{2,1,0:T(8,128)(2,1)S(1)}, bf16[2,32,512]{2,1,0:T(8,128)(2,1)S(1)}, u32[]{:S(2)}, u32[]{:S(2)}) %collective-permute-start.6) | collective-permute-done | bytes 65568 | tf_op jit(solution)/shard_map/ppermute | solution.py:493
  44.4 4.9 %collective-permute-start.8 = (bf16[2,3,32,512]{3,2,0,1:T(8,128)(2,1)S(1)}, bf16[2,3,32,512]{3,2,0,1:T(8,128)(2,1)S(1)}, u32[]{:S(2)}, u32[]{:S(2)}) collective-permute-start(bf16[2,3,32,512]{3,2,0,1:T(8,128)(2,1)S(1)} %pad_maximum_fusion.5), channel_id=1, source_target_pairs={{12,0},{0,4},{4,8},{8,12},{13,1},{1,5},{5,9},{9,13},{14,2},{2,6},{... | collective-permute-start | bytes 589832 | tf_op jit(solution)/shard_map/ppermute | solution.py:493
  49.2 0.0 collective-permute-start.9
  49.3 4.3 %collective-permute-done.8 = bf16[2,3,32,512]{3,2,0,1:T(8,128)(2,1)S(1)} collective-permute-done((bf16[2,3,32,512]{3,2,0,1:T(8,128)(2,1)S(1)}, bf16[2,3,32,512]{3,2,0,1:T(8,128)(2,1)S(1)}, u32[]{:S(2)}, u32[]{:S(2)}) %collective-permute-start.8) | collective-permute-done | bytes 196640 | tf_op jit(solution)/shard_map/ppermute | solution.py:493
  53.6 2.2 %collective-permute-done.9 = bf16[2,3,32,512]{3,2,0,1:T(8,128)(2,1)S(1)} collective-permute-done((bf16[2,3,32,512]{3,2,0,1:T(8,128)(2,1)S(1)}, bf16[2,3,32,512]{3,2,0,1:T(8,128)(2,1)S(1)}, u32[]{:S(2)}, u32[]{:S(2)}) %collective-permute-start.9) | collective-permute-done | bytes 196640 | tf_op jit(solution)/shard_map/ppermute | solution.py:493
  55.9 4.9 %collective-permute-start.11 = (bf16[3,3,32,512]{3,2,0,1:T(8,128)(2,1)S(1)}, bf16[3,3,32,512]{3,2,0,1:T(8,128)(2,1)S(1)}, u32[]{:S(2)}, u32[]{:S(2)}) collective-permute-start(bf16[3,3,32,512]{3,2,0,1:T(8,128)(2,1)S(1)} %pad_maximum_fusion.3), channel_id=1, source_target_pairs={{16,0},{32,16},{48,32},{64,48},{80,64},{96,80},{112,96},{0,112},{1... | collective-permute-start | bytes 884744 | tf_op jit(solution)/shard_map/ppermute | solution.py:493
  60.8 0.1 collective-permute-start.10
  61.0 0.0 copy-start.5
  61.0 4.0 %own_part_1.1.refs_4_ = f32[72,512]{1,0:T(8,128)S(1)} custom-call(s32[2]{0:T(128)S(1)} %bitcast.51, bf16[2,3,32,512]{3,2,1,0:T(8,128)(2,1)S(1)} %copy.40.refs_1_, bf16[2,3,32,512]{3,2,1,0:T(8,128)(2,1)S(1)} %copy.41.refs_2_, bf16[2,3,32,512]{3,2,1,0:T(8,128)(2,1)S(1)} %copy.42.refs_3_, bf16[2,512,80]{2,1,0:T(8,128)(2,1)S(1)} %fusion.2.refs_4_.refs_5_, ...), custom_call_target="tpu_custom_call" | custom-call | flops 6039797760 | bytes 4000000 | tf_op jit(solution)/shard_map/own_part_1/pallas_call | solution.py:401
  64.9 1.6 %collective-permute-done.11 = bf16[3,3,32,512]{3,2,0,1:T(8,128)(2,1)S(1)} collective-permute-done((bf16[3,3,32,512]{3,2,0,1:T(8,128)(2,1)S(1)}, bf16[3,3,32,512]{3,2,0,1:T(8,128)(2,1)S(1)}, u32[]{:S(2)}, u32[]{:S(2)}) %collective-permute-start.11) | collective-permute-done | bytes 294944 | tf_op jit(solution)/shard_map/ppermute | solution.py:493
  66.6 4.4 %collective-permute-done.10 = bf16[3,3,32,512]{3,2,0,1:T(8,128)(2,1)S(1)} collective-permute-done((bf16[3,3,32,512]{3,2,0,1:T(8,128)(2,1)S(1)}, bf16[3,3,32,512]{3,2,0,1:T(8,128)(2,1)S(1)}, u32[]{:S(2)}, u32[]{:S(2)}) %collective-permute-start.10) | collective-permute-done | bytes 294944 | tf_op jit(solution)/shard_map/ppermute | solution.py:493
  71.0 3.4 %side_part_1.1 = (bf16[2,32,128]{2,1,0:T(8,128)(2,1)}, bf16[2,3,32,128]{3,2,1,0:T(8,128)(2,1)}, f32[128,128]{1,0:T(8,128)S(1)}) custom-call(s32[2]{0:T(128)S(1)} %bitcast.52, bf16[3,3,32,512]{3,2,1,0:T(8,128)(2,1)S(1)} %copy.43.refs_1_, bf16[3,3,32,512]{3,2,1,0:T(8,128)(2,1)S(1)} %copy.44.refs_2_, bf16[2,32,512]{2,1,0:T(8,128)(2,1)S(1)} %bitcast.47, ...), custom_call_target="tpu_custom_call" | custom-call | flops 3019898880 | bytes 4000000 | tf_op jit(solution)/shard_map/side_part_1/pallas_call | solution.py:432
  74.4 19.8 %all_to_all.9 = f32[128,1,128]{2,1,0:T(1,128)S(1)} all-to-all(f32[128,1,128]{2,1,0:T(1,128)S(1)} %bitcast.43), channel_id=1, replica_groups=mesh['gx'=8,'gy'=4,'gz'=4] {'gx','gy','gz'}, dimensions={0} | all-to-all | bytes 131072 | tf_op jit(solution)/shard_map/all_to_all | solution.py:555
  94.2 0.7 reduce_sum.9
  (31 shorter events, 0.4 us)
Async XLA Ops:
  1.7 5.2 %collective-permute-start = (bf16[2,32,640]{2,1,0:T(8,128)(2,1)S(1)}, bf16[2,32,640]{2,1,0:T(8,128)(2,1)S(1)}, u32[]{:S(2)}, u32[]{:S(2)}) collective-permute-start(bf16[2,32,640]{2,1,0:T(8,128)(2,1)S(1)} %pack.1.refs_3_), channel_id=1, source_target_pairs={{3,0},{0,1},{1,2},{2,3},{7,4},{4,5},{5,6},{6,7},{11,8},{8,9},{9,10... | collective-permute-start | bytes 245768 | tf_op jit(solution)/shard_map/ppermute | solution.py:493
  3.9 3.3 %collective-permute-start.1 = (bf16[2,32,640]{2,1,0:T(8,128)(2,1)S(1)}, bf16[2,32,640]{2,1,0:T(8,128)(2,1)S(1)}, u32[]{:S(2)}, u32[]{:S(2)}) collective-permute-start(bf16[2,32,640]{2,1,0:T(8,128)(2,1)S(1)} %pack.1.refs_3_), channel_id=1, source_target_pairs={{1,0},{2,1},{3,2},{0,3},{5,4},{6,5},{7,6},{4,7},{9,8},{10,9},{11,1... | collective-permute-start | bytes 245768 | tf_op jit(solution)/shard_map/ppermute | solution.py:493
  7.2 11.4 %collective-permute-start.2 = (bf16[2,3,32,640]{3,2,1,0:T(8,128)(2,1)S(1)}, bf16[2,3,32,640]{3,2,1,0:T(8,128)(2,1)S(1)}, u32[]{:S(2)}, u32[]{:S(2)}) collective-permute-start(bf16[2,3,32,640]{3,2,1,0:T(8,128)(2,1)S(1)} %pad_maximum_fusion.4.refs_2_), channel_id=1, source_target_pairs={{12,0},{0,4},{4,8},{8,12},{13,1},{1,5},{5,9},{9,13},{14,2},{2,6},{... | collective-permute-start | bytes 737288 | tf_op jit(solution)/shard_map/ppermute | solution.py:493
  12.8 7.1 %collective-permute-start.3 = (bf16[2,3,32,640]{3,2,1,0:T(8,128)(2,1)S(1)}, bf16[2,3,32,640]{3,2,1,0:T(8,128)(2,1)S(1)}, u32[]{:S(2)}, u32[]{:S(2)}) collective-permute-start(bf16[2,3,32,640]{3,2,1,0:T(8,128)(2,1)S(1)} %pad_maximum_fusion.4.refs_2_), channel_id=1, source_target_pairs={{4,0},{8,4},{12,8},{0,12},{5,1},{9,5},{13,9},{1,13},{6,2},{10,6},{... | collective-permute-start | bytes 737288 | tf_op jit(solution)/shard_map/ppermute | solution.py:493
  14.8 8.7 %copy-start = (s32[2,1,1]{0,2,1:T(1,128)S(1)}, s32[2,1,1]{0,2,1:T(1,128)}, u32[]{:S(2)}) copy-start(s32[2,1,1]{0,2,1:T(1,128)} %param.14) | copy-start | bytes 28
  14.8 8.7 %copy-start.1 = (bf16[2,128,512]{2,1,0:T(8,128)(2,1)S(1)}, bf16[2,128,512]{2,1,0:T(8,128)(2,1)}, u32[]{:S(2)}) copy-start(bf16[2,128,512]{2,1,0:T(8,128)(2,1)} %refs_9_.3) | copy-start | bytes 786436
  14.8 8.7 %copy-start.2 = (bf16[2,64,512]{2,1,0:T(8,128)(2,1)S(1)}, bf16[2,64,512]{2,1,0:T(8,128)(2,1)}, u32[]{:S(2)}) copy-start(bf16[2,64,512]{2,1,0:T(8,128)(2,1)} %refs_6_.7) | copy-start | bytes 393220
  14.8 8.7 %copy-start.3 = (bf16[2,128,128]{2,1,0:T(8,128)(2,1)S(1)}, bf16[2,128,128]{2,1,0:T(8,128)(2,1)}, u32[]{:S(2)}) copy-start(bf16[2,128,128]{2,1,0:T(8,128)(2,1)} %refs_7_.7) | copy-start | bytes 196612
  14.8 8.7 %copy-start.4 = (f32[2,128]{1,0:T(2,128)S(1)}, f32[2,128]{1,0:T(2,128)}, u32[]{:S(2)}) copy-start(f32[2,128]{1,0:T(2,128)} %refs_8_.7) | copy-start | bytes 3076
  20.1 11.2 %collective-permute-start.5 = (bf16[3,3,32,640]{3,2,1,0:T(8,128)(2,1)S(1)}, bf16[3,3,32,640]{3,2,1,0:T(8,128)(2,1)S(1)}, u32[]{:S(2)}, u32[]{:S(2)}) collective-permute-start(bf16[3,3,32,640]{3,2,1,0:T(8,128)(2,1)S(1)} %pad_maximum_fusion.1), channel_id=1, source_target_pairs={{16,0},{32,16},{48,32},{64,48},{80,64},{96,80},{112,96},{0,112},{1... | collective-permute-start | bytes 1105928 | tf_op jit(solution)/shard_map/ppermute | solution.py:493
  23.4 12.3 %collective-permute-start.4 = (bf16[3,3,32,640]{3,2,1,0:T(8,128)(2,1)S(1)}, bf16[3,3,32,640]{3,2,1,0:T(8,128)(2,1)S(1)}, u32[]{:S(2)}, u32[]{:S(2)}) collective-permute-start(bf16[3,3,32,640]{3,2,1,0:T(8,128)(2,1)S(1)} %pad_maximum_fusion), channel_id=1, source_target_pairs={{112,0},{0,16},{16,32},{32,48},{48,64},{64,80},{80,96},{96,112},{1... | collective-permute-start | bytes 1105928 | tf_op jit(solution)/shard_map/ppermute | solution.py:493
  35.7 7.0 %copy-start.8 = (bf16[128,64]{0,1:T(8,128)(2,1)S(1)}, bf16[128,64]{0,1:T(8,128)(2,1)}, u32[]{:S(2)}) copy-start(bf16[128,64]{0,1:T(8,128)(2,1)} %param.23) | copy-start | bytes 49156
  39.9 4.4 %collective-permute-start.6 = (bf16[2,32,512]{2,1,0:T(8,128)(2,1)S(1)}, bf16[2,32,512]{2,1,0:T(8,128)(2,1)S(1)}, u32[]{:S(2)}, u32[]{:S(2)}) collective-permute-start(bf16[2,32,512]{2,1,0:T(8,128)(2,1)S(1)} %bitcast.44), channel_id=1, source_target_pairs={{3,0},{0,1},{1,2},{2,3},{7,4},{4,5},{5,6},{6,7},{11,8},{8,9},{9,10... | collective-permute-start | bytes 196616 | tf_op jit(solution)/shard_map/ppermute | solution.py:493
  41.2 3.1 %collective-permute-start.7 = (bf16[2,32,512]{2,1,0:T(8,128)(2,1)S(1)}, bf16[2,32,512]{2,1,0:T(8,128)(2,1)S(1)}, u32[]{:S(2)}, u32[]{:S(2)}) collective-permute-start(bf16[2,32,512]{2,1,0:T(8,128)(2,1)S(1)} %bitcast.45), channel_id=1, source_target_pairs={{1,0},{2,1},{3,2},{0,3},{5,4},{6,5},{7,6},{4,7},{9,8},{10,9},{11,1... | collective-permute-start | bytes 196616 | tf_op jit(solution)/shard_map/ppermute | solution.py:493
  42.9 18.1 %copy-start.6 = (f32[12,72,640]{2,1,0:T(8,128)S(1)}, f32[12,72,640]{2,1,0:T(8,128)}, u32[]{:S(2)}) copy-start(f32[12,72,640]{2,1,0:T(8,128)} %get-tuple-element.22.refs_9_) | copy-start | bytes 6635524
  42.9 18.1 %copy-start.7 = (bf16[640,576]{1,0:T(8,128)(2,1)S(1)}, bf16[640,576]{1,0:T(8,128)(2,1)}, u32[]{:S(2)}) copy-start(bf16[640,576]{1,0:T(8,128)(2,1)} %get-tuple-element.23.refs_10_) | copy-start | bytes 2211844
  44.4 9.2 %collective-permute-start.8 = (bf16[2,3,32,512]{3,2,0,1:T(8,128)(2,1)S(1)}, bf16[2,3,32,512]{3,2,0,1:T(8,128)(2,1)S(1)}, u32[]{:S(2)}, u32[]{:S(2)}) collective-permute-start(bf16[2,3,32,512]{3,2,0,1:T(8,128)(2,1)S(1)} %pad_maximum_fusion.5), channel_id=1, source_target_pairs={{12,0},{0,4},{4,8},{8,12},{13,1},{1,5},{5,9},{9,13},{14,2},{2,6},{... | collective-permute-start | bytes 589832 | tf_op jit(solution)/shard_map/ppermute | solution.py:493
  49.2 6.6 %collective-permute-start.9 = (bf16[2,3,32,512]{3,2,0,1:T(8,128)(2,1)S(1)}, bf16[2,3,32,512]{3,2,0,1:T(8,128)(2,1)S(1)}, u32[]{:S(2)}, u32[]{:S(2)}) collective-permute-start(bf16[2,3,32,512]{3,2,0,1:T(8,128)(2,1)S(1)} %pad_maximum_fusion.5), channel_id=1, source_target_pairs={{4,0},{8,4},{12,8},{0,12},{5,1},{9,5},{13,9},{1,13},{6,2},{10,6},{... | collective-permute-start | bytes 589832 | tf_op jit(solution)/shard_map/ppermute | solution.py:493
  55.9 10.7 %collective-permute-start.11 = (bf16[3,3,32,512]{3,2,0,1:T(8,128)(2,1)S(1)}, bf16[3,3,32,512]{3,2,0,1:T(8,128)(2,1)S(1)}, u32[]{:S(2)}, u32[]{:S(2)}) collective-permute-start(bf16[3,3,32,512]{3,2,0,1:T(8,128)(2,1)S(1)} %pad_maximum_fusion.3), channel_id=1, source_target_pairs={{16,0},{32,16},{48,32},{64,48},{80,64},{96,80},{112,96},{0,112},{1... | collective-permute-start | bytes 884744 | tf_op jit(solution)/shard_map/ppermute | solution.py:493
  60.8 10.2 %collective-permute-start.10 = (bf16[3,3,32,512]{3,2,0,1:T(8,128)(2,1)S(1)}, bf16[3,3,32,512]{3,2,0,1:T(8,128)(2,1)S(1)}, u32[]{:S(2)}, u32[]{:S(2)}) collective-permute-start(bf16[3,3,32,512]{3,2,0,1:T(8,128)(2,1)S(1)} %pad_maximum_fusion.2), channel_id=1, source_target_pairs={{112,0},{0,16},{16,32},{32,48},{48,64},{64,80},{80,96},{96,112},{1... | collective-permute-start | bytes 884744 | tf_op jit(solution)/shard_map/ppermute | solution.py:493
  61.0 10.0 %copy-start.5 = (f32[64]{0:T(128)S(1)}, f32[64]{0:T(128)}, u32[]{:S(2)}) copy-start(f32[64]{0:T(128)} %param.24) | copy-start | bytes 772
where the time goes:
time: 95.9 us; the launch traced here: 94.8 us
  waiting for transfers between devices  25.4 us (26%)
  starting transfers between devices  25.1 us (26%)
  blocking collectives  19.8 us (21%)
  Pallas kernels  19.1 us (20%)
  local copies, waits for them, and re-layouts  2.65 us (3%)
  other arithmetic  1.8 us (2%)
  between operations  0.96 us (1%)
    ppermute x12, waiting for transfers between devices, shifted(): lax.ppermute(value, axis, [((i + step) % count, i) for i in range(count)])  25.4 us
    ppermute x12, starting transfers between devices, shifted(): lax.ppermute(value, axis, [((i + step) % count, i) for i in range(count)])  25.1 us
    all_to_all x1, blocking collectives, on_device(): every = lax.all_to_all(energy, ('gx', 'gy', 'gz'), 0, 0, tiled=True)  19.8 us
    pallas_call x2, Pallas kernels, own_call(): pl.pallas_call(functools.partial(own_kernel, layer), out_shape=shapes, in...  10.4 us
    pallas_call x2, Pallas kernels, side_call(): pl.pallas_call(functools.partial(side_kernel, layer, last), out_shape=sha...  7.58 us
    mul x6, local copies, waits for them, and re-layouts, radial_rows(): radial_in.transpose(0, 2, 1)[:, None, :, :, None] * eye[:, None, None, :]  2.13 us
  transfers between devices with their start and end apart: 12, of which 11 were waited for; matrix products, arithmetic and copies ran while one was open for 4% of the time, Pallas kernels for 11%

commit v1 on v0

--- a/solution.py
+++ b/solution.py
@@ -135,25 +135,30 @@
         feats[1 + k][part, :] = jnp.concatenate([gc, gg * vec[k]], axis=1)
 
 
-def messages(layer, count, place, window, weights, pairs_ref, feats, edges, delta):
+def rows_from(start):
+    return pl.ds(pl.multiple_of(start, block), block)
+
+
+def hidden_of(rin, pairs_ref, rows, window):
+    width = window.stop - window.start
+    slab = pairs_ref[0:8, rows, window].reshape(8 * block, width)
+    slab = jnp.concatenate([slab, jnp.ones((depth - 8 * block, width), f32)], axis=0)
+    return dot(rin, slab.astype(bf16)), pairs_ref[8:12, rows, window]
+
+
+def edge(r, y, w, out):
+    part = slice(r * hidden, (r + 1) * hidden)
+    width = y.shape[1]
+    s = half_silu(y[part]).astype(bf16).reshape(4, 16, width)
+    for g in range(4):
+        line = jnp.broadcast_to(w[g][r : r + 1, :], (16, width)).astype(bf16)
+        out[g][part, :width] = (s * line[None]).reshape(hidden, width)
+
+
+def messages(layer, count, place, window, weights, pairs_ref, feats, edges, delta, ready=None):
     rin_ref, rout_ref = weights[:2]
     width = window.stop - window.start
     even, odd = edges[:4], edges[4:]
-
-    def rows_at(b):
-        return pl.ds(pl.multiple_of(place(b)[0], block), block)
-
-    def hidden_of(b):
-        slab = pairs_ref[0:8, rows_at(b), window].reshape(8 * block, width)
-        slab = jnp.concatenate([slab, jnp.ones((depth - 8 * block, width), f32)], axis=0)
-        return dot(rin_ref[layer], slab.astype(bf16)), pairs_ref[8:12, rows_at(b), window]
-
-    def edge(r, y, w, out):
-        part = slice(r * hidden, (r + 1) * hidden)
-        s = half_silu(y[part]).astype(bf16).reshape(4, 16, width)
-        for g in range(4):
-            line = jnp.broadcast_to(w[g][r : r + 1, :], (16, width)).astype(bf16)
-            out[g][part, :width] = (s * line[None]).reshape(hidden, width)
 
     def product(n, used, atoms):
         if n < 2:
@@ -172,9 +177,12 @@
     def step(b, used, following):
         radial = [rout_ref[layer, :, g * chan : (g + 1) * chan].astype(f32)[None] for g in range(4)]
         sums = [None] * 4
-        atoms = pl.ds(pl.multiple_of(place(b)[1], chan), width)
+        row, start = place(b)
+        atoms = pl.ds(pl.multiple_of(start, chan), width)
+        if ready is not None:
+            used = [ready.at[b, g] for g in range(4)]
         if following is not None:
-            y, w = hidden_of(b + 1)
+            y, w = hidden_of(rin_ref[layer], pairs_ref, rows_from(place(b + 1)[0]), window)
         made, previous = 0, None
         for n in range(5):
             result = product(n, used, atoms)
@@ -186,11 +194,14 @@
             previous = result
         gather(4, previous, radial, sums)
         for g in range(4):
-            delta[rows_at(b), g * chan : (g + 1) * chan] += sums[g]
-
-    y, w = hidden_of(0)
-    for r in range(block):
-        edge(r, y, w, even)
+            delta[rows_from(row), g * chan : (g + 1) * chan] += sums[g]
+
+    if ready is None:
+        y, w = hidden_of(rin_ref[layer], pairs_ref, rows_from(place(0)[0]), window)
+        for r in range(block):
+            edge(r, y, w, even)
+    else:
+        even = odd = None
 
     def two_steps(t, carry):
         step(2 * t, even, odd)
@@ -202,6 +213,35 @@
     @pl.when(count % 2 == 1)
     def _():
         step(count - 1, even, None)
+
+
+def blocks_of(count):
+    return (count + block - 1) // block
+
+
+def side_place(counts_ref, start):
+    below = blocks_of(counts_ref[0])
+
+    def place(b):
+        q = jnp.where(b >= below, 1, 0)
+        return b * block + q * (slots - below * block), q * side_span + start
+
+    return below + blocks_of(counts_ref[1]), place
+
+
+def edge_kernel(layer, counts_ref, rin_ref, own_pairs, side_pairs, own_out, side_out):
+    def make(count, place, pairs, window, out):
+        def one(b, carry):
+            y, w = hidden_of(rin_ref[layer], pairs, rows_from(place(b)[0]), window)
+            for r in range(block):
+                edge(r, y, w, [out.at[b, g] for g in range(4)])
+            return carry
+
+        lax.fori_loop(0, count, one, 0)
+
+    count = blocks_of(counts_ref[0] + counts_ref[1])
+    make(count, lambda b: (b * block, 0), own_pairs, slice(0, own_main), own_out)
+    make(*side_place(counts_ref, 0), side_pairs, slice(0, side_main), side_out)
 
 
 def own_kernel(layer, *refs):
@@ -213,8 +253,8 @@
         refs = refs[4:]
         pairs, order, done = refs[12:]
     else:
-        pairs, order, more, delta = refs[:4]
-        refs = refs[4:]
+        pairs, order, more, ready, delta = refs[:5]
+        refs = refs[5:]
     feats, edges = refs[:4], refs[4:12]
     parts = [ref[...].reshape(own_atoms // 3, -1) for ref in (low, middle, high)]
     third = own_atoms // 3
@@ -250,9 +290,9 @@
 
     delta[...] = jnp.zeros_like(delta)
     main, rest = slice(0, own_main), slice(own_main, own_span)
-    count = (counts_ref[0] + counts_ref[1] + block - 1) // block
-
-    def add(part):
+    count = blocks_of(counts_ref[0] + counts_ref[1])
+
+    def add(part, ready=None):
         gathered(part)
         messages(
             layer,
@@ -264,9 +304,10 @@
             feats,
             edges,
             delta,
+            ready,
         )
 
-    add(main)
+    add(main, None if layer == 0 else ready)
 
     @pl.when(more[0] > 0)
     def _():
@@ -285,7 +326,7 @@
         read_in_ref, read_out_ref = refs[:2]
         refs = refs[2:]
     if layer > 0:
-        (pairs, order, more), refs = refs[:3], refs[3:]
+        (pairs, order, more, ready), refs = refs[:4], refs[4:]
     if last:
         (scalar_ref, vector_ref, energy_ref), refs = refs[:3], refs[3:]
     else:
@@ -308,22 +349,17 @@
             number = lax.broadcasted_iota(jnp.int32, (slots, 1), 0) + (q * slots + 1)
             geometry(row, mine, number, (-cutoff, cutoff)[q], pairs, at)
         more[0] = jnp.where(jnp.maximum(total[0], total[1]) > side_main + 0.5, 1, 0)
-    below = (counts_ref[0] + block - 1) // block
-    above = (counts_ref[1] + block - 1) // block
-
-    def add(part):
+
+    def add(part, ready=None):
         for q in range(2):
             x = dot(order[q, part, :], atoms[q][:, : 4 * chan])
             rows = slice(q * side_span + part.start, q * side_span + part.stop)
             features(layer, x.astype(bf16), rows, weights, feats)
 
-        def place(b):
-            q = jnp.where(b >= below, 1, 0)
-            return b * block + q * (slots - below * block), q * side_span + part.start
-
-        messages(layer, below + above, place, part, weights, pairs, feats, edges, delta)
-
-    add(main)
+        count, place = side_place(counts_ref, part.start)
+        messages(layer, count, place, part, weights, pairs, feats, edges, delta, ready)
+
+    add(main, None if layer == 0 else ready)
 
     @pl.when(more[0] > 0)
     def _():
@@ -369,7 +405,10 @@
     )
 
 
-params = pltpu.CompilerParams(vmem_limit_bytes=24 * 1024 * 1024)
+params = [
+    pltpu.CompilerParams(vmem_limit_bytes=24 * 1024 * 1024),
+    pltpu.CompilerParams(vmem_limit_bytes=12 * 1024 * 1024),
+]
 delta_shape = jax.ShapeDtypeStruct((room, 4 * chan), f32)
 
 
@@ -388,7 +427,7 @@
     operands = [counts, *ys, *weights]
     specs = [smem] + [vmem] * (len(operands) - 1)
     shapes, outs = (delta_shape,), (vmem,)
-    held = scratch(own_span, own_main)
+    held = scratch(own_span, own_main if layer == 0 else own_span - own_main)
     if layer == 0:
         kept_out = kept_shapes(own_span, (own_span, own_atoms))
         shapes += tuple(pltpu.HBM(k.shape, k.dtype) for k in kept_out[:2]) + kept_out[2:]
@@ -397,17 +436,35 @@
         held += [pltpu.SemaphoreType.DMA((2,))]
     else:
         operands += kept
-        specs += kept_specs
+        specs += kept_specs + (vmem,)
     return pl.pallas_call(
         functools.partial(own_kernel, layer),
         out_shape=shapes,
         in_specs=specs,
         out_specs=outs,
         scratch_shapes=held,
-        compiler_params=params,
+        compiler_params=params[min(layer, 1)],
         cost_estimate=cost(own_atoms),
         name=f"own_part_{layer}",
     )(*operands)
+
+
+def edge_call(layer, counts, rin, own_pairs, side_pairs):
+    count = 2 * slots // block
+    return pl.pallas_call(
+        functools.partial(edge_kernel, layer),
+        out_shape=(
+            pltpu.VMEM((count, 4, block * hidden, own_main), bf16),
+            pltpu.VMEM((count, 4, block * hidden, side_main), bf16),
+        ),
+        in_specs=[smem, vmem, vmem, vmem],
+        out_specs=(vmem, vmem),
+        compiler_params=params[1],
+        cost_estimate=pl.CostEstimate(
+            flops=1000000000, bytes_accessed=4000000, transcendentals=4000000
+        ),
+        name=f"edges_{layer}",
+    )(counts, rin, own_pairs, side_pairs)
 
 
 def side_call(layer, last, counts, low, high, own, delta, weights, readout, kept):
@@ -428,14 +485,14 @@
         outs += kept_specs
     else:
         operands += kept
-        specs += kept_specs
+        specs += kept_specs + (vmem,)
     return pl.pallas_call(
         functools.partial(side_kernel, layer, last),
         out_shape=shapes,
         in_specs=specs,
         out_specs=outs,
-        scratch_shapes=scratch(2 * side_span, side_main) + [pltpu.VMEM(delta_shape.shape, f32)],
-        compiler_params=params,
+        scratch_shapes=scratch(2 * side_span, side_main if layer == 0 else side_span - side_main) + [pltpu.VMEM(delta_shape.shape, f32)],
+        compiler_params=params[min(layer, 1)],
         cost_estimate=cost(side_atoms),
         name=f"side_part_{layer}",
     )(*operands)
@@ -536,14 +593,20 @@
             y, radial_in, radial_bias = lax.optimization_barrier((y, radial_in, radial_bias))
             rin = radial_rows(radial_in, radial_bias)
             weights = [rin, radial_out, atom_in, atom_bias, atom_out]
+            own_ready = side_ready = []
+        else:
+            y, own_kept, side_kept = lax.optimization_barrier((y, own_kept, side_kept))
+            own_ready, side_ready = (
+                [e] for e in edge_call(layer, counts, rin, own_kept[0], side_kept[0])
+            )
         ys = [shifted(y, "gy", -1), y, shifted(y, "gy", 1)]
         low = shifted(jnp.stack([v[1] for v in ys]), "gx", -1)
         high = shifted(jnp.stack([v[0] for v in ys]), "gx", 1)
-        delta, *kept = own_call(layer, counts, ys, weights, own_kept)
+        delta, *kept = own_call(layer, counts, ys, weights, [*own_kept, *own_ready])
         own_kept = own_kept or kept
         readout = [readout_in, readout_out[None, :]]
         state, *kept = side_call(
-            layer, last, counts, low, high, own, delta, weights, readout, side_kept
+            layer, last, counts, low, high, own, delta, weights, readout, [*side_kept, *side_ready]
         )
         if last:
             vector_state, energy = kept

time: 95.9 us -> 102 us (1.064); the launches traced: 94.8 us -> 102 us
  waiting for transfers between devices: 25.4 us -> 19.6 us
  local copies, waits for them, and re-layouts: 2.65 us -> 8.28 us
  starting transfers between devices: 25.1 us -> 30.4 us
  blocking collectives: 19.8 us -> 23.3 us
  Pallas kernels: 19.1 us -> 17.9 us
    ppermute x12, waiting for transfers between devices: 25.4 us -> 19.6 us  [shifted(): lax.ppermute(value, axis, [((i + step) % count, i) for i in range(count)])]
    unnamed x19 -> x31, local copies, waits for them, and re-layouts: 0.16 us -> 5.79 us
    ppermute x12, starting transfers between devices: 25.1 us -> 30.4 us  [shifted(): lax.ppermute(value, axis, [((i + step) % count, i) for i in range(count)])]
    all_to_all x1, blocking collectives: 19.8 us -> 23.3 us  [on_device(): every = lax.all_to_all(energy, ('gx', 'gy', 'gz'), 0, 0, tiled=True)]
    pallas_call x2, Pallas kernels: 10.4 us -> 7.84 us  [own_call(): pl.pallas_call(functools.partial(own_kernel, layer), out_shape=shapes, in...]
    pallas_call x0 -> x1, Pallas kernels: none -> 1.64 us  [edge_call(): pl.pallas_call(functools.partial(edge_kernel, layer), out_shape=(pltpu.VM...]
  transfers between devices with their start and end apart: 12 -> 12, of which waited for: 11 -> 10; matrix products, arithmetic and copies ran while one was open for 4% -> 3% of each run, Pallas kernels for 11% -> 9%
where the time goes in v1:
time: 102 us
  starting transfers between devices  30.4 us (30%)
  blocking collectives  23.3 us (23%)
  waiting for transfers between devices  19.6 us (19%)
  Pallas kernels  17.9 us (18%)
  local copies, waits for them, and re-layouts  8.28 us (8%)
  other arithmetic  1.8 us (2%)
    ppermute x12, starting transfers between devices, shifted(): lax.ppermute(value, axis, [((i + step) % count, i) for i in range(count)])  30.4 us
    all_to_all x1, blocking collectives, on_device(): every = lax.all_to_all(energy, ('gx', 'gy', 'gz'), 0, 0, tiled=True)  23.3 us
    ppermute x12, waiting for transfers between devices, shifted(): lax.ppermute(value, axis, [((i + step) % count, i) for i in range(count)])  19.6 us
    pallas_call x2, Pallas kernels, own_call(): pl.pallas_call(functools.partial(own_kernel, layer), out_shape=shapes, in...  7.84 us
    pallas_call x2, Pallas kernels, side_call(): pl.pallas_call(functools.partial(side_kernel, layer, last), out_shape=sha...  7.27 us
    unnamed x31, local copies, waits for them, and re-layouts  5.79 us
    mul x6, local copies, waits for them, and re-layouts, radial_rows(): radial_in.transpose(0, 2, 1)[:, None, :, :, None] * eye[:, None, None, :]  2.13 us
  transfers between devices with their start and end apart: 12, of which 10 were waited for; matrix products, arithmetic and copies ran while one was open for 3% of the time, Pallas kernels for 9%

profile of v1, /device:TPU:1, one launch (start us, length us, event | category | flops | bytes accessed | tf_op | source)
XLA Modules:
  0.0 102.1 jit_solution(14097312269409418916)
XLA Ops:
  0.6 1.1 %pack.1.refs_3_ = bf16[2,32,640]{2,1,0:T(8,128)(2,1)S(1)} custom-call(s32[2]{0:T(128)} %bitcast.48, f32[2,3,1,32]{3,2,1,0:T(1,128)} %bitcast.63, bf16[2,32,128]{2,1,0:T(8,128)(2,1)} %bitcast.61, bf16[2,3,32,128]{3,2,1,0:T(8,128)(2,1)} %bitcast.60), custom_call_target="tpu_custom_call" | custom-call | tf_op jit(solution)/shard_map/pack/pallas_call | solution.py:533
  1.7 2.1 %collective-permute-start = (bf16[2,32,640]{2,1,0:T(8,128)(2,1)S(1)}, bf16[2,32,640]{2,1,0:T(8,128)(2,1)S(1)}, u32[]{:S(2)}, u32[]{:S(2)}) collective-permute-start(bf16[2,32,640]{2,1,0:T(8,128)(2,1)S(1)} %pack.1.refs_3_), channel_id=1, source_target_pairs={{3,0},{0,1},{1,2},{2,3},{7,4},{4,5},{5,6},{6,7},{11,8},{8,9},{9,10... | collective-permute-start | bytes 245768 | tf_op jit(solution)/shard_map/ppermute | solution.py:550
  3.9 1.3 %collective-permute-start.1 = (bf16[2,32,640]{2,1,0:T(8,128)(2,1)S(1)}, bf16[2,32,640]{2,1,0:T(8,128)(2,1)S(1)}, u32[]{:S(2)}, u32[]{:S(2)}) collective-permute-start(bf16[2,32,640]{2,1,0:T(8,128)(2,1)S(1)} %pack.1.refs_3_), channel_id=1, source_target_pairs={{1,0},{2,1},{3,2},{0,3},{5,4},{6,5},{7,6},{4,7},{9,8},{10,9},{11,1... | collective-permute-start | bytes 245768 | tf_op jit(solution)/shard_map/ppermute | solution.py:550
  5.2 0.8 mul.31
  6.0 0.1 mul.32
  6.1 0.1 copy.37
  6.2 0.7 collective-permute-done
  7.0 0.2 collective-permute-done.1
  7.2 5.7 %collective-permute-start.2 = (bf16[2,3,32,640]{3,2,1,0:T(8,128)(2,1)S(1)}, bf16[2,3,32,640]{3,2,1,0:T(8,128)(2,1)S(1)}, u32[]{:S(2)}, u32[]{:S(2)}) collective-permute-start(bf16[2,3,32,640]{3,2,1,0:T(8,128)(2,1)S(1)} %pad_maximum_fusion.4.refs_2_), channel_id=1, source_target_pairs={{12,0},{0,4},{4,8},{8,12},{13,1},{1,5},{5,9},{9,13},{14,2},{2,6},{... | collective-permute-start | bytes 737288 | tf_op jit(solution)/shard_map/ppermute | solution.py:550
  12.8 0.7 fusion.6
  13.5 0.1 copy.39
  13.7 0.7 mul.29
  14.4 0.2 mul.30
  14.6 0.2 copy.38
  14.9 0.2 fusion.2.refs_4_.refs_5_.rin_ref
  15.1 3.5 %collective-permute-done.2.refs_1_ = bf16[2,3,32,640]{3,2,1,0:T(8,128)(2,1)S(1)} collective-permute-done((bf16[2,3,32,640]{3,2,1,0:T(8,128)(2,1)S(1)}, bf16[2,3,32,640]{3,2,1,0:T(8,128)(2,1)S(1)}, u32[]{:S(2)}, u32[]{:S(2)}) %collective-permute-start.2) | collective-permute-done | bytes 245792 | tf_op jit(solution)/shard_map/ppermute | solution.py:550
  18.6 1.3 %collective-permute-done.3.refs_3_ = bf16[2,3,32,640]{3,2,1,0:T(8,128)(2,1)S(1)} collective-permute-done((bf16[2,3,32,640]{3,2,1,0:T(8,128)(2,1)S(1)}, bf16[2,3,32,640]{3,2,1,0:T(8,128)(2,1)S(1)}, u32[]{:S(2)}, u32[]{:S(2)}) %collective-permute-start.3) | collective-permute-done | bytes 245792 | tf_op jit(solution)/shard_map/ppermute | solution.py:550
  20.0 0.1 pad_maximum_fusion.1
  20.1 3.3 %collective-permute-start.5 = (bf16[3,3,32,640]{3,2,1,0:T(8,128)(2,1)S(1)}, bf16[3,3,32,640]{3,2,1,0:T(8,128)(2,1)S(1)}, u32[]{:S(2)}, u32[]{:S(2)}) collective-permute-start(bf16[3,3,32,640]{3,2,1,0:T(8,128)(2,1)S(1)} %pad_maximum_fusion.1), channel_id=1, source_target_pairs={{16,0},{32,16},{48,32},{64,48},{80,64},{96,80},{112,96},{0,112},{1... | collective-permute-start | bytes 1105928 | tf_op jit(solution)/shard_map/ppermute | solution.py:550
  23.3 0.1 pad_maximum_fusion
  23.4 0.1 collective-permute-start.4
  23.4 0.0 copy-start
  23.5 0.9 copy-done
  24.4 0.9 copy-done.2
  25.3 0.8 copy-done.4
  26.1 0.7 copy-done.6
  26.8 0.7 copy-done.8
  27.5 5.3 %own_part_0.1 = (f32[72,512]{1,0:T(8,128)S(1)}, f32[12,72,640]{2,1,0:T(8,128)}, bf16[640,576]{1,0:T(8,128)(2,1)}, s32[2]{0:T(128)S(1)}) custom-call(s32[2]{0:T(128)S(1)} %bitcast.49, bf16[2,3,32,640]{3,2,1,0:T(8,128)(2,1)S(1)} %collective-permute-done.2.refs_1_, bf16[2,3,32,640]{3,2,1,0:T(8,128)(2,1)S(1)} %pad_maximum_fusion.4.refs_2_, ...), custom_call_target="tpu_custom_call" | custom-call | flops 6039797760 | bytes 4000000 | tf_op jit(solution)/shard_map/own_part_0/pallas_call | solution.py:440
  32.8 0.0 copy-start.14
  32.9 2.8 %collective-permute-done.4.refs_1_ = bf16[3,3,32,640]{3,2,1,0:T(8,128)(2,1)S(1)} collective-permute-done((bf16[3,3,32,640]{3,2,1,0:T(8,128)(2,1)S(1)}, bf16[3,3,32,640]{3,2,1,0:T(8,128)(2,1)S(1)}, u32[]{:S(2)}, u32[]{:S(2)}) %collective-permute-start.4) | collective-permute-done | bytes 368672 | tf_op jit(solution)/shard_map/ppermute | solution.py:550
  35.7 4.2 %side_part_0.1 = (bf16[64,512]{1,0:T(8,128)(2,1)S(1)}, f32[12,72,384]{2,1,0:T(8,128)S(1)}, bf16[2,384,288]{2,1,0:T(8,128)(2,1)S(1)}, s32[2]{0:T(128)S(1)}) custom-call(s32[2]{0:T(128)S(1)} %bitcast.50, bf16[3,3,32,640]{3,2,1,0:T(8,128)(2,1)S(1)} %collective-permute-done.4.refs_1_, bf16[3,3,32,640]{3,2,1,0:T(8,128)(2,1)S(1)} %collective-permute-done.5.refs_2_, ...), custom_call_target="tpu_custom_call" | custom-call | flops 3019898880 | bytes 4000000 | tf_op jit(solution)/shard_map/side_part_0/pallas_call | solution.py:489
  39.9 1.3 %collective-permute-start.6 = (bf16[2,32,512]{2,1,0:T(8,128)(2,1)S(1)}, bf16[2,32,512]{2,1,0:T(8,128)(2,1)S(1)}, u32[]{:S(2)}, u32[]{:S(2)}) collective-permute-start(bf16[2,32,512]{2,1,0:T(8,128)(2,1)S(1)} %bitcast.43), channel_id=1, source_target_pairs={{3,0},{0,1},{1,2},{2,3},{7,4},{4,5},{5,6},{6,7},{11,8},{8,9},{9,10... | collective-permute-start | bytes 196616 | tf_op jit(solution)/shard_map/ppermute | solution.py:550
  41.2 1.6 %collective-permute-start.7 = (bf16[2,32,512]{2,1,0:T(8,128)(2,1)S(1)}, bf16[2,32,512]{2,1,0:T(8,128)(2,1)S(1)}, u32[]{:S(2)}, u32[]{:S(2)}) collective-permute-start(bf16[2,32,512]{2,1,0:T(8,128)(2,1)S(1)} %bitcast.44), channel_id=1, source_target_pairs={{1,0},{2,1},{3,2},{0,3},{5,4},{6,5},{7,6},{4,7},{9,8},{10,9},{11,1... | collective-permute-start | bytes 196616 | tf_op jit(solution)/shard_map/ppermute | solution.py:550
  42.8 0.1 copy.45.refs_10_
  42.9 1.5 %collective-permute-done.6 = bf16[2,32,512]{2,1,0:T(8,128)(2,1)S(1)} collective-permute-done((bf16[2,32,512]{2,1,0:T(8,128)(2,1)S(1)}, bf16[2,32,512]{2,1,0:T(8,128)(2,1)S(1)}, u32[]{:S(2)}, u32[]{:S(2)}) %collective-permute-start.6) | collective-permute-done | bytes 65568 | tf_op jit(solution)/shard_map/ppermute | solution.py:550
  44.4 5.1 %collective-permute-start.8 = (bf16[2,3,32,512]{3,2,0,1:T(8,128)(2,1)S(1)}, bf16[2,3,32,512]{3,2,0,1:T(8,128)(2,1)S(1)}, u32[]{:S(2)}, u32[]{:S(2)}) collective-permute-start(bf16[2,3,32,512]{3,2,0,1:T(8,128)(2,1)S(1)} %pad_maximum_fusion.5), channel_id=1, source_target_pairs={{12,0},{0,4},{4,8},{8,12},{13,1},{1,5},{5,9},{9,13},{14,2},{2,6},{... | collective-permute-start | bytes 589832 | tf_op jit(solution)/shard_map/ppermute | solution.py:550
  49.5 1.6 %copy-done.11 = f32[12,72,640]{2,1,0:T(8,128)S(1)} copy-done((f32[12,72,640]{2,1,0:T(8,128)S(1)}, f32[12,72,640]{2,1,0:T(8,128)}, u32[]{:S(2)}) %copy-start.11) | copy-done | bytes 2211864
  51.1 1.6 %edges_1.1 = (bf16[8,4,512,512]{3,2,1,0:T(8,128)(2,1)S(1)}, bf16[8,4,512,256]{3,2,1,0:T(8,128)(2,1)S(1)}) custom-call(s32[2]{0:T(128)S(1)} %bitcast.51, bf16[2,512,80]{2,1,0:T(8,128)(2,1)S(1)} %fusion.2.refs_4_.refs_5_.rin_ref, f32[12,72,640]{2,1,0:T(8,128)S(1)} %copy-done.11, f32[12,72,384]{2,1,0:T(8,128)S(1)} %get-tuple-element.41.side_pairs.refs_12_), custom_call_target="tpu_custom_call" | custom-call | flops 1000000000 | bytes 4000000 | tf_op jit(solution)/shard_map/edges_1/pallas_call | solution.py:454
  52.8 1.2 %collective-permute-done.8 = bf16[2,3,32,512]{3,2,0,1:T(8,128)(2,1)S(1)} collective-permute-done((bf16[2,3,32,512]{3,2,0,1:T(8,128)(2,1)S(1)}, bf16[2,3,32,512]{3,2,0,1:T(8,128)(2,1)S(1)}, u32[]{:S(2)}, u32[]{:S(2)}) %collective-permute-start.8) | collective-permute-done | bytes 196640 | tf_op jit(solution)/shard_map/ppermute | solution.py:550
  54.0 2.1 %collective-permute-done.9 = bf16[2,3,32,512]{3,2,0,1:T(8,128)(2,1)S(1)} collective-permute-done((bf16[2,3,32,512]{3,2,0,1:T(8,128)(2,1)S(1)}, bf16[2,3,32,512]{3,2,0,1:T(8,128)(2,1)S(1)}, u32[]{:S(2)}, u32[]{:S(2)}) %collective-permute-start.9) | collective-permute-done | bytes 196640 | tf_op jit(solution)/shard_map/ppermute | solution.py:550
  56.1 9.9 %collective-permute-start.11 = (bf16[3,3,32,512]{3,2,0,1:T(8,128)(2,1)S(1)}, bf16[3,3,32,512]{3,2,0,1:T(8,128)(2,1)S(1)}, u32[]{:S(2)}, u32[]{:S(2)}) collective-permute-start(bf16[3,3,32,512]{3,2,0,1:T(8,128)(2,1)S(1)} %pad_maximum_fusion.3), channel_id=1, source_target_pairs={{16,0},{32,16},{48,32},{64,48},{80,64},{96,80},{112,96},{0,112},{1... | collective-permute-start | bytes 884744 | tf_op jit(solution)/shard_map/ppermute | solution.py:550
  66.1 0.1 collective-permute-start.10
  66.2 2.5 %own_part_1.1.refs_4_ = f32[72,512]{1,0:T(8,128)S(1)} custom-call(s32[2]{0:T(128)S(1)} %bitcast.52, bf16[2,3,32,512]{3,2,1,0:T(8,128)(2,1)S(1)} %copy.40.refs_1_, bf16[2,3,32,512]{3,2,1,0:T(8,128)(2,1)S(1)} %copy.41.refs_2_, bf16[2,3,32,512]{3,2,1,0:T(8,128)(2,1)S(1)} %copy.42.refs_3_, bf16[2,512,80]{2,1,0:T(8,128)(2,1)S(1)} %fusion.2.refs_4_.refs_5_.rin_ref, ...), custom_call_target="tpu_custom_call" | custom-call | flops 6039797760 | bytes 4000000 | tf_op jit(solution)/shard_map/own_part_1/pallas_call | solution.py:440
  68.8 2.1 %collective-permute-done.11 = bf16[3,3,32,512]{3,2,0,1:T(8,128)(2,1)S(1)} collective-permute-done((bf16[3,3,32,512]{3,2,0,1:T(8,128)(2,1)S(1)}, bf16[3,3,32,512]{3,2,0,1:T(8,128)(2,1)S(1)}, u32[]{:S(2)}, u32[]{:S(2)}) %collective-permute-start.11) | collective-permute-done | bytes 294944 | tf_op jit(solution)/shard_map/ppermute | solution.py:550
  70.9 4.1 %collective-permute-done.10 = bf16[3,3,32,512]{3,2,0,1:T(8,128)(2,1)S(1)} collective-permute-done((bf16[3,3,32,512]{3,2,0,1:T(8,128)(2,1)S(1)}, bf16[3,3,32,512]{3,2,0,1:T(8,128)(2,1)S(1)}, u32[]{:S(2)}, u32[]{:S(2)}) %collective-permute-start.10) | collective-permute-done | bytes 294944 | tf_op jit(solution)/shard_map/ppermute | solution.py:550
  75.0 3.1 %side_part_1.1 = (bf16[2,32,128]{2,1,0:T(8,128)(2,1)}, bf16[2,3,32,128]{3,2,1,0:T(8,128)(2,1)}, f32[128,128]{1,0:T(8,128)S(1)}) custom-call(s32[2]{0:T(128)S(1)} %bitcast.53, bf16[3,3,32,512]{3,2,1,0:T(8,128)(2,1)S(1)} %copy.43.refs_1_, bf16[3,3,32,512]{3,2,1,0:T(8,128)(2,1)S(1)} %copy.44.refs_2_, bf16[2,32,512]{2,1,0:T(8,128)(2,1)S(1)} %bitcast.46, ...), custom_call_target="tpu_custom_call" | custom-call | flops 3019898880 | bytes 4000000 | tf_op jit(solution)/shard_map/side_part_1/pallas_call | solution.py:489
  78.1 23.3 %all_to_all.9 = f32[128,1,128]{2,1,0:T(1,128)S(1)} all-to-all(f32[128,1,128]{2,1,0:T(1,128)S(1)} %bitcast.47), channel_id=1, replica_groups=mesh['gx'=8,'gy'=4,'gz'=4] {'gx','gy','gz'}, dimensions={0} | all-to-all | bytes 131072 | tf_op jit(solution)/shard_map/all_to_all | solution.py:618
  101.4 0.7 reduce_sum.9
  (44 shorter events, 0.5 us)
Async XLA Ops:
  1.7 5.2 %collective-permute-start = (bf16[2,32,640]{2,1,0:T(8,128)(2,1)S(1)}, bf16[2,32,640]{2,1,0:T(8,128)(2,1)S(1)}, u32[]{:S(2)}, u32[]{:S(2)}) collective-permute-start(bf16[2,32,640]{2,1,0:T(8,128)(2,1)S(1)} %pack.1.refs_3_), channel_id=1, source_target_pairs={{3,0},{0,1},{1,2},{2,3},{7,4},{4,5},{5,6},{6,7},{11,8},{8,9},{9,10... | collective-permute-start | bytes 245768 | tf_op jit(solution)/shard_map/ppermute | solution.py:550
  3.9 3.3 %collective-permute-start.1 = (bf16[2,32,640]{2,1,0:T(8,128)(2,1)S(1)}, bf16[2,32,640]{2,1,0:T(8,128)(2,1)S(1)}, u32[]{:S(2)}, u32[]{:S(2)}) collective-permute-start(bf16[2,32,640]{2,1,0:T(8,128)(2,1)S(1)} %pack.1.refs_3_), channel_id=1, source_target_pairs={{1,0},{2,1},{3,2},{0,3},{5,4},{6,5},{7,6},{4,7},{9,8},{10,9},{11,1... | collective-permute-start | bytes 245768 | tf_op jit(solution)/shard_map/ppermute | solution.py:550
  7.2 11.4 %collective-permute-start.2 = (bf16[2,3,32,640]{3,2,1,0:T(8,128)(2,1)S(1)}, bf16[2,3,32,640]{3,2,1,0:T(8,128)(2,1)S(1)}, u32[]{:S(2)}, u32[]{:S(2)}) collective-permute-start(bf16[2,3,32,640]{3,2,1,0:T(8,128)(2,1)S(1)} %pad_maximum_fusion.4.refs_2_), channel_id=1, source_target_pairs={{12,0},{0,4},{4,8},{8,12},{13,1},{1,5},{5,9},{9,13},{14,2},{2,6},{... | collective-permute-start | bytes 737288 | tf_op jit(solution)/shard_map/ppermute | solution.py:550
  12.8 7.1 %collective-permute-start.3 = (bf16[2,3,32,640]{3,2,1,0:T(8,128)(2,1)S(1)}, bf16[2,3,32,640]{3,2,1,0:T(8,128)(2,1)S(1)}, u32[]{:S(2)}, u32[]{:S(2)}) collective-permute-start(bf16[2,3,32,640]{3,2,1,0:T(8,128)(2,1)S(1)} %pad_maximum_fusion.4.refs_2_), channel_id=1, source_target_pairs={{4,0},{8,4},{12,8},{0,12},{5,1},{9,5},{13,9},{1,13},{6,2},{10,6},{... | collective-permute-start | bytes 737288 | tf_op jit(solution)/shard_map/ppermute | solution.py:550
  20.1 12.8 %collective-permute-start.5 = (bf16[3,3,32,640]{3,2,1,0:T(8,128)(2,1)S(1)}, bf16[3,3,32,640]{3,2,1,0:T(8,128)(2,1)S(1)}, u32[]{:S(2)}, u32[]{:S(2)}) collective-permute-start(bf16[3,3,32,640]{3,2,1,0:T(8,128)(2,1)S(1)} %pad_maximum_fusion.1), channel_id=1, source_target_pairs={{16,0},{32,16},{48,32},{64,48},{80,64},{96,80},{112,96},{0,112},{1... | collective-permute-start | bytes 1105928 | tf_op jit(solution)/shard_map/ppermute | solution.py:550
  23.4 12.3 %collective-permute-start.4 = (bf16[3,3,32,640]{3,2,1,0:T(8,128)(2,1)S(1)}, bf16[3,3,32,640]{3,2,1,0:T(8,128)(2,1)S(1)}, u32[]{:S(2)}, u32[]{:S(2)}) collective-permute-start(bf16[3,3,32,640]{3,2,1,0:T(8,128)(2,1)S(1)} %pad_maximum_fusion), channel_id=1, source_target_pairs={{112,0},{0,16},{16,32},{32,48},{48,64},{64,80},{80,96},{96,112},{1... | collective-permute-start | bytes 1105928 | tf_op jit(solution)/shard_map/ppermute | solution.py:550
  23.4 1.0 copy-start
  24.4 0.9 copy-start.2
  25.3 0.8 copy-start.4
  26.1 0.7 copy-start.6
  26.8 0.7 copy-start.8
  27.5 8.2 %copy-start.1 = (bf16[2,128,512]{2,1,0:T(8,128)(2,1)S(1)}, bf16[2,128,512]{2,1,0:T(8,128)(2,1)}, u32[]{:S(2)}) copy-start(bf16[2,128,512]{2,1,0:T(8,128)(2,1)} %refs_9_.3) | copy-start | bytes 786436
  27.5 8.2 %copy-start.3 = (bf16[2,64,512]{2,1,0:T(8,128)(2,1)S(1)}, bf16[2,64,512]{2,1,0:T(8,128)(2,1)}, u32[]{:S(2)}) copy-start(bf16[2,64,512]{2,1,0:T(8,128)(2,1)} %refs_6_.7) | copy-start | bytes 393220
  27.5 8.2 %copy-start.5 = (bf16[2,128,128]{2,1,0:T(8,128)(2,1)S(1)}, bf16[2,128,128]{2,1,0:T(8,128)(2,1)}, u32[]{:S(2)}) copy-start(bf16[2,128,128]{2,1,0:T(8,128)(2,1)} %refs_7_.7) | copy-start | bytes 196612
  27.5 8.2 %copy-start.7 = (s32[2,1,1]{0,2,1:T(1,128)S(1)}, s32[2,1,1]{0,2,1:T(1,128)}, u32[]{:S(2)}) copy-start(s32[2,1,1]{0,2,1:T(1,128)} %param.14) | copy-start | bytes 28
  27.5 8.2 %copy-start.9 = (f32[2,128]{1,0:T(2,128)S(1)}, f32[2,128]{1,0:T(2,128)}, u32[]{:S(2)}) copy-start(f32[2,128]{1,0:T(2,128)} %refs_8_.7) | copy-start | bytes 3076
  32.8 9.9 %copy-start.14 = (bf16[128,64]{0,1:T(8,128)(2,1)S(1)}, bf16[128,64]{0,1:T(8,128)(2,1)}, u32[]{:S(2)}) copy-start(bf16[128,64]{0,1:T(8,128)(2,1)} %param.23) | copy-start | bytes 49156
  39.9 4.4 %collective-permute-start.6 = (bf16[2,32,512]{2,1,0:T(8,128)(2,1)S(1)}, bf16[2,32,512]{2,1,0:T(8,128)(2,1)S(1)}, u32[]{:S(2)}, u32[]{:S(2)}) collective-permute-start(bf16[2,32,512]{2,1,0:T(8,128)(2,1)S(1)} %bitcast.43), channel_id=1, source_target_pairs={{3,0},{0,1},{1,2},{2,3},{7,4},{4,5},{5,6},{6,7},{11,8},{8,9},{9,10... | collective-permute-start | bytes 196616 | tf_op jit(solution)/shard_map/ppermute | solution.py:550
  41.2 3.1 %collective-permute-start.7 = (bf16[2,32,512]{2,1,0:T(8,128)(2,1)S(1)}, bf16[2,32,512]{2,1,0:T(8,128)(2,1)S(1)}, u32[]{:S(2)}, u32[]{:S(2)}) collective-permute-start(bf16[2,32,512]{2,1,0:T(8,128)(2,1)S(1)} %bitcast.44), channel_id=1, source_target_pairs={{1,0},{2,1},{3,2},{0,3},{5,4},{6,5},{7,6},{4,7},{9,8},{10,9},{11,1... | collective-permute-start | bytes 196616 | tf_op jit(solution)/shard_map/ppermute | solution.py:550
  44.4 9.6 %collective-permute-start.8 = (bf16[2,3,32,512]{3,2,0,1:T(8,128)(2,1)S(1)}, bf16[2,3,32,512]{3,2,0,1:T(8,128)(2,1)S(1)}, u32[]{:S(2)}, u32[]{:S(2)}) collective-permute-start(bf16[2,3,32,512]{3,2,0,1:T(8,128)(2,1)S(1)} %pad_maximum_fusion.5), channel_id=1, source_target_pairs={{12,0},{0,4},{4,8},{8,12},{13,1},{1,5},{5,9},{9,13},{14,2},{2,6},{... | collective-permute-start | bytes 589832 | tf_op jit(solution)/shard_map/ppermute | solution.py:550
  49.5 6.6 %collective-permute-start.9 = (bf16[2,3,32,512]{3,2,0,1:T(8,128)(2,1)S(1)}, bf16[2,3,32,512]{3,2,0,1:T(8,128)(2,1)S(1)}, u32[]{:S(2)}, u32[]{:S(2)}) collective-permute-start(bf16[2,3,32,512]{3,2,0,1:T(8,128)(2,1)S(1)} %pad_maximum_fusion.5), channel_id=1, source_target_pairs={{4,0},{8,4},{12,8},{0,12},{5,1},{9,5},{13,9},{1,13},{6,2},{10,6},{... | collective-permute-start | bytes 589832 | tf_op jit(solution)/shard_map/ppermute | solution.py:550
  49.5 1.6 %copy-start.11 = (f32[12,72,640]{2,1,0:T(8,128)S(1)}, f32[12,72,640]{2,1,0:T(8,128)}, u32[]{:S(2)}) copy-start(f32[12,72,640]{2,1,0:T(8,128)} %get-tuple-element.38.own_pairs.refs_9_) | copy-start | bytes 6635524
  51.1 15.1 %copy-start.12 = (f32[12,72,640]{2,1,0:T(8,128)S(1)}, f32[12,72,640]{2,1,0:T(8,128)}, u32[]{:S(2)}) copy-start(f32[12,72,640]{2,1,0:T(8,128)} %get-tuple-element.38.own_pairs.refs_9_) | copy-start | bytes 6635524
  51.1 15.1 %copy-start.13 = (bf16[640,576]{1,0:T(8,128)(2,1)S(1)}, bf16[640,576]{1,0:T(8,128)(2,1)}, u32[]{:S(2)}) copy-start(bf16[640,576]{1,0:T(8,128)(2,1)} %get-tuple-element.39.refs_10_) | copy-start | bytes 2211844
  56.1 14.7 %collective-permute-start.11 = (bf16[3,3,32,512]{3,2,0,1:T(8,128)(2,1)S(1)}, bf16[3,3,32,512]{3,2,0,1:T(8,128)(2,1)S(1)}, u32[]{:S(2)}, u32[]{:S(2)}) collective-permute-start(bf16[3,3,32,512]{3,2,0,1:T(8,128)(2,1)S(1)} %pad_maximum_fusion.3), channel_id=1, source_target_pairs={{16,0},{32,16},{48,32},{64,48},{80,64},{96,80},{112,96},{0,112},{1... | collective-permute-start | bytes 884744 | tf_op jit(solution)/shard_map/ppermute | solution.py:550
  66.1 8.9 %collective-permute-start.10 = (bf16[3,3,32,512]{3,2,0,1:T(8,128)(2,1)S(1)}, bf16[3,3,32,512]{3,2,0,1:T(8,128)(2,1)S(1)}, u32[]{:S(2)}, u32[]{:S(2)}) collective-permute-start(bf16[3,3,32,512]{3,2,0,1:T(8,128)(2,1)S(1)} %pad_maximum_fusion.2), channel_id=1, source_target_pairs={{112,0},{0,16},{16,32},{32,48},{48,64},{64,80},{80,96},{96,112},{1... | collective-permute-start | bytes 884744 | tf_op jit(solution)/shard_map/ppermute | solution.py:550
  66.2 8.8 %copy-start.10 = (f32[64]{0:T(128)S(1)}, f32[64]{0:T(128)}, u32[]{:S(2)}) copy-start(f32[64]{0:T(128)} %param.24) | copy-start | bytes 772

commit v2 on v0

--- a/solution.py
+++ b/solution.py
@@ -204,24 +204,29 @@
         step(count - 1, even, None)
 
 
-def own_kernel(layer, *refs):
+def ready_kernel(layer, *refs):
     counts_ref, low, middle, high = refs[:4]
-    weights = refs[4:9]
-    refs = refs[9:]
-    if layer == 0:
-        delta, pairs_out, order_out, more = refs[:4]
-        refs = refs[4:]
-        pairs, order, done = refs[12:]
+    weights = (None, None, *refs[4:7])
+    refs = refs[7:]
+    if layer == 0:
+        feats, refs = refs[:4], refs[4:]
+        pairs, order_out, more, order, done = refs
     else:
-        pairs, order, more, delta = refs[:4]
-        refs = refs[4:]
-    feats, edges = refs[:4], refs[4:12]
+        order, feats = refs[0], refs[1:]
     parts = [ref[...].reshape(own_atoms // 3, -1) for ref in (low, middle, high)]
     third = own_atoms // 3
     if layer == 0:
         geo = [p[:, 4 * chan :] + own_table(n) for n, p in enumerate(parts)]
         geo = jnp.concatenate(geo, axis=0)
         order[...], total = compaction(geo[:, 3:4].astype(f32), own_span)
+        keep = pltpu.make_async_copy(order, order_out, done.at[0])
+        keep.start()
+    x = None
+    for n in range(3):
+        y = dot(order[:, n * third : (n + 1) * third], parts[n][:, : 4 * chan])
+        x = y if n == 0 else x + y
+    features(layer, x.astype(bf16), slice(0, own_span), weights, feats)
+    if layer == 0:
         row = rows_of(dot(order[...], geo).astype(bf16))
         more[0] = jnp.where(jnp.sum(total) > own_main + 0.5, 1, 0)
         first = counts_ref[0]
@@ -234,26 +239,21 @@
         number = jnp.where(place < first, place + 1, place - first + (slots + 1))
         shift = jnp.where(place < first, 0.0, -cutoff)
         geometry(row, mine, number, shift, pairs, slice(0, 2 * slots))
-        keep = [
-            pltpu.make_async_copy(pairs, pairs_out, done.at[0]),
-            pltpu.make_async_copy(order, order_out, done.at[1]),
-        ]
-        for copy in keep:
-            copy.start()
-
-    def gathered(part):
-        x = None
-        for n in range(3):
-            y = dot(order[part, n * third : (n + 1) * third], parts[n][:, : 4 * chan])
-            x = y if n == 0 else x + y
-        features(layer, x.astype(bf16), part, weights, feats)
-
+        keep.wait()
+
+
+def own_kernel(layer, *refs):
+    counts_ref, weights, feats, pairs, more, delta = refs[0], refs[1:3], refs[3:7], *refs[7:10]
+    refs = refs[10:]
+    if layer == 0:
+        pairs_out, done, refs = refs[0], refs[-1], refs[1:-1]
+        keep = pltpu.make_async_copy(pairs, pairs_out, done.at[0])
+        keep.start()
+    edges = refs
+    count = (counts_ref[0] + counts_ref[1] + block - 1) // block
     delta[...] = jnp.zeros_like(delta)
-    main, rest = slice(0, own_main), slice(own_main, own_span)
-    count = (counts_ref[0] + counts_ref[1] + block - 1) // block
 
     def add(part):
-        gathered(part)
         messages(
             layer,
             count,
@@ -266,15 +266,14 @@
             delta,
         )
 
-    add(main)
+    add(slice(0, own_main))
 
     @pl.when(more[0] > 0)
     def _():
-        add(rest)
-
-    if layer == 0:
-        for copy in keep:
-            copy.wait()
+        add(slice(own_main, own_span))
+
+    if layer == 0:
+        keep.wait()
 
 
 def side_kernel(layer, last, *refs):
@@ -291,7 +290,8 @@
     else:
         state_ref, refs = refs[0], refs[1:]
     if layer == 0:
-        (pairs, order, more), refs = refs[:3], refs[3:]
+        (pairs, order_out, more), refs = refs[:3], refs[3:]
+        order, done = refs[13:]
     feats, edges, delta = refs[:4], refs[4:12], refs[12]
     delta[...] = jnp.zeros_like(delta)
     main, rest = slice(0, side_main), slice(side_main, side_span)
@@ -308,6 +308,8 @@
             number = lax.broadcasted_iota(jnp.int32, (slots, 1), 0) + (q * slots + 1)
             geometry(row, mine, number, (-cutoff, cutoff)[q], pairs, at)
         more[0] = jnp.where(jnp.maximum(total[0], total[1]) > side_main + 0.5, 1, 0)
+        keep = pltpu.make_async_copy(order, order_out, done.at[0])
+        keep.start()
     below = (counts_ref[0] + block - 1) // block
     above = (counts_ref[1] + block - 1) // block
 
@@ -337,6 +339,8 @@
     moved = pltpu.roll(packed, slots - counts_ref[0], 0)
     change = delta[0 : 2 * slots, :] + jnp.where(slot < slots, packed, moved)
     state = ((mine + message_scale * change) * live).astype(bf16)
+    if layer == 0:
+        keep.wait()
     if not last:
         state_ref[...] = state
     else:
@@ -384,24 +388,41 @@
 kept_specs = (vmem, vmem, smem)
 
 
-def own_call(layer, counts, ys, weights, kept):
-    operands = [counts, *ys, *weights]
-    specs = [smem] + [vmem] * (len(operands) - 1)
-    shapes, outs = (delta_shape,), (vmem,)
-    held = scratch(own_span, own_main)
-    if layer == 0:
-        kept_out = kept_shapes(own_span, (own_span, own_atoms))
-        shapes += tuple(pltpu.HBM(k.shape, k.dtype) for k in kept_out[:2]) + kept_out[2:]
-        outs += (hbm, hbm, smem)
-        held += [pltpu.VMEM(k.shape, k.dtype) for k in kept_out[:2]]
-        held += [pltpu.SemaphoreType.DMA((2,))]
-    else:
-        operands += kept
-        specs += kept_specs
+def feature_shapes(rows):
+    return [jax.ShapeDtypeStruct((rows, width * chan), bf16) for width in (4, 2, 2, 2)]
+
+
+def ready_call(layer, counts, ys, weights, order):
+    operands = [counts, *ys, *weights[2:]] + ([] if layer == 0 else [order])
+    shapes, outs, held = feature_shapes(own_span), [vmem] * 4, []
+    if layer == 0:
+        pairs, order, more = kept_shapes(own_span, (own_span, own_atoms))
+        shapes += [pairs, pltpu.HBM(order.shape, order.dtype), more]
+        outs += [vmem, hbm, smem]
+        held = [pltpu.VMEM(order.shape, order.dtype), pltpu.SemaphoreType.DMA((1,))]
+    return pl.pallas_call(
+        functools.partial(ready_kernel, layer),
+        out_shape=shapes,
+        in_specs=[smem] + [vmem] * (len(operands) - 1),
+        out_specs=outs,
+        scratch_shapes=held,
+        compiler_params=params,
+        name=f"ready_part_{layer}",
+    )(*operands)
+
+
+def own_call(layer, counts, weights, feats, pairs, more):
+    operands = [counts, *weights[:2], *feats, pairs, more]
+    shapes, outs = [delta_shape], [vmem]
+    held = [pltpu.VMEM((block * hidden, own_main), bf16)] * 8
+    if layer == 0:
+        shapes.append(pltpu.HBM(pairs.shape, pairs.dtype))
+        outs.append(hbm)
+        held.append(pltpu.SemaphoreType.DMA((1,)))
     return pl.pallas_call(
         functools.partial(own_kernel, layer),
         out_shape=shapes,
-        in_specs=specs,
+        in_specs=[smem] + [vmem] * (len(operands) - 2) + [smem],
         out_specs=outs,
         scratch_shapes=held,
         compiler_params=params,
@@ -423,9 +444,12 @@
             jax.ShapeDtypeStruct((chan, chan), f32),
         )
         outs = (vmem,) * 3
-    if layer == 0:
-        shapes += kept_shapes(side_span, (2, side_span, side_atoms))
-        outs += kept_specs
+    held = scratch(2 * side_span, side_main) + [pltpu.VMEM(delta_shape.shape, f32)]
+    if layer == 0:
+        pairs, order, more = kept_shapes(side_span, (2, side_span, side_atoms))
+        shapes += (pairs, pltpu.HBM(order.shape, order.dtype), more)
+        outs += (vmem, hbm, smem)
+        held += [pltpu.VMEM(order.shape, order.dtype), pltpu.SemaphoreType.DMA((1,))]
     else:
         operands += kept
         specs += kept_specs
@@ -434,7 +458,7 @@
         out_shape=shapes,
         in_specs=specs,
         out_specs=outs,
-        scratch_shapes=scratch(2 * side_span, side_main) + [pltpu.VMEM(delta_shape.shape, f32)],
+        scratch_shapes=held,
         compiler_params=params,
         cost_estimate=cost(side_atoms),
         name=f"side_part_{layer}",
@@ -528,7 +552,7 @@
         vectors.reshape(2, slots, 3, chan).transpose(0, 2, 1, 3),
     )
     layers = radial_in.shape[0]
-    own_kept = side_kept = ()
+    side_kept = ()
     for layer in range(layers):
         last = layer == layers - 1
         y = jnp.stack([shifted(own, "gz", -1), own, shifted(own, "gz", 1)], axis=1)
@@ -537,10 +561,16 @@
             rin = radial_rows(radial_in, radial_bias)
             weights = [rin, radial_out, atom_in, atom_bias, atom_out]
         ys = [shifted(y, "gy", -1), y, shifted(y, "gy", 1)]
-        low = shifted(jnp.stack([v[1] for v in ys]), "gx", -1)
-        high = shifted(jnp.stack([v[0] for v in ys]), "gx", 1)
-        delta, *kept = own_call(layer, counts, ys, weights, own_kept)
-        own_kept = own_kept or kept
+        if layer == 0:
+            *feats, pairs, order, more = ready_call(layer, counts, ys, weights, None)
+        else:
+            feats = ready_call(layer, counts, ys, weights, order)
+        low, high = jnp.stack([v[1] for v in ys]), jnp.stack([v[0] for v in ys])
+        low, high, feats = lax.optimization_barrier((low, high, feats))
+        low, high = shifted(low, "gx", -1), shifted(high, "gx", 1)
+        delta, *kept = own_call(layer, counts, weights, feats, pairs, more)
+        if layer == 0:
+            pairs = kept[0]
         readout = [readout_in, readout_out[None, :]]
         state, *kept = side_call(
             layer, last, counts, low, high, own, delta, weights, readout, side_kept

time: 95.9 us -> 94.1 us (0.981); the launches traced: 94.8 us -> 94 us
  waiting for transfers between devices: 25.4 us -> 22.4 us
  blocking collectives: 19.8 us -> 22.7 us
    pallas_call x2, Pallas kernels: 10.4 us -> 4.16 us  [own_call(): pl.pallas_call(functools.partial(own_kernel, layer), out_shape=shapes, in...]
    pallas_call x0 -> x2, Pallas kernels: none -> 5.46 us  [ready_call(): pl.pallas_call(functools.partial(ready_kernel, layer), out_shape=shapes,...]
    ppermute x12, waiting for transfers between devices: 25.4 us -> 22.4 us  [shifted(): lax.ppermute(value, axis, [((i + step) % count, i) for i in range(count)])]
    all_to_all x1, blocking collectives: 19.8 us -> 22.7 us  [on_device(): every = lax.all_to_all(energy, ('gx', 'gy', 'gz'), 0, 0, tiled=True)]
  transfers between devices with their start and end apart: 12 -> 12, of which waited for: 11 -> 8; matrix products, arithmetic and copies ran while one was open for 4% -> 4% of each run, Pallas kernels for 11% -> 4%
where the time goes in v2:
time: 94.1 us; the launch traced here: 94 us
  starting transfers between devices  25.2 us (27%)
  blocking collectives  22.7 us (24%)
  waiting for transfers between devices  22.4 us (24%)
  Pallas kernels  18.4 us (20%)
  local copies, waits for them, and re-layouts  2.66 us (3%)
  other arithmetic  1.8 us (2%)
  between operations  0.98 us (1%)
    ppermute x12, starting transfers between devices, shifted(): lax.ppermute(value, axis, [((i + step) % count, i) for i in range(count)])  25.2 us
    all_to_all x1, blocking collectives, on_device(): every = lax.all_to_all(energy, ('gx', 'gy', 'gz'), 0, 0, tiled=True)  22.7 us
    ppermute x12, waiting for transfers between devices, shifted(): lax.ppermute(value, axis, [((i + step) % count, i) for i in range(count)])  22.4 us
    pallas_call x2, Pallas kernels, side_call(): pl.pallas_call(functools.partial(side_kernel, layer, last), out_shape=sha...  7.63 us
    pallas_call x2, Pallas kernels, ready_call(): pl.pallas_call(functools.partial(ready_kernel, layer), out_shape=shapes,...  5.46 us
    pallas_call x2, Pallas kernels, own_call(): pl.pallas_call(functools.partial(own_kernel, layer), out_shape=shapes, in...  4.16 us
    mul x6, local copies, waits for them, and re-layouts, radial_rows(): radial_in.transpose(0, 2, 1)[:, None, :, :, None] * eye[:, None, None, :]  2.13 us
  transfers between devices with their start and end apart: 12, of which 8 were waited for; matrix products, arithmetic and copies ran while one was open for 4% of the time, Pallas kernels for 4%

profile of v2, /device:TPU:1, one launch (start us, length us, event | category | flops | bytes accessed | tf_op | source)
XLA Modules:
  0.0 94.0 jit_solution(70012239837630879)
XLA Ops:
  0.6 1.1 %pack.1.refs_3_ = bf16[2,32,640]{2,1,0:T(8,128)(2,1)S(1)} custom-call(s32[2]{0:T(128)} %bitcast.48, f32[2,3,1,32]{3,2,1,0:T(1,128)} %bitcast.64, bf16[2,32,128]{2,1,0:T(8,128)(2,1)} %bitcast.62, bf16[2,3,32,128]{3,2,1,0:T(8,128)(2,1)} %bitcast.61), custom_call_target="tpu_custom_call" | custom-call | tf_op jit(solution)/shard_map/pack/pallas_call | solution.py:500
  1.7 3.4 %collective-permute-start.1 = (bf16[2,32,640]{2,1,0:T(8,128)(2,1)S(1)}, bf16[2,32,640]{2,1,0:T(8,128)(2,1)S(1)}, u32[]{:S(2)}, u32[]{:S(2)}) collective-permute-start(bf16[2,32,640]{2,1,0:T(8,128)(2,1)S(1)} %pack.1.refs_3_), channel_id=1, source_target_pairs={{1,0},{2,1},{3,2},{0,3},{5,4},{6,5},{7,6},{4,7},{9,8},{10,9},{11,1... | collective-permute-start | bytes 245768 | tf_op jit(solution)/shard_map/ppermute | solution.py:517
  5.1 0.0 collective-permute-start
  5.1 0.8 mul.31
  5.9 0.1 mul.32
  6.0 0.1 copy.37
  6.2 0.4 collective-permute-done.1
  6.6 3.0 %collective-permute-done = bf16[2,32,640]{2,1,0:T(8,128)(2,1)S(1)} collective-permute-done((bf16[2,32,640]{2,1,0:T(8,128)(2,1)S(1)}, bf16[2,32,640]{2,1,0:T(8,128)(2,1)S(1)}, u32[]{:S(2)}, u32[]{:S(2)}) %collective-permute-start) | collective-permute-done | bytes 81952 | tf_op jit(solution)/shard_map/ppermute | solution.py:517
  9.7 2.2 %collective-permute-start.3 = (bf16[2,3,32,640]{3,2,1,0:T(8,128)(2,1)S(1)}, bf16[2,3,32,640]{3,2,1,0:T(8,128)(2,1)S(1)}, u32[]{:S(2)}, u32[]{:S(2)}) collective-permute-start(bf16[2,3,32,640]{3,2,1,0:T(8,128)(2,1)S(1)} %pad_maximum_fusion.4.refs_2_), channel_id=1, source_target_pairs={{4,0},{8,4},{12,8},{0,12},{5,1},{9,5},{13,9},{1,13},{6,2},{10,6},{... | collective-permute-start | bytes 737288 | tf_op jit(solution)/shard_map/ppermute | solution.py:517
  11.8 3.6 %collective-permute-start.2 = (bf16[2,3,32,640]{3,2,1,0:T(8,128)(2,1)S(1)}, bf16[2,3,32,640]{3,2,1,0:T(8,128)(2,1)S(1)}, u32[]{:S(2)}, u32[]{:S(2)}) collective-permute-start(bf16[2,3,32,640]{3,2,1,0:T(8,128)(2,1)S(1)} %pad_maximum_fusion.4.refs_2_), channel_id=1, source_target_pairs={{12,0},{0,4},{4,8},{8,12},{13,1},{1,5},{5,9},{9,13},{14,2},{2,6},{... | collective-permute-start | bytes 737288 | tf_op jit(solution)/shard_map/ppermute | solution.py:517
  15.4 0.7 fusion.6
  16.1 0.1 copy.39
  16.2 0.7 mul.29
  16.9 0.2 mul.30
  17.2 0.2 copy.38
  17.3 0.0 copy-start
  17.3 0.0 copy-start.2
  17.4 0.0 copy-start.3
  17.4 0.0 copy-start.4
  17.5 0.0 copy-start.5
  17.5 0.2 fusion.2.refs_1_.refs_5_
  17.7 3.5 %collective-permute-done.3.refs_3_ = bf16[2,3,32,640]{3,2,1,0:T(8,128)(2,1)S(1)} collective-permute-done((bf16[2,3,32,640]{3,2,1,0:T(8,128)(2,1)S(1)}, bf16[2,3,32,640]{3,2,1,0:T(8,128)(2,1)S(1)}, u32[]{:S(2)}, u32[]{:S(2)}) %collective-permute-start.3) | collective-permute-done | bytes 245792 | tf_op jit(solution)/shard_map/ppermute | solution.py:517
  21.2 0.0 collective-permute-done.2.refs_1_
  21.2 0.1 pad_maximum_fusion
  21.4 3.9 %ready_part_0.1 = (bf16[640,512]{1,0:T(8,128)(2,1)S(1)}, bf16[640,256]{1,0:T(8,128)(2,1)S(1)}, bf16[640,256]{1,0:T(8,128)(2,1)S(1)}, bf16[640,256]{1,0:T(8,128)(...) custom-call(s32[2]{0:T(128)S(1)} %bitcast.49, ...), custom_call_target="tpu_custom_call" | custom-call | tf_op jit(solution)/shard_map/ready_part_0/pallas_call | solution.py:403
  25.3 1.4 %collective-permute-start.4 = (bf16[3,3,32,640]{3,2,1,0:T(8,128)(2,1)S(1)}, bf16[3,3,32,640]{3,2,1,0:T(8,128)(2,1)S(1)}, u32[]{:S(2)}, u32[]{:S(2)}) collective-permute-start(bf16[3,3,32,640]{3,2,1,0:T(8,128)(2,1)S(1)} %get-tuple-element.43), channel_id=1, source_target_pairs={{112,0},{0,16},{16,32},{32,48},{48,64},{64,80},{80,96},{96,112},{1... | collective-permute-start | bytes 1105928 | tf_op jit(solution)/shard_map/ppermute | solution.py:517
  26.7 2.3 %collective-permute-start.5 = (bf16[3,3,32,640]{3,2,1,0:T(8,128)(2,1)S(1)}, bf16[3,3,32,640]{3,2,1,0:T(8,128)(2,1)S(1)}, u32[]{:S(2)}, u32[]{:S(2)}) collective-permute-start(bf16[3,3,32,640]{3,2,1,0:T(8,128)(2,1)S(1)} %get-tuple-element.44), channel_id=1, source_target_pairs={{16,0},{32,16},{48,32},{64,48},{80,64},{96,80},{112,96},{0,112},{1... | collective-permute-start | bytes 1105928 | tf_op jit(solution)/shard_map/ppermute | solution.py:517
  29.0 2.1 %own_part_0.1 = (f32[72,512]{1,0:T(8,128)S(1)}, f32[12,72,640]{2,1,0:T(8,128)}) custom-call(s32[2]{0:T(128)S(1)} %bitcast.50, bf16[2,512,80]{2,1,0:T(8,128)(2,1)S(1)} %fusion.2.refs_1_.refs_5_, bf16[2,64,512]{2,1,0:T(8,128)(2,1)S(1)} %copy-done.5, bf16[640,512]{1,0:T(8,128)(2,1)S(1)} %get-tuple-element.47.refs_3_, ...), custom_call_target="tpu_custom_call" | custom-call | flops 6039797760 | bytes 4000000 | tf_op jit(solution)/shard_map/own_part_0/pallas_call | solution.py:422
  31.1 5.2 %collective-permute-done.4.refs_1_ = bf16[3,3,32,640]{3,2,1,0:T(8,128)(2,1)S(1)} collective-permute-done((bf16[3,3,32,640]{3,2,1,0:T(8,128)(2,1)S(1)}, bf16[3,3,32,640]{3,2,1,0:T(8,128)(2,1)S(1)}, u32[]{:S(2)}, u32[]{:S(2)}) %collective-permute-start.4) | collective-permute-done | bytes 368672 | tf_op jit(solution)/shard_map/ppermute | solution.py:517
  36.3 0.0 collective-permute-done.5.refs_2_
  36.3 4.3 %side_part_0.1 = (bf16[64,512]{1,0:T(8,128)(2,1)S(1)}, f32[12,72,384]{2,1,0:T(8,128)S(1)}, bf16[2,384,288]{2,1,0:T(8,128)(2,1)}, s32[2]{0:T(128)S(1)}) custom-call(s32[2]{0:T(128)S(1)} %bitcast.51, bf16[3,3,32,640]{3,2,1,0:T(8,128)(2,1)S(1)} %collective-permute-done.4.refs_1_, bf16[3,3,32,640]{3,2,1,0:T(8,128)(2,1)S(1)} %collective-permute-done.5.refs_2_, ...), custom_call_target="tpu_custom_call" | custom-call | flops 3019898880 | bytes 4000000 | tf_op jit(solution)/shard_map/side_part_0/pallas_call | solution.py:456
  40.6 0.1 collective-permute-start.7
  40.7 1.5 %collective-permute-start.6 = (bf16[2,32,512]{2,1,0:T(8,128)(2,1)S(1)}, bf16[2,32,512]{2,1,0:T(8,128)(2,1)S(1)}, u32[]{:S(2)}, u32[]{:S(2)}) collective-permute-start(bf16[2,32,512]{2,1,0:T(8,128)(2,1)S(1)} %bitcast.45), channel_id=1, source_target_pairs={{3,0},{0,1},{1,2},{2,3},{7,4},{4,5},{5,6},{6,7},{11,8},{8,9},{9,10... | collective-permute-start | bytes 196616 | tf_op jit(solution)/shard_map/ppermute | solution.py:517
  42.1 0.1 copy.45.refs_10_
  42.2 1.5 %collective-permute-done.7 = bf16[2,32,512]{2,1,0:T(8,128)(2,1)S(1)} collective-permute-done((bf16[2,32,512]{2,1,0:T(8,128)(2,1)S(1)}, bf16[2,32,512]{2,1,0:T(8,128)(2,1)S(1)}, u32[]{:S(2)}, u32[]{:S(2)}) %collective-permute-start.7) | collective-permute-done | bytes 65568 | tf_op jit(solution)/shard_map/ppermute | solution.py:517
  43.8 1.3 %collective-permute-done.6 = bf16[2,32,512]{2,1,0:T(8,128)(2,1)S(1)} collective-permute-done((bf16[2,32,512]{2,1,0:T(8,128)(2,1)S(1)}, bf16[2,32,512]{2,1,0:T(8,128)(2,1)S(1)}, u32[]{:S(2)}, u32[]{:S(2)}) %collective-permute-start.6) | collective-permute-done | bytes 65568 | tf_op jit(solution)/shard_map/ppermute | solution.py:517
  45.1 3.5 %collective-permute-start.9 = (bf16[2,3,32,512]{3,2,0,1:T(8,128)(2,1)S(1)}, bf16[2,3,32,512]{3,2,0,1:T(8,128)(2,1)S(1)}, u32[]{:S(2)}, u32[]{:S(2)}) collective-permute-start(bf16[2,3,32,512]{3,2,0,1:T(8,128)(2,1)S(1)} %pad_maximum_fusion.5), channel_id=1, source_target_pairs={{4,0},{8,4},{12,8},{0,12},{5,1},{9,5},{13,9},{1,13},{6,2},{10,6},{... | collective-permute-start | bytes 589832 | tf_op jit(solution)/shard_map/ppermute | solution.py:517
  48.5 1.4 %collective-permute-start.8 = (bf16[2,3,32,512]{3,2,0,1:T(8,128)(2,1)S(1)}, bf16[2,3,32,512]{3,2,0,1:T(8,128)(2,1)S(1)}, u32[]{:S(2)}, u32[]{:S(2)}) collective-permute-start(bf16[2,3,32,512]{3,2,0,1:T(8,128)(2,1)S(1)} %pad_maximum_fusion.5), channel_id=1, source_target_pairs={{12,0},{0,4},{4,8},{8,12},{13,1},{1,5},{5,9},{9,13},{14,2},{2,6},{... | collective-permute-start | bytes 589832 | tf_op jit(solution)/shard_map/ppermute | solution.py:517
  50.0 4.2 %collective-permute-done.9 = bf16[2,3,32,512]{3,2,0,1:T(8,128)(2,1)S(1)} collective-permute-done((bf16[2,3,32,512]{3,2,0,1:T(8,128)(2,1)S(1)}, bf16[2,3,32,512]{3,2,0,1:T(8,128)(2,1)S(1)}, u32[]{:S(2)}, u32[]{:S(2)}) %collective-permute-start.9) | collective-permute-done | bytes 196640 | tf_op jit(solution)/shard_map/ppermute | solution.py:517
  54.4 1.5 %ready_part_1.1 = (bf16[640,512]{1,0:T(8,128)(2,1)S(1)}, bf16[640,256]{1,0:T(8,128)(2,1)S(1)}, bf16[640,256]{1,0:T(8,128)(2,1)S(1)}, bf16[640,256]{1,0:T(8,128)(2,1)S(1)}) custom-call(s32[2]{0:T(128)S(1)} %bitcast.52, bf16[2,3,32,512]{3,2,1,0:T(8,128)(2,1)S(1)} %copy.40.refs_1_, bf16[2,3,32,512]{3,2,1,0:T(8,128)(2,1)S(1)} %copy.41.refs_2_, ...), custom_call_target="tpu_custom_call" | custom-call | tf_op jit(solution)/shard_map/ready_part_1/pallas_call | solution.py:403
  55.9 0.6 collective-permute-start.10
  56.5 5.5 %collective-permute-start.11 = (bf16[3,3,32,512]{3,2,0,1:T(8,128)(2,1)S(1)}, bf16[3,3,32,512]{3,2,0,1:T(8,128)(2,1)S(1)}, u32[]{:S(2)}, u32[]{:S(2)}) collective-permute-start(bf16[3,3,32,512]{3,2,0,1:T(8,128)(2,1)S(1)} %pad_maximum_fusion.3), channel_id=1, source_target_pairs={{16,0},{32,16},{48,32},{64,48},{80,64},{96,80},{112,96},{0,112},{1... | collective-permute-start | bytes 884744 | tf_op jit(solution)/shard_map/ppermute | solution.py:517
  62.0 2.1 %own_part_1.1.refs_4_ = f32[72,512]{1,0:T(8,128)S(1)} custom-call(s32[2]{0:T(128)S(1)} %bitcast.53, bf16[2,512,80]{2,1,0:T(8,128)(2,1)S(1)} %fusion.2.refs_1_.refs_5_, bf16[2,64,512]{2,1,0:T(8,128)(2,1)S(1)} %copy-done.5, bf16[640,512]{1,0:T(8,128)(2,1)S(1)} %get-tuple-element.62.refs_3_, bf16[640,256]{1,0:T(8,128)(2,1)S(1)} %get-tuple-element.63.refs_4_, ...), custom_call_target="tpu_custom_call" | custom-call | flops 6039797760 | bytes 4000000 | tf_op jit(solution)/shard_map/own_part_1/pallas_call | solution.py:422
  64.1 3.1 %collective-permute-done.10 = bf16[3,3,32,512]{3,2,0,1:T(8,128)(2,1)S(1)} collective-permute-done((bf16[3,3,32,512]{3,2,0,1:T(8,128)(2,1)S(1)}, bf16[3,3,32,512]{3,2,0,1:T(8,128)(2,1)S(1)}, u32[]{:S(2)}, u32[]{:S(2)}) %collective-permute-start.10) | collective-permute-done | bytes 294944 | tf_op jit(solution)/shard_map/ppermute | solution.py:517
  67.2 0.0 collective-permute-done.11
  67.3 3.4 %side_part_1.1 = (bf16[2,32,128]{2,1,0:T(8,128)(2,1)}, bf16[2,3,32,128]{3,2,1,0:T(8,128)(2,1)}, f32[128,128]{1,0:T(8,128)S(1)}) custom-call(s32[2]{0:T(128)S(1)} %bitcast.54, bf16[3,3,32,512]{3,2,1,0:T(8,128)(2,1)S(1)} %copy.43.refs_1_, bf16[3,3,32,512]{3,2,1,0:T(8,128)(2,1)S(1)} %copy.44.refs_2_, bf16[2,32,512]{2,1,0:T(8,128)(2,1)S(1)} %bitcast.47, ...), custom_call_target="tpu_custom_call" | custom-call | flops 3019898880 | bytes 4000000 | tf_op jit(solution)/shard_map/side_part_1/pallas_call | solution.py:456
  70.7 22.7 %all_to_all.9 = f32[128,1,128]{2,1,0:T(1,128)S(1)} all-to-all(f32[128,1,128]{2,1,0:T(1,128)S(1)} %bitcast.43), channel_id=1, replica_groups=mesh['gx'=8,'gy'=4,'gz'=4] {'gx','gy','gz'}, dimensions={0} | all-to-all | bytes 131072 | tf_op jit(solution)/shard_map/all_to_all | solution.py:585
  93.4 0.7 reduce_sum.9
  (34 shorter events, 0.4 us)
Async XLA Ops:
  1.7 4.9 %collective-permute-start.1 = (bf16[2,32,640]{2,1,0:T(8,128)(2,1)S(1)}, bf16[2,32,640]{2,1,0:T(8,128)(2,1)S(1)}, u32[]{:S(2)}, u32[]{:S(2)}) collective-permute-start(bf16[2,32,640]{2,1,0:T(8,128)(2,1)S(1)} %pack.1.refs_3_), channel_id=1, source_target_pairs={{1,0},{2,1},{3,2},{0,3},{5,4},{6,5},{7,6},{4,7},{9,8},{10,9},{11,1... | collective-permute-start | bytes 245768 | tf_op jit(solution)/shard_map/ppermute | solution.py:517
  5.1 4.5 %collective-permute-start = (bf16[2,32,640]{2,1,0:T(8,128)(2,1)S(1)}, bf16[2,32,640]{2,1,0:T(8,128)(2,1)S(1)}, u32[]{:S(2)}, u32[]{:S(2)}) collective-permute-start(bf16[2,32,640]{2,1,0:T(8,128)(2,1)S(1)} %pack.1.refs_3_), channel_id=1, source_target_pairs={{3,0},{0,1},{1,2},{2,3},{7,4},{4,5},{5,6},{6,7},{11,8},{8,9},{9,10... | collective-permute-start | bytes 245768 | tf_op jit(solution)/shard_map/ppermute | solution.py:517
  9.7 11.5 %collective-permute-start.3 = (bf16[2,3,32,640]{3,2,1,0:T(8,128)(2,1)S(1)}, bf16[2,3,32,640]{3,2,1,0:T(8,128)(2,1)S(1)}, u32[]{:S(2)}, u32[]{:S(2)}) collective-permute-start(bf16[2,3,32,640]{3,2,1,0:T(8,128)(2,1)S(1)} %pad_maximum_fusion.4.refs_2_), channel_id=1, source_target_pairs={{4,0},{8,4},{12,8},{0,12},{5,1},{9,5},{13,9},{1,13},{6,2},{10,6},{... | collective-permute-start | bytes 737288 | tf_op jit(solution)/shard_map/ppermute | solution.py:517
  11.8 9.4 %collective-permute-start.2 = (bf16[2,3,32,640]{3,2,1,0:T(8,128)(2,1)S(1)}, bf16[2,3,32,640]{3,2,1,0:T(8,128)(2,1)S(1)}, u32[]{:S(2)}, u32[]{:S(2)}) collective-permute-start(bf16[2,3,32,640]{3,2,1,0:T(8,128)(2,1)S(1)} %pad_maximum_fusion.4.refs_2_), channel_id=1, source_target_pairs={{12,0},{0,4},{4,8},{8,12},{13,1},{1,5},{5,9},{9,13},{14,2},{2,6},{... | collective-permute-start | bytes 737288 | tf_op jit(solution)/shard_map/ppermute | solution.py:517
  17.3 4.0 %copy-start = (bf16[2,128,512]{2,1,0:T(8,128)(2,1)S(1)}, bf16[2,128,512]{2,1,0:T(8,128)(2,1)}, u32[]{:S(2)}) copy-start(bf16[2,128,512]{2,1,0:T(8,128)(2,1)} %refs_9_.3) | copy-start | bytes 786436
  17.3 4.0 %copy-start.2 = (bf16[2,128,128]{2,1,0:T(8,128)(2,1)S(1)}, bf16[2,128,128]{2,1,0:T(8,128)(2,1)}, u32[]{:S(2)}) copy-start(bf16[2,128,128]{2,1,0:T(8,128)(2,1)} %refs_7_.3) | copy-start | bytes 196612
  17.4 4.0 %copy-start.3 = (s32[2,1,1]{0,2,1:T(1,128)S(1)}, s32[2,1,1]{0,2,1:T(1,128)}, u32[]{:S(2)}) copy-start(s32[2,1,1]{0,2,1:T(1,128)} %param.14) | copy-start | bytes 28
  17.4 4.0 %copy-start.4 = (f32[2,128]{1,0:T(2,128)S(1)}, f32[2,128]{1,0:T(2,128)}, u32[]{:S(2)}) copy-start(f32[2,128]{1,0:T(2,128)} %refs_8_.3) | copy-start | bytes 3076
  17.5 11.5 %copy-start.5 = (bf16[2,64,512]{2,1,0:T(8,128)(2,1)S(1)}, bf16[2,64,512]{2,1,0:T(8,128)(2,1)}, u32[]{:S(2)}) copy-start(bf16[2,64,512]{2,1,0:T(8,128)(2,1)} %refs_6_.7) | copy-start | bytes 393220
  25.3 10.9 %collective-permute-start.4 = (bf16[3,3,32,640]{3,2,1,0:T(8,128)(2,1)S(1)}, bf16[3,3,32,640]{3,2,1,0:T(8,128)(2,1)S(1)}, u32[]{:S(2)}, u32[]{:S(2)}) collective-permute-start(bf16[3,3,32,640]{3,2,1,0:T(8,128)(2,1)S(1)} %get-tuple-element.43), channel_id=1, source_target_pairs={{112,0},{0,16},{16,32},{32,48},{48,64},{64,80},{80,96},{96,112},{1... | collective-permute-start | bytes 1105928 | tf_op jit(solution)/shard_map/ppermute | solution.py:517
  26.7 9.6 %collective-permute-start.5 = (bf16[3,3,32,640]{3,2,1,0:T(8,128)(2,1)S(1)}, bf16[3,3,32,640]{3,2,1,0:T(8,128)(2,1)S(1)}, u32[]{:S(2)}, u32[]{:S(2)}) collective-permute-start(bf16[3,3,32,640]{3,2,1,0:T(8,128)(2,1)S(1)} %get-tuple-element.44), channel_id=1, source_target_pairs={{16,0},{32,16},{48,32},{64,48},{80,64},{96,80},{112,96},{0,112},{1... | collective-permute-start | bytes 1105928 | tf_op jit(solution)/shard_map/ppermute | solution.py:517
  36.3 5.8 %copy-start.9 = (bf16[128,64]{0,1:T(8,128)(2,1)S(1)}, bf16[128,64]{0,1:T(8,128)(2,1)}, u32[]{:S(2)}) copy-start(bf16[128,64]{0,1:T(8,128)(2,1)} %param.23) | copy-start | bytes 49156
  40.6 13.8 %copy-start.1 = (bf16[640,576]{1,0:T(8,128)(2,1)S(1)}, bf16[640,576]{1,0:T(8,128)(2,1)}, u32[]{:S(2)}) copy-start(bf16[640,576]{1,0:T(8,128)(2,1)} %get-tuple-element.55.refs_7_) | copy-start | bytes 2211844
  40.6 3.2 %collective-permute-start.7 = (bf16[2,32,512]{2,1,0:T(8,128)(2,1)S(1)}, bf16[2,32,512]{2,1,0:T(8,128)(2,1)S(1)}, u32[]{:S(2)}, u32[]{:S(2)}) collective-permute-start(bf16[2,32,512]{2,1,0:T(8,128)(2,1)S(1)} %bitcast.44), channel_id=1, source_target_pairs={{1,0},{2,1},{3,2},{0,3},{5,4},{6,5},{7,6},{4,7},{9,8},{10,9},{11,1... | collective-permute-start | bytes 196616 | tf_op jit(solution)/shard_map/ppermute | solution.py:517
  40.7 4.4 %collective-permute-start.6 = (bf16[2,32,512]{2,1,0:T(8,128)(2,1)S(1)}, bf16[2,32,512]{2,1,0:T(8,128)(2,1)S(1)}, u32[]{:S(2)}, u32[]{:S(2)}) collective-permute-start(bf16[2,32,512]{2,1,0:T(8,128)(2,1)S(1)} %bitcast.45), channel_id=1, source_target_pairs={{3,0},{0,1},{1,2},{2,3},{7,4},{4,5},{5,6},{6,7},{11,8},{8,9},{9,10... | collective-permute-start | bytes 196616 | tf_op jit(solution)/shard_map/ppermute | solution.py:517
  45.1 9.1 %collective-permute-start.9 = (bf16[2,3,32,512]{3,2,0,1:T(8,128)(2,1)S(1)}, bf16[2,3,32,512]{3,2,0,1:T(8,128)(2,1)S(1)}, u32[]{:S(2)}, u32[]{:S(2)}) collective-permute-start(bf16[2,3,32,512]{3,2,0,1:T(8,128)(2,1)S(1)} %pad_maximum_fusion.5), channel_id=1, source_target_pairs={{4,0},{8,4},{12,8},{0,12},{5,1},{9,5},{13,9},{1,13},{6,2},{10,6},{... | collective-permute-start | bytes 589832 | tf_op jit(solution)/shard_map/ppermute | solution.py:517
  48.5 5.6 %collective-permute-start.8 = (bf16[2,3,32,512]{3,2,0,1:T(8,128)(2,1)S(1)}, bf16[2,3,32,512]{3,2,0,1:T(8,128)(2,1)S(1)}, u32[]{:S(2)}, u32[]{:S(2)}) collective-permute-start(bf16[2,3,32,512]{3,2,0,1:T(8,128)(2,1)S(1)} %pad_maximum_fusion.5), channel_id=1, source_target_pairs={{12,0},{0,4},{4,8},{8,12},{13,1},{1,5},{5,9},{9,13},{14,2},{2,6},{... | collective-permute-start | bytes 589832 | tf_op jit(solution)/shard_map/ppermute | solution.py:517
  49.9 12.0 %copy-start.8 = (f32[12,72,640]{2,1,0:T(8,128)S(1)}, f32[12,72,640]{2,1,0:T(8,128)}, u32[]{:S(2)}) copy-start(f32[12,72,640]{2,1,0:T(8,128)} %get-tuple-element.66.refs_7_) | copy-start | bytes 6635524
  55.9 11.3 %collective-permute-start.10 = (bf16[3,3,32,512]{3,2,0,1:T(8,128)(2,1)S(1)}, bf16[3,3,32,512]{3,2,0,1:T(8,128)(2,1)S(1)}, u32[]{:S(2)}, u32[]{:S(2)}) collective-permute-start(bf16[3,3,32,512]{3,2,0,1:T(8,128)(2,1)S(1)} %pad_maximum_fusion.2), channel_id=1, source_target_pairs={{112,0},{0,16},{16,32},{32,48},{48,64},{64,80},{80,96},{96,112},{1... | collective-permute-start | bytes 884744 | tf_op jit(solution)/shard_map/ppermute | solution.py:517
  56.5 10.8 %collective-permute-start.11 = (bf16[3,3,32,512]{3,2,0,1:T(8,128)(2,1)S(1)}, bf16[3,3,32,512]{3,2,0,1:T(8,128)(2,1)S(1)}, u32[]{:S(2)}, u32[]{:S(2)}) collective-permute-start(bf16[3,3,32,512]{3,2,0,1:T(8,128)(2,1)S(1)} %pad_maximum_fusion.3), channel_id=1, source_target_pairs={{16,0},{32,16},{48,32},{64,48},{80,64},{96,80},{112,96},{0,112},{1... | collective-permute-start | bytes 884744 | tf_op jit(solution)/shard_map/ppermute | solution.py:517
  62.0 5.3 %copy-start.6 = (f32[64]{0:T(128)S(1)}, f32[64]{0:T(128)}, u32[]{:S(2)}) copy-start(f32[64]{0:T(128)} %param.24) | copy-start | bytes 772
  62.0 5.3 %copy-start.7 = (bf16[2,384,288]{2,1,0:T(8,128)(2,1)S(1)}, bf16[2,384,288]{2,1,0:T(8,128)(2,1)}, u32[]{:S(2)}) copy-start(bf16[2,384,288]{2,1,0:T(8,128)(2,1)} %get-tuple-element.68.refs_13_) | copy-start | bytes 1327108

commit v3 on v2

--- a/solution.py
+++ b/solution.py
@@ -108,17 +108,24 @@
         dist2 = d * d if k == 0 else dist2 + d * d
     live = row[3:4]
     itself = flag(row[7:8] == number.astype(f32))
-    dist = jnp.sqrt(dist2 + itself + (1.0 - live))
-    smooth = jnp.where(dist < cutoff, 0.5 * (jnp.cos(math.pi * dist / cutoff) + 1.0), 0.0)
+    dist2 = dist2 + itself + (1.0 - live)
+    inverse = lax.rsqrt(dist2)
+    dist = dist2 * inverse
+    phase = 0.5 - dist * (1.0 / cutoff)
+    square = phase * phase
+    series = 0.0
+    for k in range(6, -1, -1):
+        series = series * square + 0.5 * (-1.0) ** k * math.pi ** (2 * k + 1) / math.factorial(2 * k + 1)
+    smooth = jnp.where(dist < cutoff, 0.5 + phase * series, 0.0)
     weight = smooth * live * (1.0 - itself)
-    scaled = weight / dist
+    scaled = weight * inverse
     pairs_ref[8, at, :] = weight
     for k in range(3):
         pairs_ref[9 + k, at, :] = scaled * disp[k]
-    sharp = 0.5 * (7.0 / cutoff) ** 2
+    sharp = 0.5 * (7.0 / cutoff) ** 2 / math.log(2.0)
     for k in range(8):
         away = dist - k * (cutoff / 7.0)
-        pairs_ref[k, at, :] = jnp.exp(-sharp * (away * away))
+        pairs_ref[k, at, :] = jnp.exp2(away * away * -sharp)
 
 
 def features(layer, x, part, weights, feats):
@@ -135,7 +142,7 @@
         feats[1 + k][part, :] = jnp.concatenate([gc, gg * vec[k]], axis=1)
 
 
-def messages(layer, count, place, window, weights, pairs_ref, feats, edges, delta):
+def messages(layer, count, place, window, weights, pairs_ref, feats, edges, delta, fill=None):
     rin_ref, rout_ref = weights[:2]
     width = window.stop - window.start
     even, odd = edges[:4], edges[4:]
@@ -188,9 +195,13 @@
         for g in range(4):
             delta[rows_at(b), g * chan : (g + 1) * chan] += sums[g]
 
+    if fill is not None and layer == 0:
+        fill()
     y, w = hidden_of(0)
     for r in range(block):
         edge(r, y, w, even)
+    if fill is not None and layer > 0:
+        fill()
 
     def two_steps(t, carry):
         step(2 * t, even, odd)
@@ -204,56 +215,61 @@
         step(count - 1, even, None)
 
 
-def ready_kernel(layer, *refs):
-    counts_ref, low, middle, high = refs[:4]
-    weights = (None, None, *refs[4:7])
-    refs = refs[7:]
+def packed_features(layer, ys, order, part, weights, feats):
+    third = own_atoms // 3
+    x = None
+    for n, ref in enumerate(ys):
+        atoms = ref[...].reshape(third, -1)[:, : 4 * chan]
+        y = dot(order[part, n * third : (n + 1) * third], atoms)
+        x = y if n == 0 else x + y
+    features(layer, x.astype(bf16), part, weights, feats)
+
+
+def geometry_kernel(counts_ref, low, middle, high, pairs, order, more):
+    geo = [
+        ref[...].reshape(own_atoms // 3, -1)[:, 4 * chan :] + own_table(n)
+        for n, ref in enumerate((low, middle, high))
+    ]
+    geo = jnp.concatenate(geo, axis=0)
+    order[...], total = compaction(geo[:, 3:4].astype(f32), own_span)
+    row = rows_of(dot(order[...], geo).astype(bf16))
+    more[0] = jnp.where(jnp.sum(total) > own_main + 0.5, 1, 0)
+    first = counts_ref[0]
+    mine = columns_of(jnp.concatenate([middle[q, 1][:, 4 * chan :] for q in range(2)], axis=0))
+    place = lax.broadcasted_iota(jnp.int32, (2 * slots, 1), 0)
+    moved = pltpu.roll(mine, lax.rem(first + slots, 2 * slots), 0)
+    mine = jnp.where(place < first, mine, moved)
+    number = jnp.where(place < first, place + 1, place - first + (slots + 1))
+    shift = jnp.where(place < first, 0.0, -cutoff)
+    geometry(row, mine, number, shift, pairs, slice(0, 2 * slots))
+
+
+def feature_kernel(layer, low, middle, high, ain_ref, abias_ref, aout_ref, order, *feats):
+    weights = (None, None, ain_ref, abias_ref, aout_ref)
+    packed_features(layer, (low, middle, high), order, slice(0, own_span), weights, feats)
+
+
+def own_kernel(layer, *refs):
+    counts_ref, weights, refs = refs[0], refs[1:6], refs[6:]
     if layer == 0:
-        feats, refs = refs[:4], refs[4:]
-        pairs, order_out, more, order, done = refs
+        ys, order, refs = refs[:3], refs[3], refs[4:]
+        pairs, more, delta, pairs_out, order_out = refs[:5]
+        feats, edges, done = refs[5:9], refs[9:17], refs[17]
+        keep = [
+            pltpu.make_async_copy(pairs, pairs_out, done.at[0]),
+            pltpu.make_async_copy(order, order_out, done.at[1]),
+        ]
+        for copy in keep:
+            copy.start()
     else:
-        order, feats = refs[0], refs[1:]
-    parts = [ref[...].reshape(own_atoms // 3, -1) for ref in (low, middle, high)]
-    third = own_atoms // 3
-    if layer == 0:
-        geo = [p[:, 4 * chan :] + own_table(n) for n, p in enumerate(parts)]
-        geo = jnp.concatenate(geo, axis=0)
-        order[...], total = compaction(geo[:, 3:4].astype(f32), own_span)
-        keep = pltpu.make_async_copy(order, order_out, done.at[0])
-        keep.start()
-    x = None
-    for n in range(3):
-        y = dot(order[:, n * third : (n + 1) * third], parts[n][:, : 4 * chan])
-        x = y if n == 0 else x + y
-    features(layer, x.astype(bf16), slice(0, own_span), weights, feats)
-    if layer == 0:
-        row = rows_of(dot(order[...], geo).astype(bf16))
-        more[0] = jnp.where(jnp.sum(total) > own_main + 0.5, 1, 0)
-        first = counts_ref[0]
-        mine = columns_of(
-            jnp.concatenate([middle[q, 1][:, 4 * chan :] for q in range(2)], axis=0)
-        )
-        place = lax.broadcasted_iota(jnp.int32, (2 * slots, 1), 0)
-        moved = pltpu.roll(mine, lax.rem(first + slots, 2 * slots), 0)
-        mine = jnp.where(place < first, mine, moved)
-        number = jnp.where(place < first, place + 1, place - first + (slots + 1))
-        shift = jnp.where(place < first, 0.0, -cutoff)
-        geometry(row, mine, number, shift, pairs, slice(0, 2 * slots))
-        keep.wait()
-
-
-def own_kernel(layer, *refs):
-    counts_ref, weights, feats, pairs, more, delta = refs[0], refs[1:3], refs[3:7], *refs[7:10]
-    refs = refs[10:]
-    if layer == 0:
-        pairs_out, done, refs = refs[0], refs[-1], refs[1:-1]
-        keep = pltpu.make_async_copy(pairs, pairs_out, done.at[0])
-        keep.start()
-    edges = refs
+        feats, (pairs, more, delta), edges = refs[:4], refs[4:7], refs[7:]
     count = (counts_ref[0] + counts_ref[1] + block - 1) // block
     delta[...] = jnp.zeros_like(delta)
 
     def add(part):
+        def fill():
+            packed_features(layer, ys, order, part, weights, feats)
+
         messages(
             layer,
             count,
@@ -264,6 +280,7 @@
             feats,
             edges,
             delta,
+            fill if layer == 0 else None,
         )
 
     add(slice(0, own_main))
@@ -273,7 +290,8 @@
         add(slice(own_main, own_span))
 
     if layer == 0:
-        keep.wait()
+        for copy in keep:
+            copy.wait()
 
 
 def side_kernel(layer, last, *refs):
@@ -314,16 +332,17 @@
     above = (counts_ref[1] + block - 1) // block
 
     def add(part):
-        for q in range(2):
-            x = dot(order[q, part, :], atoms[q][:, : 4 * chan])
-            rows = slice(q * side_span + part.start, q * side_span + part.stop)
-            features(layer, x.astype(bf16), rows, weights, feats)
+        def fill():
+            for q in range(2):
+                x = dot(order[q, part, :], atoms[q][:, : 4 * chan])
+                rows = slice(q * side_span + part.start, q * side_span + part.stop)
+                features(layer, x.astype(bf16), rows, weights, feats)
 
         def place(b):
             q = jnp.where(b >= below, 1, 0)
             return b * block + q * (slots - below * block), q * side_span + part.start
 
-        messages(layer, below + above, place, part, weights, pairs, feats, edges, delta)
+        messages(layer, below + above, place, part, weights, pairs, feats, edges, delta, fill)
 
     add(main)
 
@@ -392,33 +411,37 @@
     return [jax.ShapeDtypeStruct((rows, width * chan), bf16) for width in (4, 2, 2, 2)]
 
 
-def ready_call(layer, counts, ys, weights, order):
-    operands = [counts, *ys, *weights[2:]] + ([] if layer == 0 else [order])
-    shapes, outs, held = feature_shapes(own_span), [vmem] * 4, []
-    if layer == 0:
-        pairs, order, more = kept_shapes(own_span, (own_span, own_atoms))
-        shapes += [pairs, pltpu.HBM(order.shape, order.dtype), more]
-        outs += [vmem, hbm, smem]
-        held = [pltpu.VMEM(order.shape, order.dtype), pltpu.SemaphoreType.DMA((1,))]
+def geometry_call(counts, ys):
     return pl.pallas_call(
-        functools.partial(ready_kernel, layer),
-        out_shape=shapes,
-        in_specs=[smem] + [vmem] * (len(operands) - 1),
-        out_specs=outs,
-        scratch_shapes=held,
+        geometry_kernel,
+        out_shape=kept_shapes(own_span, (own_span, own_atoms)),
+        in_specs=[smem] + [vmem] * 3,
+        out_specs=kept_specs,
         compiler_params=params,
-        name=f"ready_part_{layer}",
-    )(*operands)
-
-
-def own_call(layer, counts, weights, feats, pairs, more):
-    operands = [counts, *weights[:2], *feats, pairs, more]
+        name="geometry_part",
+    )(counts, *ys)
+
+
+def feature_call(layer, ys, weights, order):
+    return pl.pallas_call(
+        functools.partial(feature_kernel, layer),
+        out_shape=feature_shapes(own_span),
+        in_specs=[vmem] * 7,
+        out_specs=[vmem] * 4,
+        compiler_params=params,
+        name=f"feature_part_{layer}",
+    )(*ys, *weights[2:], order)
+
+
+def own_call(layer, counts, weights, given, pairs, more):
+    operands = [counts, *weights, *given, pairs, more]
     shapes, outs = [delta_shape], [vmem]
     held = [pltpu.VMEM((block * hidden, own_main), bf16)] * 8
     if layer == 0:
-        shapes.append(pltpu.HBM(pairs.shape, pairs.dtype))
-        outs.append(hbm)
-        held.append(pltpu.SemaphoreType.DMA((1,)))
+        shapes += [pltpu.HBM(x.shape, x.dtype) for x in (pairs, given[3])]
+        outs += [hbm, hbm]
+        held = [pltpu.VMEM(f.shape, f.dtype) for f in feature_shapes(own_span)] + held
+        held.append(pltpu.SemaphoreType.DMA((2,)))
     return pl.pallas_call(
         functools.partial(own_kernel, layer),
         out_shape=shapes,
@@ -561,16 +584,18 @@
             rin = radial_rows(radial_in, radial_bias)
             weights = [rin, radial_out, atom_in, atom_bias, atom_out]
         ys = [shifted(y, "gy", -1), y, shifted(y, "gy", 1)]
+        low, high = jnp.stack([v[1] for v in ys]), jnp.stack([v[0] for v in ys])
         if layer == 0:
-            *feats, pairs, order, more = ready_call(layer, counts, ys, weights, None)
+            pairs, order, more = geometry_call(counts, ys)
+            low, high, pairs = lax.optimization_barrier((low, high, pairs))
+            given = [*ys, order]
         else:
-            feats = ready_call(layer, counts, ys, weights, order)
-        low, high = jnp.stack([v[1] for v in ys]), jnp.stack([v[0] for v in ys])
-        low, high, feats = lax.optimization_barrier((low, high, feats))
+            given = feature_call(layer, ys, weights, order)
+            low, high, given = lax.optimization_barrier((low, high, given))
         low, high = shifted(low, "gx", -1), shifted(high, "gx", 1)
-        delta, *kept = own_call(layer, counts, weights, feats, pairs, more)
+        delta, *kept = own_call(layer, counts, weights, given, pairs, more)
         if layer == 0:
-            pairs = kept[0]
+            pairs, order = kept
         readout = [readout_in, readout_out[None, :]]
         state, *kept = side_call(
             layer, last, counts, low, high, own, delta, weights, readout, side_kept

time: 94.1 us -> 94.5 us (level)
  Pallas kernels: 18.4 us -> 16.4 us
  waiting for transfers between devices: 22.4 us -> 23.8 us
    pallas_call x2, Pallas kernels: 5.46 us -> 3.28 us  [the longest x1 2.29 us: geometry_call(): pl.pallas_call(geometry_kernel, out_shape=kept_shapes(own_span, (own_span...]
    ppermute x12, waiting for transfers between devices: 22.4 us -> 23.8 us  [shifted(): lax.ppermute(value, axis, [((i + step) % count, i) for i in range(count)])]
  transfers between devices with their start and end apart: 12 -> 12, of which waited for: 8 -> 9; matrix products, arithmetic and copies ran while one was open for 4% -> 4% of each run, Pallas kernels for 4% -> 5%
where the time goes in v3:
time: 94.5 us; the launch traced here: 94.6 us
  starting transfers between devices  26.1 us (28%)
  waiting for transfers between devices  23.8 us (25%)
  blocking collectives  23 us (24%)
  Pallas kernels  16.4 us (17%)
  local copies, waits for them, and re-layouts  2.65 us (3%)
  other arithmetic  1.8 us (2%)
    ppermute x12, starting transfers between devices, shifted(): lax.ppermute(value, axis, [((i + step) % count, i) for i in range(count)])  26.1 us
    ppermute x12, waiting for transfers between devices, shifted(): lax.ppermute(value, axis, [((i + step) % count, i) for i in range(count)])  23.8 us
    all_to_all x1, blocking collectives, on_device(): every = lax.all_to_all(energy, ('gx', 'gy', 'gz'), 0, 0, tiled=True)  23 us
    pallas_call x2, Pallas kernels, side_call(): pl.pallas_call(functools.partial(side_kernel, layer, last), out_shape=sha...  7.52 us
    pallas_call x2, Pallas kernels, own_call(): pl.pallas_call(functools.partial(own_kernel, layer), out_shape=shapes, in...  4.49 us
    pallas_call x1, Pallas kernels, geometry_call(): pl.pallas_call(geometry_kernel, out_shape=kept_shapes(own_span, (own_span...  2.29 us
    mul x6, local copies, waits for them, and re-layouts, radial_rows(): radial_in.transpose(0, 2, 1)[:, None, :, :, None] * eye[:, None, None, :]  2.13 us
  transfers between devices with their start and end apart: 12, of which 9 were waited for; matrix products, arithmetic and copies ran while one was open for 4% of the time, Pallas kernels for 5%

profile of v3, /device:TPU:1, one launch (start us, length us, event | category | flops | bytes accessed | tf_op | source)
XLA Modules:
  0.0 94.6 jit_solution(3979491214665065631)
XLA Ops:
  0.6 1.1 %pack.1.refs_3_ = bf16[2,32,640]{2,1,0:T(8,128)(2,1)S(1)} custom-call(s32[2]{0:T(128)} %bitcast.48, f32[2,3,1,32]{3,2,1,0:T(1,128)} %bitcast.63, bf16[2,32,128]{2,1,0:T(8,128)(2,1)} %bitcast.61, bf16[2,3,32,128]{3,2,1,0:T(8,128)(2,1)} %bitcast.60), custom_call_target="tpu_custom_call" | custom-call | tf_op jit(solution)/shard_map/pack/pallas_call | solution.py:523
  1.7 2.1 %collective-permute-start = (bf16[2,32,640]{2,1,0:T(8,128)(2,1)S(1)}, bf16[2,32,640]{2,1,0:T(8,128)(2,1)S(1)}, u32[]{:S(2)}, u32[]{:S(2)}) collective-permute-start(bf16[2,32,640]{2,1,0:T(8,128)(2,1)S(1)} %pack.1.refs_3_), channel_id=1, source_target_pairs={{3,0},{0,1},{1,2},{2,3},{7,4},{4,5},{5,6},{6,7},{11,8},{8,9},{9,10... | collective-permute-start | bytes 245768 | tf_op jit(solution)/shard_map/ppermute | solution.py:540
  3.9 1.3 %collective-permute-start.1 = (bf16[2,32,640]{2,1,0:T(8,128)(2,1)S(1)}, bf16[2,32,640]{2,1,0:T(8,128)(2,1)S(1)}, u32[]{:S(2)}, u32[]{:S(2)}) collective-permute-start(bf16[2,32,640]{2,1,0:T(8,128)(2,1)S(1)} %pack.1.refs_3_), channel_id=1, source_target_pairs={{1,0},{2,1},{3,2},{0,3},{5,4},{6,5},{7,6},{4,7},{9,8},{10,9},{11,1... | collective-permute-start | bytes 245768 | tf_op jit(solution)/shard_map/ppermute | solution.py:540
  5.2 0.8 mul.31
  6.0 0.1 mul.32
  6.1 0.1 copy.37
  6.2 0.7 collective-permute-done
  7.0 0.2 collective-permute-done.1
  7.2 5.7 %collective-permute-start.2 = (bf16[2,3,32,640]{3,2,1,0:T(8,128)(2,1)S(1)}, bf16[2,3,32,640]{3,2,1,0:T(8,128)(2,1)S(1)}, u32[]{:S(2)}, u32[]{:S(2)}) collective-permute-start(bf16[2,3,32,640]{3,2,1,0:T(8,128)(2,1)S(1)} %pad_maximum_fusion.4.middle.refs_7_), channel_id=1, source_target_pairs={{12,0},{0,4},{4,8},{8,12},{13,1},{1,5},{5,9},{9,13},{14,2},{2,6},{... | collective-permute-start | bytes 737288 | tf_op jit(solution)/shard_map/ppermute | solution.py:540
  12.8 0.0 collective-permute-start.3
  12.8 0.7 fusion.6
  13.5 0.1 copy.39
  13.7 0.7 mul.29
  14.4 0.2 mul.30
  14.6 0.2 copy.38
  14.8 0.0 copy-start.3
  14.9 0.0 copy-start.1
  14.9 0.0 copy-start.2
  14.9 0.0 copy-start.4
  14.9 0.0 copy-start.5
  15.0 0.2 fusion.2.refs_1_.refs_5_
  15.1 3.5 %collective-permute-done.2.low.refs_6_ = bf16[2,3,32,640]{3,2,1,0:T(8,128)(2,1)S(1)} collective-permute-done((bf16[2,3,32,640]{3,2,1,0:T(8,128)(2,1)S(1)}, bf16[2,3,32,640]{3,2,1,0:T(8,128)(2,1)S(1)}, u32[]{:S(2)}, u32[]{:S(2)}) %collective-permute-start.2) | collective-permute-done | bytes 245792 | tf_op jit(solution)/shard_map/ppermute | solution.py:540
  18.6 1.3 %collective-permute-done.3.high.refs_8_ = bf16[2,3,32,640]{3,2,1,0:T(8,128)(2,1)S(1)} collective-permute-done((bf16[2,3,32,640]{3,2,1,0:T(8,128)(2,1)S(1)}, bf16[2,3,32,640]{3,2,1,0:T(8,128)(2,1)S(1)}, u32[]{:S(2)}, u32[]{:S(2)}) %collective-permute-start.3) | collective-permute-done | bytes 245792 | tf_op jit(solution)/shard_map/ppermute | solution.py:540
  20.0 0.1 pad_maximum_fusion
  20.1 2.3 %geometry_part.1 = (f32[12,72,640]{2,1,0:T(8,128)S(1)}, bf16[640,576]{1,0:T(8,128)(2,1)S(1)}, s32[2]{0:T(128)S(1)}) custom-call(s32[2]{0:T(128)S(1)} %bitcast.49, bf16[2,3,32,640]{3,2,1,0:T(8,128)(2,1)S(1)} %collective-permute-done.2.low.refs_6_, bf16[2,3,32,640]{3,2,1,0:T(8,128)(2,1)S(1)} %pad_maximum_fusion.4.middle.refs_7_, ...), custom_call_target="tpu_custom_call" | custom-call | tf_op jit(solution)/shard_map/geometry_part/pallas_call | solution.py:415
  22.4 1.4 %collective-permute-start.4 = (bf16[3,3,32,640]{3,2,1,0:T(8,128)(2,1)S(1)}, bf16[3,3,32,640]{3,2,1,0:T(8,128)(2,1)S(1)}, u32[]{:S(2)}, u32[]{:S(2)}) collective-permute-start(bf16[3,3,32,640]{3,2,1,0:T(8,128)(2,1)S(1)} %get-tuple-element.34), channel_id=1, source_target_pairs={{112,0},{0,16},{16,32},{32,48},{48,64},{64,80},{80,96},{96,112},{1... | collective-permute-start | bytes 1105928 | tf_op jit(solution)/shard_map/ppermute | solution.py:540
  23.8 2.3 %collective-permute-start.5 = (bf16[3,3,32,640]{3,2,1,0:T(8,128)(2,1)S(1)}, bf16[3,3,32,640]{3,2,1,0:T(8,128)(2,1)S(1)}, u32[]{:S(2)}, u32[]{:S(2)}) collective-permute-start(bf16[3,3,32,640]{3,2,1,0:T(8,128)(2,1)S(1)} %get-tuple-element.35), channel_id=1, source_target_pairs={{16,0},{32,16},{48,32},{64,48},{80,64},{96,80},{112,96},{0,112},{1... | collective-permute-start | bytes 1105928 | tf_op jit(solution)/shard_map/ppermute | solution.py:540
  26.1 2.6 %own_part_0.1 = (f32[72,512]{1,0:T(8,128)S(1)}, f32[12,72,640]{2,1,0:T(8,128)}, bf16[640,576]{1,0:T(8,128)(2,1)}) custom-call(s32[2]{0:T(128)S(1)} %bitcast.50, bf16[2,512,80]{2,1,0:T(8,128)(2,1)S(1)} %fusion.2.refs_1_.refs_5_, bf16[2,64,512]{2,1,0:T(8,128)(2,1)S(1)} %copy-done.5, bf16[2,128,128]{2,1,0:T(8,128)(2,1)S(1)} %copy-done.2, ...), custom_call_target="tpu_custom_call" | custom-call | flops 6039797760 | bytes 4000000 | tf_op jit(solution)/shard_map/own_part_0/pallas_call | solution.py:445
  28.7 5.6 %collective-permute-done.4.refs_1_ = bf16[3,3,32,640]{3,2,1,0:T(8,128)(2,1)S(1)} collective-permute-done((bf16[3,3,32,640]{3,2,1,0:T(8,128)(2,1)S(1)}, bf16[3,3,32,640]{3,2,1,0:T(8,128)(2,1)S(1)}, u32[]{:S(2)}, u32[]{:S(2)}) %collective-permute-start.4) | collective-permute-done | bytes 368672 | tf_op jit(solution)/shard_map/ppermute | solution.py:540
  34.3 0.0 collective-permute-done.5.refs_2_
  34.3 4.2 %side_part_0.1 = (bf16[64,512]{1,0:T(8,128)(2,1)S(1)}, f32[12,72,384]{2,1,0:T(8,128)S(1)}, bf16[2,384,288]{2,1,0:T(8,128)(2,1)}, s32[2]{0:T(128)S(1)}) custom-call(s32[2]{0:T(128)S(1)} %bitcast.51, bf16[3,3,32,640]{3,2,1,0:T(8,128)(2,1)S(1)} %collective-permute-done.4.refs_1_, bf16[3,3,32,640]{3,2,1,0:T(8,128)(2,1)S(1)} %collective-permute-done.5.refs_2_, ...), custom_call_target="tpu_custom_call" | custom-call | flops 3019898880 | bytes 4000000 | tf_op jit(solution)/shard_map/side_part_0/pallas_call | solution.py:479
  38.5 1.3 %collective-permute-start.6 = (bf16[2,32,512]{2,1,0:T(8,128)(2,1)S(1)}, bf16[2,32,512]{2,1,0:T(8,128)(2,1)S(1)}, u32[]{:S(2)}, u32[]{:S(2)}) collective-permute-start(bf16[2,32,512]{2,1,0:T(8,128)(2,1)S(1)} %bitcast.44), channel_id=1, source_target_pairs={{3,0},{0,1},{1,2},{2,3},{7,4},{4,5},{5,6},{6,7},{11,8},{8,9},{9,10... | collective-permute-start | bytes 196616 | tf_op jit(solution)/shard_map/ppermute | solution.py:540
  39.8 1.5 %collective-permute-start.7 = (bf16[2,32,512]{2,1,0:T(8,128)(2,1)S(1)}, bf16[2,32,512]{2,1,0:T(8,128)(2,1)S(1)}, u32[]{:S(2)}, u32[]{:S(2)}) collective-permute-start(bf16[2,32,512]{2,1,0:T(8,128)(2,1)S(1)} %bitcast.45), channel_id=1, source_target_pairs={{1,0},{2,1},{3,2},{0,3},{5,4},{6,5},{7,6},{4,7},{9,8},{10,9},{11,1... | collective-permute-start | bytes 196616 | tf_op jit(solution)/shard_map/ppermute | solution.py:540
  41.2 0.1 copy.45.refs_10_
  41.4 2.0 %collective-permute-done.6 = bf16[2,32,512]{2,1,0:T(8,128)(2,1)S(1)} collective-permute-done((bf16[2,32,512]{2,1,0:T(8,128)(2,1)S(1)}, bf16[2,32,512]{2,1,0:T(8,128)(2,1)S(1)}, u32[]{:S(2)}, u32[]{:S(2)}) %collective-permute-start.6) | collective-permute-done | bytes 65568 | tf_op jit(solution)/shard_map/ppermute | solution.py:540
  43.3 0.0 collective-permute-done.7
  43.4 4.5 %collective-permute-start.8 = (bf16[2,3,32,512]{3,2,0,1:T(8,128)(2,1)S(1)}, bf16[2,3,32,512]{3,2,0,1:T(8,128)(2,1)S(1)}, u32[]{:S(2)}, u32[]{:S(2)}) collective-permute-start(bf16[2,3,32,512]{3,2,0,1:T(8,128)(2,1)S(1)} %pad_maximum_fusion.5), channel_id=1, source_target_pairs={{12,0},{0,4},{4,8},{8,12},{13,1},{1,5},{5,9},{9,13},{14,2},{2,6},{... | collective-permute-start | bytes 589832 | tf_op jit(solution)/shard_map/ppermute | solution.py:540
  47.9 0.0 collective-permute-start.9
  47.9 4.5 %collective-permute-done.8 = bf16[2,3,32,512]{3,2,0,1:T(8,128)(2,1)S(1)} collective-permute-done((bf16[2,3,32,512]{3,2,0,1:T(8,128)(2,1)S(1)}, bf16[2,3,32,512]{3,2,0,1:T(8,128)(2,1)S(1)}, u32[]{:S(2)}, u32[]{:S(2)}) %collective-permute-start.8) | collective-permute-done | bytes 196640 | tf_op jit(solution)/shard_map/ppermute | solution.py:540
  52.5 2.0 %collective-permute-done.9 = bf16[2,3,32,512]{3,2,0,1:T(8,128)(2,1)S(1)} collective-permute-done((bf16[2,3,32,512]{3,2,0,1:T(8,128)(2,1)S(1)}, bf16[2,3,32,512]{3,2,0,1:T(8,128)(2,1)S(1)}, u32[]{:S(2)}, u32[]{:S(2)}) %collective-permute-start.9) | collective-permute-done | bytes 196640 | tf_op jit(solution)/shard_map/ppermute | solution.py:540
  54.6 1.0 %feature_part_1.1 = (bf16[640,512]{1,0:T(8,128)(2,1)S(1)}, bf16[640,256]{1,0:T(8,128)(2,1)S(1)}, bf16[640,256]{1,0:T(8,128)(2,1)S(1)}, bf16[640,256]{1,0:T(8,128)(2,1)S(1)}) custom-call(bf16[2,3,32,512]{3,2,1,0:T(8,128)(2,1)S(1)} %copy.40.low, bf16[2,3,32,512]{3,2,1,0:T(8,128)(2,1)S(1)} %copy.41.middle, bf16[2,3,32,512]{3,2,1,0:T(8,128)(2,1)S(1)} %copy.42.high, ...), custom_call_target="tpu_custom_call" | custom-call | tf_op jit(solution)/shard_map/feature_part_1/pallas_call | solution.py:426
  55.6 0.5 collective-permute-start.10
  56.1 5.5 %collective-permute-start.11 = (bf16[3,3,32,512]{3,2,0,1:T(8,128)(2,1)S(1)}, bf16[3,3,32,512]{3,2,0,1:T(8,128)(2,1)S(1)}, u32[]{:S(2)}, u32[]{:S(2)}) collective-permute-start(bf16[3,3,32,512]{3,2,0,1:T(8,128)(2,1)S(1)} %pad_maximum_fusion.3), channel_id=1, source_target_pairs={{16,0},{32,16},{48,32},{64,48},{80,64},{96,80},{112,96},{0,112},{1... | collective-permute-start | bytes 884744 | tf_op jit(solution)/shard_map/ppermute | solution.py:540
  61.7 1.9 %own_part_1.1.refs_4_ = f32[72,512]{1,0:T(8,128)S(1)} custom-call(s32[2]{0:T(128)S(1)} %bitcast.52, bf16[2,512,80]{2,1,0:T(8,128)(2,1)S(1)} %fusion.2.refs_1_.refs_5_, bf16[2,64,512]{2,1,0:T(8,128)(2,1)S(1)} %copy-done.5, bf16[2,128,128]{2,1,0:T(8,128)(2,1)S(1)} %copy-done.2, f32[2,128]{1,0:T(2,128)S(1)} %copy-done.4, bf16[2,128,512]{2,1,0:T(8,128)(2,1)S(1)} %copy-done.1, ...), custom_call_target="tpu_custom_call" | custom-call | flops 6039797760 | bytes 4000000 | tf_op jit(solution)/shard_map/own_part_1/pallas_call | solution.py:445
  63.6 4.0 %collective-permute-done.10 = bf16[3,3,32,512]{3,2,0,1:T(8,128)(2,1)S(1)} collective-permute-done((bf16[3,3,32,512]{3,2,0,1:T(8,128)(2,1)S(1)}, bf16[3,3,32,512]{3,2,0,1:T(8,128)(2,1)S(1)}, u32[]{:S(2)}, u32[]{:S(2)}) %collective-permute-start.10) | collective-permute-done | bytes 294944 | tf_op jit(solution)/shard_map/ppermute | solution.py:540
  67.6 3.3 %side_part_1.1 = (bf16[2,32,128]{2,1,0:T(8,128)(2,1)}, bf16[2,3,32,128]{3,2,1,0:T(8,128)(2,1)}, f32[128,128]{1,0:T(8,128)S(1)}) custom-call(s32[2]{0:T(128)S(1)} %bitcast.53, bf16[3,3,32,512]{3,2,1,0:T(8,128)(2,1)S(1)} %copy.43.refs_1_, bf16[3,3,32,512]{3,2,1,0:T(8,128)(2,1)S(1)} %copy.44.refs_2_, bf16[2,32,512]{2,1,0:T(8,128)(2,1)S(1)} %bitcast.47, ...), custom_call_target="tpu_custom_call" | custom-call | flops 3019898880 | bytes 4000000 | tf_op jit(solution)/shard_map/side_part_1/pallas_call | solution.py:479
  71.0 23.0 %all_to_all.9 = f32[128,1,128]{2,1,0:T(1,128)S(1)} all-to-all(f32[128,1,128]{2,1,0:T(1,128)S(1)} %bitcast.43), channel_id=1, replica_groups=mesh['gx'=8,'gy'=4,'gz'=4] {'gx','gy','gz'}, dimensions={0} | all-to-all | bytes 131072 | tf_op jit(solution)/shard_map/all_to_all | solution.py:610
  93.9 0.7 reduce_sum.9
  (34 shorter events, 0.4 us)
Async XLA Ops:
  1.7 5.2 %collective-permute-start = (bf16[2,32,640]{2,1,0:T(8,128)(2,1)S(1)}, bf16[2,32,640]{2,1,0:T(8,128)(2,1)S(1)}, u32[]{:S(2)}, u32[]{:S(2)}) collective-permute-start(bf16[2,32,640]{2,1,0:T(8,128)(2,1)S(1)} %pack.1.refs_3_), channel_id=1, source_target_pairs={{3,0},{0,1},{1,2},{2,3},{7,4},{4,5},{5,6},{6,7},{11,8},{8,9},{9,10... | collective-permute-start | bytes 245768 | tf_op jit(solution)/shard_map/ppermute | solution.py:540
  3.9 3.3 %collective-permute-start.1 = (bf16[2,32,640]{2,1,0:T(8,128)(2,1)S(1)}, bf16[2,32,640]{2,1,0:T(8,128)(2,1)S(1)}, u32[]{:S(2)}, u32[]{:S(2)}) collective-permute-start(bf16[2,32,640]{2,1,0:T(8,128)(2,1)S(1)} %pack.1.refs_3_), channel_id=1, source_target_pairs={{1,0},{2,1},{3,2},{0,3},{5,4},{6,5},{7,6},{4,7},{9,8},{10,9},{11,1... | collective-permute-start | bytes 245768 | tf_op jit(solution)/shard_map/ppermute | solution.py:540
  7.2 11.4 %collective-permute-start.2 = (bf16[2,3,32,640]{3,2,1,0:T(8,128)(2,1)S(1)}, bf16[2,3,32,640]{3,2,1,0:T(8,128)(2,1)S(1)}, u32[]{:S(2)}, u32[]{:S(2)}) collective-permute-start(bf16[2,3,32,640]{3,2,1,0:T(8,128)(2,1)S(1)} %pad_maximum_fusion.4.middle.refs_7_), channel_id=1, source_target_pairs={{12,0},{0,4},{4,8},{8,12},{13,1},{1,5},{5,9},{9,13},{14,2},{2,6},{... | collective-permute-start | bytes 737288 | tf_op jit(solution)/shard_map/ppermute | solution.py:540
  12.8 7.1 %collective-permute-start.3 = (bf16[2,3,32,640]{3,2,1,0:T(8,128)(2,1)S(1)}, bf16[2,3,32,640]{3,2,1,0:T(8,128)(2,1)S(1)}, u32[]{:S(2)}, u32[]{:S(2)}) collective-permute-start(bf16[2,3,32,640]{3,2,1,0:T(8,128)(2,1)S(1)} %pad_maximum_fusion.4.middle.refs_7_), channel_id=1, source_target_pairs={{4,0},{8,4},{12,8},{0,12},{5,1},{9,5},{13,9},{1,13},{6,2},{10,6},{... | collective-permute-start | bytes 737288 | tf_op jit(solution)/shard_map/ppermute | solution.py:540
  14.8 5.3 %copy-start.3 = (s32[2,1,1]{0,2,1:T(1,128)S(1)}, s32[2,1,1]{0,2,1:T(1,128)}, u32[]{:S(2)}) copy-start(s32[2,1,1]{0,2,1:T(1,128)} %param.14) | copy-start | bytes 28
  14.9 11.2 %copy-start.1 = (bf16[2,128,512]{2,1,0:T(8,128)(2,1)S(1)}, bf16[2,128,512]{2,1,0:T(8,128)(2,1)}, u32[]{:S(2)}) copy-start(bf16[2,128,512]{2,1,0:T(8,128)(2,1)} %refs_9_.3) | copy-start | bytes 786436
  14.9 11.2 %copy-start.2 = (bf16[2,128,128]{2,1,0:T(8,128)(2,1)S(1)}, bf16[2,128,128]{2,1,0:T(8,128)(2,1)}, u32[]{:S(2)}) copy-start(bf16[2,128,128]{2,1,0:T(8,128)(2,1)} %refs_7_.3) | copy-start | bytes 196612
  14.9 11.2 %copy-start.4 = (f32[2,128]{1,0:T(2,128)S(1)}, f32[2,128]{1,0:T(2,128)}, u32[]{:S(2)}) copy-start(f32[2,128]{1,0:T(2,128)} %refs_8_.3) | copy-start | bytes 3076
  14.9 11.2 %copy-start.5 = (bf16[2,64,512]{2,1,0:T(8,128)(2,1)S(1)}, bf16[2,64,512]{2,1,0:T(8,128)(2,1)}, u32[]{:S(2)}) copy-start(bf16[2,64,512]{2,1,0:T(8,128)(2,1)} %refs_6_.3) | copy-start | bytes 393220
  22.4 11.9 %collective-permute-start.4 = (bf16[3,3,32,640]{3,2,1,0:T(8,128)(2,1)S(1)}, bf16[3,3,32,640]{3,2,1,0:T(8,128)(2,1)S(1)}, u32[]{:S(2)}, u32[]{:S(2)}) collective-permute-start(bf16[3,3,32,640]{3,2,1,0:T(8,128)(2,1)S(1)} %get-tuple-element.34), channel_id=1, source_target_pairs={{112,0},{0,16},{16,32},{32,48},{48,64},{64,80},{80,96},{96,112},{1... | collective-permute-start | bytes 1105928 | tf_op jit(solution)/shard_map/ppermute | solution.py:540
  23.8 10.5 %collective-permute-start.5 = (bf16[3,3,32,640]{3,2,1,0:T(8,128)(2,1)S(1)}, bf16[3,3,32,640]{3,2,1,0:T(8,128)(2,1)S(1)}, u32[]{:S(2)}, u32[]{:S(2)}) collective-permute-start(bf16[3,3,32,640]{3,2,1,0:T(8,128)(2,1)S(1)} %get-tuple-element.35), channel_id=1, source_target_pairs={{16,0},{32,16},{48,32},{64,48},{80,64},{96,80},{112,96},{0,112},{1... | collective-permute-start | bytes 1105928 | tf_op jit(solution)/shard_map/ppermute | solution.py:540
  34.3 6.9 %copy-start.9 = (bf16[128,64]{0,1:T(8,128)(2,1)S(1)}, bf16[128,64]{0,1:T(8,128)(2,1)}, u32[]{:S(2)}) copy-start(bf16[128,64]{0,1:T(8,128)(2,1)} %param.23) | copy-start | bytes 49156
  38.5 16.1 %copy-start = (bf16[640,576]{1,0:T(8,128)(2,1)S(1)}, bf16[640,576]{1,0:T(8,128)(2,1)}, u32[]{:S(2)}) copy-start(bf16[640,576]{1,0:T(8,128)(2,1)} %get-tuple-element.43.order) | copy-start | bytes 2211844
  38.5 4.8 %collective-permute-start.6 = (bf16[2,32,512]{2,1,0:T(8,128)(2,1)S(1)}, bf16[2,32,512]{2,1,0:T(8,128)(2,1)S(1)}, u32[]{:S(2)}, u32[]{:S(2)}) collective-permute-start(bf16[2,32,512]{2,1,0:T(8,128)(2,1)S(1)} %bitcast.44), channel_id=1, source_target_pairs={{3,0},{0,1},{1,2},{2,3},{7,4},{4,5},{5,6},{6,7},{11,8},{8,9},{9,10... | collective-permute-start | bytes 196616 | tf_op jit(solution)/shard_map/ppermute | solution.py:540
  39.8 3.6 %collective-permute-start.7 = (bf16[2,32,512]{2,1,0:T(8,128)(2,1)S(1)}, bf16[2,32,512]{2,1,0:T(8,128)(2,1)S(1)}, u32[]{:S(2)}, u32[]{:S(2)}) collective-permute-start(bf16[2,32,512]{2,1,0:T(8,128)(2,1)S(1)} %bitcast.45), channel_id=1, source_target_pairs={{1,0},{2,1},{3,2},{0,3},{5,4},{6,5},{7,6},{4,7},{9,8},{10,9},{11,1... | collective-permute-start | bytes 196616 | tf_op jit(solution)/shard_map/ppermute | solution.py:540
  43.4 9.1 %collective-permute-start.8 = (bf16[2,3,32,512]{3,2,0,1:T(8,128)(2,1)S(1)}, bf16[2,3,32,512]{3,2,0,1:T(8,128)(2,1)S(1)}, u32[]{:S(2)}, u32[]{:S(2)}) collective-permute-start(bf16[2,3,32,512]{3,2,0,1:T(8,128)(2,1)S(1)} %pad_maximum_fusion.5), channel_id=1, source_target_pairs={{12,0},{0,4},{4,8},{8,12},{13,1},{1,5},{5,9},{9,13},{14,2},{2,6},{... | collective-permute-start | bytes 589832 | tf_op jit(solution)/shard_map/ppermute | solution.py:540
  47.9 6.6 %collective-permute-start.9 = (bf16[2,3,32,512]{3,2,0,1:T(8,128)(2,1)S(1)}, bf16[2,3,32,512]{3,2,0,1:T(8,128)(2,1)S(1)}, u32[]{:S(2)}, u32[]{:S(2)}) collective-permute-start(bf16[2,3,32,512]{3,2,0,1:T(8,128)(2,1)S(1)} %pad_maximum_fusion.5), channel_id=1, source_target_pairs={{4,0},{8,4},{12,8},{0,12},{5,1},{9,5},{13,9},{1,13},{6,2},{10,6},{... | collective-permute-start | bytes 589832 | tf_op jit(solution)/shard_map/ppermute | solution.py:540
  47.9 13.7 %copy-start.8 = (f32[12,72,640]{2,1,0:T(8,128)S(1)}, f32[12,72,640]{2,1,0:T(8,128)}, u32[]{:S(2)}) copy-start(f32[12,72,640]{2,1,0:T(8,128)} %get-tuple-element.54.refs_10_) | copy-start | bytes 6635524
  55.6 11.9 %collective-permute-start.10 = (bf16[3,3,32,512]{3,2,0,1:T(8,128)(2,1)S(1)}, bf16[3,3,32,512]{3,2,0,1:T(8,128)(2,1)S(1)}, u32[]{:S(2)}, u32[]{:S(2)}) collective-permute-start(bf16[3,3,32,512]{3,2,0,1:T(8,128)(2,1)S(1)} %pad_maximum_fusion.2), channel_id=1, source_target_pairs={{112,0},{0,16},{16,32},{32,48},{48,64},{64,80},{80,96},{96,112},{1... | collective-permute-start | bytes 884744 | tf_op jit(solution)/shard_map/ppermute | solution.py:540
  56.1 11.4 %collective-permute-start.11 = (bf16[3,3,32,512]{3,2,0,1:T(8,128)(2,1)S(1)}, bf16[3,3,32,512]{3,2,0,1:T(8,128)(2,1)S(1)}, u32[]{:S(2)}, u32[]{:S(2)}) collective-permute-start(bf16[3,3,32,512]{3,2,0,1:T(8,128)(2,1)S(1)} %pad_maximum_fusion.3), channel_id=1, source_target_pairs={{16,0},{32,16},{48,32},{64,48},{80,64},{96,80},{112,96},{0,112},{1... | collective-permute-start | bytes 884744 | tf_op jit(solution)/shard_map/ppermute | solution.py:540
  61.7 6.0 %copy-start.6 = (f32[64]{0:T(128)S(1)}, f32[64]{0:T(128)}, u32[]{:S(2)}) copy-start(f32[64]{0:T(128)} %param.24) | copy-start | bytes 772
  61.7 6.0 %copy-start.7 = (bf16[2,384,288]{2,1,0:T(8,128)(2,1)S(1)}, bf16[2,384,288]{2,1,0:T(8,128)(2,1)}, u32[]{:S(2)}) copy-start(bf16[2,384,288]{2,1,0:T(8,128)(2,1)} %get-tuple-element.56.refs_13_) | copy-start | bytes 1327108

commit v4 on v3

--- a/solution.py
+++ b/solution.py
@@ -295,9 +295,10 @@
 
 
 def side_kernel(layer, last, *refs):
-    counts_ref, low, high, own_ref, before = refs[:5]
-    weights = refs[5:10]
-    refs = refs[10:]
+    counts_ref, *around = refs[:5]
+    own_ref, before = refs[5:7]
+    weights = refs[7:12]
+    refs = refs[12:]
     if last:
         read_in_ref, read_out_ref = refs[:2]
         refs = refs[2:]
@@ -313,7 +314,11 @@
     feats, edges, delta = refs[:4], refs[4:12], refs[12]
     delta[...] = jnp.zeros_like(delta)
     main, rest = slice(0, side_main), slice(side_main, side_span)
-    atoms = [ref[...].reshape(side_atoms, -1) for ref in (low, high)]
+    third = side_atoms // 3
+    atoms = []
+    for middle, outer in (around[:2], around[2:]):
+        rows = [ref.reshape(third, -1) for ref in (outer[0], middle[...], outer[1])]
+        atoms.append(jnp.concatenate(rows, axis=0))
     if layer == 0:
         total = []
         for q in range(2):
@@ -454,8 +459,8 @@
     )(*operands)
 
 
-def side_call(layer, last, counts, low, high, own, delta, weights, readout, kept):
-    operands = [counts, low, high, own, delta, *weights]
+def side_call(layer, last, counts, around, own, delta, weights, readout, kept):
+    operands = [counts, *around, own, delta, *weights]
     specs = [smem] + [vmem] * (len(operands) - 1)
     shapes, outs = (jax.ShapeDtypeStruct((2 * slots, 4 * chan), bf16),), (vmem,)
     if last:
@@ -584,7 +589,8 @@
             rin = radial_rows(radial_in, radial_bias)
             weights = [rin, radial_out, atom_in, atom_bias, atom_out]
         ys = [shifted(y, "gy", -1), y, shifted(y, "gy", 1)]
-        low, high = jnp.stack([v[1] for v in ys]), jnp.stack([v[0] for v in ys])
+        around = [shifted(y[1], "gx", -1), shifted(y[0], "gx", 1)]
+        low, high = (jnp.stack([ys[0][p], ys[2][p]]) for p in (1, 0))
         if layer == 0:
             pairs, order, more = geometry_call(counts, ys)
             low, high, pairs = lax.optimization_barrier((low, high, pairs))
@@ -592,13 +598,13 @@
         else:
             given = feature_call(layer, ys, weights, order)
             low, high, given = lax.optimization_barrier((low, high, given))
-        low, high = shifted(low, "gx", -1), shifted(high, "gx", 1)
+        around = [around[0], shifted(low, "gx", -1), around[1], shifted(high, "gx", 1)]
         delta, *kept = own_call(layer, counts, weights, given, pairs, more)
         if layer == 0:
             pairs, order = kept
         readout = [readout_in, readout_out[None, :]]
         state, *kept = side_call(
-            layer, last, counts, low, high, own, delta, weights, readout, side_kept
+            layer, last, counts, around, own, delta, weights, readout, side_kept
         )
         if last:
             vector_state, energy = kept

time: 94.5 us -> 93.9 us (level); the launches traced: 94.6 us -> 92.8 us
  waiting for transfers between devices: 23.8 us -> 6.9 us
  starting transfers between devices: 26.1 us -> 39 us
  Pallas kernels: 16.4 us -> 18.7 us
    ppermute x12 -> x16, waiting for transfers between devices: 23.8 us -> 6.9 us  [shifted(): lax.ppermute(value, axis, [((i + step) % count, i) for i in range(count)])]
    ppermute x12 -> x16, starting transfers between devices: 26.1 us -> 39 us  [shifted(): lax.ppermute(value, axis, [((i + step) % count, i) for i in range(count)])]
    pallas_call x2, Pallas kernels: 4.49 us -> 7.19 us  [own_call(): pl.pallas_call(functools.partial(own_kernel, layer), out_shape=shapes, in...]
  transfers between devices with their start and end apart: 12 -> 16, of which waited for: 9 -> 7; matrix products, arithmetic and copies ran while one was open for 4% -> 4% of each run, Pallas kernels for 5% -> 11%
where the time goes in v4:
time: 93.9 us; the launch traced here: 92.8 us
  starting transfers between devices  39 us (42%)
  blocking collectives  22.9 us (24%)
  Pallas kernels  18.7 us (20%)
  waiting for transfers between devices  6.9 us (7%)
  local copies, waits for them, and re-layouts  2.63 us (3%)
  other arithmetic  1.73 us (2%)
  between operations  0.97 us (1%)
    ppermute x16, starting transfers between devices, shifted(): lax.ppermute(value, axis, [((i + step) % count, i) for i in range(count)])  39 us
    all_to_all x1, blocking collectives, on_device(): every = lax.all_to_all(energy, ('gx', 'gy', 'gz'), 0, 0, tiled=True)  22.9 us
    pallas_call x2, Pallas kernels, own_call(): pl.pallas_call(functools.partial(own_kernel, layer), out_shape=shapes, in...  7.19 us
    pallas_call x2, Pallas kernels, side_call(): pl.pallas_call(functools.partial(side_kernel, layer, last), out_shape=sha...  7.11 us
    ppermute x16, waiting for transfers between devices, shifted(): lax.ppermute(value, axis, [((i + step) % count, i) for i in range(count)])  6.9 us
    pallas_call x1, Pallas kernels, geometry_call(): pl.pallas_call(geometry_kernel, out_shape=kept_shapes(own_span, (own_span...  2.29 us
    mul x6, local copies, waits for them, and re-layouts, radial_rows(): radial_in.transpose(0, 2, 1)[:, None, :, :, None] * eye[:, None, None, :]  2.13 us
  transfers between devices with their start and end apart: 16, of which 7 were waited for; matrix products, arithmetic and copies ran while one was open for 4% of the time, Pallas kernels for 11%

profile of v4, /device:TPU:1, one launch (start us, length us, event | category | flops | bytes accessed | tf_op | source)
XLA Modules:
  0.0 92.8 jit_solution(628837551340090580)
XLA Ops:
  0.6 1.1 %pack.1.refs_5_ = bf16[2,32,640]{2,1,0:T(8,128)(2,1)S(1)} custom-call(s32[2]{0:T(128)} %bitcast.56, f32[2,3,1,32]{3,2,1,0:T(1,128)} %bitcast.71, bf16[2,32,128]{2,1,0:T(8,128)(2,1)} %bitcast.69, bf16[2,3,32,128]{3,2,1,0:T(8,128)(2,1)} %bitcast.68), custom_call_target="tpu_custom_call" | custom-call | tf_op jit(solution)/shard_map/pack/pallas_call | solution.py:528
  1.7 2.1 %collective-permute-start = (bf16[2,32,640]{2,1,0:T(8,128)(2,1)S(1)}, bf16[2,32,640]{2,1,0:T(8,128)(2,1)S(1)}, u32[]{:S(2)}, u32[]{:S(2)}) collective-permute-start(bf16[2,32,640]{2,1,0:T(8,128)(2,1)S(1)} %pack.1.refs_5_), channel_id=1, source_target_pairs={{3,0},{0,1},{1,2},{2,3},{7,4},{4,5},{5,6},{6,7},{11,8},{8,9},{9,10... | collective-permute-start | bytes 245768 | tf_op jit(solution)/shard_map/ppermute | solution.py:545
  3.9 1.3 %collective-permute-start.1 = (bf16[2,32,640]{2,1,0:T(8,128)(2,1)S(1)}, bf16[2,32,640]{2,1,0:T(8,128)(2,1)S(1)}, u32[]{:S(2)}, u32[]{:S(2)}) collective-permute-start(bf16[2,32,640]{2,1,0:T(8,128)(2,1)S(1)} %pack.1.refs_5_), channel_id=1, source_target_pairs={{1,0},{2,1},{3,2},{0,3},{5,4},{6,5},{7,6},{4,7},{9,8},{10,9},{11,1... | collective-permute-start | bytes 245768 | tf_op jit(solution)/shard_map/ppermute | solution.py:545
  5.2 0.8 mul.31
  6.0 0.1 mul.32
  6.1 0.1 copy.37
  6.2 0.7 collective-permute-done
  7.0 0.2 collective-permute-done.1
  7.2 5.7 %collective-permute-start.3 = (bf16[2,3,32,640]{3,2,1,0:T(8,128)(2,1)S(1)}, bf16[2,3,32,640]{3,2,1,0:T(8,128)(2,1)S(1)}, u32[]{:S(2)}, u32[]{:S(2)}) collective-permute-start(bf16[2,3,32,640]{3,2,1,0:T(8,128)(2,1)S(1)} %pad_maximum_fusion.middle.refs_7_), channel_id=1, source_target_pairs={{12,0},{0,4},{4,8},{8,12},{13,1},{1,5},{5,9},{9,13},{14,2},{2,6},{... | collective-permute-start | bytes 737288 | tf_op jit(solution)/shard_map/ppermute | solution.py:545
  12.8 0.0 collective-permute-start.4
  12.9 0.7 fusion.6
  13.6 0.1 copy.39
  13.7 0.7 mul.29
  14.4 0.0 copy-start.3
  14.4 0.2 mul.30
  14.6 0.2 copy.38
  14.8 1.4 %collective-permute-start.2 = (bf16[3,32,640]{2,1,0:T(8,128)(2,1)S(1)}, bf16[3,32,640]{2,1,0:T(8,128)(2,1)S(1)}, u32[]{:S(2)}, u32[]{:S(2)}) collective-permute-start(bf16[3,32,640]{2,1,0:T(8,128)(2,1)S(1)} %get-tuple-element.71), channel_id=1, source_target_pairs={{112,0},{0,16},{16,32},{32,48},{48,64},{64,80},{80,96},{96,112},{1... | collective-permute-start | bytes 368648 | tf_op jit(solution)/shard_map/ppermute | solution.py:545
  16.2 2.3 %collective-permute-start.6 = (bf16[3,32,640]{2,1,0:T(8,128)(2,1)S(1)}, bf16[3,32,640]{2,1,0:T(8,128)(2,1)S(1)}, u32[]{:S(2)}, u32[]{:S(2)}) collective-permute-start(bf16[3,32,640]{2,1,0:T(8,128)(2,1)S(1)} %get-tuple-element.70), channel_id=1, source_target_pairs={{16,0},{32,16},{48,32},{64,48},{80,64},{96,80},{112,96},{0,112},{1... | collective-permute-start | bytes 368648 | tf_op jit(solution)/shard_map/ppermute | solution.py:545
  18.6 0.2 fusion.2.refs_1_.refs_7_
  18.8 2.4 %collective-permute-done.3.low.refs_6_ = bf16[2,3,32,640]{3,2,1,0:T(8,128)(2,1)S(1)} collective-permute-done((bf16[2,3,32,640]{3,2,1,0:T(8,128)(2,1)S(1)}, bf16[2,3,32,640]{3,2,1,0:T(8,128)(2,1)S(1)}, u32[]{:S(2)}, u32[]{:S(2)}) %collective-permute-start.3) | collective-permute-done | bytes 245792 | tf_op jit(solution)/shard_map/ppermute | solution.py:545
  21.3 0.3 collective-permute-done.4.high.refs_8_
  21.6 0.1 pad_maximum_fusion.1
  21.7 2.3 %geometry_part.1 = (f32[12,72,640]{2,1,0:T(8,128)S(1)}, bf16[640,576]{1,0:T(8,128)(2,1)S(1)}, s32[2]{0:T(128)S(1)}) custom-call(s32[2]{0:T(128)S(1)} %bitcast.57, bf16[2,3,32,640]{3,2,1,0:T(8,128)(2,1)S(1)} %collective-permute-done.3.low.refs_6_, bf16[2,3,32,640]{3,2,1,0:T(8,128)(2,1)S(1)} %pad_maximum_fusion.middle.refs_7_, ...), custom_call_target="tpu_custom_call" | custom-call | tf_op jit(solution)/shard_map/geometry_part/pallas_call | solution.py:420
  24.0 0.1 collective-permute-start.5
  24.1 3.6 %collective-permute-start.7 = (bf16[2,3,32,640]{3,2,1,0:T(8,128)(2,1)S(1)}, bf16[2,3,32,640]{3,2,1,0:T(8,128)(2,1)S(1)}, u32[]{:S(2)}, u32[]{:S(2)}) collective-permute-start(bf16[2,3,32,640]{3,2,1,0:T(8,128)(2,1)S(1)} %get-tuple-element.35), channel_id=1, source_target_pairs={{16,0},{32,16},{48,32},{64,48},{80,64},{96,80},{112,96},{0,112},{1... | collective-permute-start | bytes 737288 | tf_op jit(solution)/shard_map/ppermute | solution.py:545
  27.6 3.9 %own_part_0.1 = (f32[72,512]{1,0:T(8,128)S(1)}, f32[12,72,640]{2,1,0:T(8,128)}, bf16[640,576]{1,0:T(8,128)(2,1)}) custom-call(s32[2]{0:T(128)S(1)} %bitcast.58, bf16[2,512,80]{2,1,0:T(8,128)(2,1)S(1)} %fusion.2.refs_1_.refs_7_, bf16[2,64,512]{2,1,0:T(8,128)(2,1)S(1)} %copy-done.5, bf16[2,128,128]{2,1,0:T(8,128)(2,1)S(1)} %copy-done.2, ...), custom_call_target="tpu_custom_call" | custom-call | flops 6039797760 | bytes 4000000 | tf_op jit(solution)/shard_map/own_part_0/pallas_call | solution.py:450
  31.6 0.0 collective-permute-done.2.refs_1_
  31.6 0.0 collective-permute-done.6.refs_3_
  31.6 0.6 collective-permute-done.5.refs_2_
  32.2 4.0 %side_part_0.1 = (bf16[64,512]{1,0:T(8,128)(2,1)S(1)}, f32[12,72,384]{2,1,0:T(8,128)S(1)}, bf16[2,384,288]{2,1,0:T(8,128)(2,1)}, s32[2]{0:T(128)S(1)}) custom-call(s32[2]{0:T(128)S(1)} %bitcast.59, bf16[3,32,640]{2,1,0:T(8,128)(2,1)S(1)} %collective-permute-done.2.refs_1_, bf16[2,3,32,640]{3,2,1,0:T(8,128)(2,1)S(1)} %collective-permute-done.5.refs_2_, ...), custom_call_target="tpu_custom_call" | custom-call | flops 3019898880 | bytes 4000000 | tf_op jit(solution)/shard_map/side_part_0/pallas_call | solution.py:484
  36.2 1.3 %collective-permute-start.8 = (bf16[2,32,512]{2,1,0:T(8,128)(2,1)S(1)}, bf16[2,32,512]{2,1,0:T(8,128)(2,1)S(1)}, u32[]{:S(2)}, u32[]{:S(2)}) collective-permute-start(bf16[2,32,512]{2,1,0:T(8,128)(2,1)S(1)} %bitcast.52), channel_id=1, source_target_pairs={{3,0},{0,1},{1,2},{2,3},{7,4},{4,5},{5,6},{6,7},{11,8},{8,9},{9,10... | collective-permute-start | bytes 196616 | tf_op jit(solution)/shard_map/ppermute | solution.py:545
  37.5 1.6 %collective-permute-start.9 = (bf16[2,32,512]{2,1,0:T(8,128)(2,1)S(1)}, bf16[2,32,512]{2,1,0:T(8,128)(2,1)S(1)}, u32[]{:S(2)}, u32[]{:S(2)}) collective-permute-start(bf16[2,32,512]{2,1,0:T(8,128)(2,1)S(1)} %bitcast.53), channel_id=1, source_target_pairs={{1,0},{2,1},{3,2},{0,3},{5,4},{6,5},{7,6},{4,7},{9,8},{10,9},{11,1... | collective-permute-start | bytes 196616 | tf_op jit(solution)/shard_map/ppermute | solution.py:545
  39.0 0.1 copy.45.refs_12_
  39.2 2.3 %collective-permute-done.8 = bf16[2,32,512]{2,1,0:T(8,128)(2,1)S(1)} collective-permute-done((bf16[2,32,512]{2,1,0:T(8,128)(2,1)S(1)}, bf16[2,32,512]{2,1,0:T(8,128)(2,1)S(1)}, u32[]{:S(2)}, u32[]{:S(2)}) %collective-permute-start.8) | collective-permute-done | bytes 65568 | tf_op jit(solution)/shard_map/ppermute | solution.py:545
  41.5 0.0 collective-permute-done.9
  41.5 6.1 %collective-permute-start.11 = (bf16[2,3,32,512]{3,2,0,1:T(8,128)(2,1)S(1)}, bf16[2,3,32,512]{3,2,0,1:T(8,128)(2,1)S(1)}, u32[]{:S(2)}, u32[]{:S(2)}) collective-permute-start(bf16[2,3,32,512]{3,2,0,1:T(8,128)(2,1)S(1)} %pad_maximum_fusion.3), channel_id=1, source_target_pairs={{12,0},{0,4},{4,8},{8,12},{13,1},{1,5},{5,9},{9,13},{14,2},{2,6},{... | collective-permute-start | bytes 589832 | tf_op jit(solution)/shard_map/ppermute | solution.py:545
  47.7 0.1 collective-permute-start.10
  47.7 6.2 %collective-permute-start.14 = (bf16[3,32,512]{2,1,0:T(8,128)(2,1)S(1)}, bf16[3,32,512]{2,1,0:T(8,128)(2,1)S(1)}, u32[]{:S(2)}, u32[]{:S(2)}) collective-permute-start(bf16[3,32,512]{2,1,0:T(8,128)(2,1)S(1)} %get-tuple-element.76), channel_id=1, source_target_pairs={{16,0},{32,16},{48,32},{64,48},{80,64},{96,80},{112,96},{0,112},{1... | collective-permute-start | bytes 294920 | tf_op jit(solution)/shard_map/ppermute | solution.py:545
  53.9 0.0 collective-permute-done.11
  53.9 0.3 collective-permute-done.12
  54.3 1.0 %feature_part_1.1 = (bf16[640,512]{1,0:T(8,128)(2,1)S(1)}, bf16[640,256]{1,0:T(8,128)(2,1)S(1)}, bf16[640,256]{1,0:T(8,128)(2,1)S(1)}, bf16[640,256]{1,0:T(8,128)(2,1)S(1)}) custom-call(bf16[2,3,32,512]{3,2,1,0:T(8,128)(2,1)S(1)} %copy.40.low, bf16[2,3,32,512]{3,2,1,0:T(8,128)(2,1)S(1)} %copy.41.middle, bf16[2,3,32,512]{3,2,1,0:T(8,128)(2,1)S(1)} %copy.42.high, ...), custom_call_target="tpu_custom_call" | custom-call | tf_op jit(solution)/shard_map/feature_part_1/pallas_call | solution.py:431
  55.3 0.1 collective-permute-start.13
  55.4 7.3 %collective-permute-start.15 = (bf16[2,3,32,512]{3,2,0,1:T(8,128)(2,1)S(1)}, bf16[2,3,32,512]{3,2,0,1:T(8,128)(2,1)S(1)}, u32[]{:S(2)}, u32[]{:S(2)}) collective-permute-start(bf16[2,3,32,512]{3,2,0,1:T(8,128)(2,1)S(1)} %pad_maximum_fusion.5), channel_id=1, source_target_pairs={{16,0},{32,16},{48,32},{64,48},{80,64},{96,80},{112,96},{0,112},{1... | collective-permute-start | bytes 589832 | tf_op jit(solution)/shard_map/ppermute | solution.py:545
  62.7 3.3 %own_part_1.1.refs_6_ = f32[72,512]{1,0:T(8,128)S(1)} custom-call(s32[2]{0:T(128)S(1)} %bitcast.60, bf16[2,512,80]{2,1,0:T(8,128)(2,1)S(1)} %fusion.2.refs_1_.refs_7_, bf16[2,64,512]{2,1,0:T(8,128)(2,1)S(1)} %copy-done.5, bf16[2,128,128]{2,1,0:T(8,128)(2,1)S(1)} %copy-done.2, f32[2,128]{1,0:T(2,128)S(1)} %copy-done.4, bf16[2,128,512]{2,1,0:T(8,128)(2,1)S(1)} %copy-done.1, ...), custom_call_target="tpu_custom_call" | custom-call | flops 6039797760 | bytes 4000000 | tf_op jit(solution)/shard_map/own_part_1/pallas_call | solution.py:450
  66.0 0.0 collective-permute-done.13
  66.1 3.1 %side_part_1.1 = (bf16[2,32,128]{2,1,0:T(8,128)(2,1)}, bf16[2,3,32,128]{3,2,1,0:T(8,128)(2,1)}, f32[128,128]{1,0:T(8,128)S(1)}) custom-call(s32[2]{0:T(128)S(1)} %bitcast.61, bf16[3,32,512]{2,1,0:T(8,128)(2,1)S(1)} %collective-permute-done.10.refs_1_, bf16[2,3,32,512]{3,2,1,0:T(8,128)(2,1)S(1)} %copy.43.refs_2_, ...), custom_call_target="tpu_custom_call" | custom-call | flops 3019898880 | bytes 4000000 | tf_op jit(solution)/shard_map/side_part_1/pallas_call | solution.py:484
  69.2 22.9 %all_to_all.9 = f32[128,1,128]{2,1,0:T(1,128)S(1)} all-to-all(f32[128,1,128]{2,1,0:T(1,128)S(1)} %bitcast.51), channel_id=1, replica_groups=mesh['gx'=8,'gy'=4,'gz'=4] {'gx','gy','gz'}, dimensions={0} | all-to-all | bytes 131072 | tf_op jit(solution)/shard_map/all_to_all | solution.py:616
  92.1 0.7 reduce_sum.9
  (42 shorter events, 0.4 us)
Async XLA Ops:
  1.7 5.2 %collective-permute-start = (bf16[2,32,640]{2,1,0:T(8,128)(2,1)S(1)}, bf16[2,32,640]{2,1,0:T(8,128)(2,1)S(1)}, u32[]{:S(2)}, u32[]{:S(2)}) collective-permute-start(bf16[2,32,640]{2,1,0:T(8,128)(2,1)S(1)} %pack.1.refs_5_), channel_id=1, source_target_pairs={{3,0},{0,1},{1,2},{2,3},{7,4},{4,5},{5,6},{6,7},{11,8},{8,9},{9,10... | collective-permute-start | bytes 245768 | tf_op jit(solution)/shard_map/ppermute | solution.py:545
  3.9 3.3 %collective-permute-start.1 = (bf16[2,32,640]{2,1,0:T(8,128)(2,1)S(1)}, bf16[2,32,640]{2,1,0:T(8,128)(2,1)S(1)}, u32[]{:S(2)}, u32[]{:S(2)}) collective-permute-start(bf16[2,32,640]{2,1,0:T(8,128)(2,1)S(1)} %pack.1.refs_5_), channel_id=1, source_target_pairs={{1,0},{2,1},{3,2},{0,3},{5,4},{6,5},{7,6},{4,7},{9,8},{10,9},{11,1... | collective-permute-start | bytes 245768 | tf_op jit(solution)/shard_map/ppermute | solution.py:545
  7.2 14.0 %collective-permute-start.3 = (bf16[2,3,32,640]{3,2,1,0:T(8,128)(2,1)S(1)}, bf16[2,3,32,640]{3,2,1,0:T(8,128)(2,1)S(1)}, u32[]{:S(2)}, u32[]{:S(2)}) collective-permute-start(bf16[2,3,32,640]{3,2,1,0:T(8,128)(2,1)S(1)} %pad_maximum_fusion.middle.refs_7_), channel_id=1, source_target_pairs={{12,0},{0,4},{4,8},{8,12},{13,1},{1,5},{5,9},{9,13},{14,2},{2,6},{... | collective-permute-start | bytes 737288 | tf_op jit(solution)/shard_map/ppermute | solution.py:545
  12.8 8.7 %collective-permute-start.4 = (bf16[2,3,32,640]{3,2,1,0:T(8,128)(2,1)S(1)}, bf16[2,3,32,640]{3,2,1,0:T(8,128)(2,1)S(1)}, u32[]{:S(2)}, u32[]{:S(2)}) collective-permute-start(bf16[2,3,32,640]{3,2,1,0:T(8,128)(2,1)S(1)} %pad_maximum_fusion.middle.refs_7_), channel_id=1, source_target_pairs={{4,0},{8,4},{12,8},{0,12},{5,1},{9,5},{13,9},{1,13},{6,2},{10,6},{... | collective-permute-start | bytes 737288 | tf_op jit(solution)/shard_map/ppermute | solution.py:545
  14.4 7.3 %copy-start.3 = (s32[2,1,1]{0,2,1:T(1,128)S(1)}, s32[2,1,1]{0,2,1:T(1,128)}, u32[]{:S(2)}) copy-start(s32[2,1,1]{0,2,1:T(1,128)} %param.14) | copy-start | bytes 28
  14.8 16.8 %collective-permute-start.2 = (bf16[3,32,640]{2,1,0:T(8,128)(2,1)S(1)}, bf16[3,32,640]{2,1,0:T(8,128)(2,1)S(1)}, u32[]{:S(2)}, u32[]{:S(2)}) collective-permute-start(bf16[3,32,640]{2,1,0:T(8,128)(2,1)S(1)} %get-tuple-element.71), channel_id=1, source_target_pairs={{112,0},{0,16},{16,32},{32,48},{48,64},{64,80},{80,96},{96,112},{1... | collective-permute-start | bytes 368648 | tf_op jit(solution)/shard_map/ppermute | solution.py:545
  16.2 11.4 %copy-start.1 = (bf16[2,128,512]{2,1,0:T(8,128)(2,1)S(1)}, bf16[2,128,512]{2,1,0:T(8,128)(2,1)}, u32[]{:S(2)}) copy-start(bf16[2,128,512]{2,1,0:T(8,128)(2,1)} %refs_11_.3) | copy-start | bytes 786436
  16.2 11.4 %copy-start.2 = (bf16[2,128,128]{2,1,0:T(8,128)(2,1)S(1)}, bf16[2,128,128]{2,1,0:T(8,128)(2,1)}, u32[]{:S(2)}) copy-start(bf16[2,128,128]{2,1,0:T(8,128)(2,1)} %refs_9_.3) | copy-start | bytes 196612
  16.2 11.4 %copy-start.4 = (f32[2,128]{1,0:T(2,128)S(1)}, f32[2,128]{1,0:T(2,128)}, u32[]{:S(2)}) copy-start(f32[2,128]{1,0:T(2,128)} %refs_10_.3) | copy-start | bytes 3076
  16.2 11.4 %copy-start.5 = (bf16[2,64,512]{2,1,0:T(8,128)(2,1)S(1)}, bf16[2,64,512]{2,1,0:T(8,128)(2,1)}, u32[]{:S(2)}) copy-start(bf16[2,64,512]{2,1,0:T(8,128)(2,1)} %refs_8_.3) | copy-start | bytes 393220
  16.2 15.4 %collective-permute-start.6 = (bf16[3,32,640]{2,1,0:T(8,128)(2,1)S(1)}, bf16[3,32,640]{2,1,0:T(8,128)(2,1)S(1)}, u32[]{:S(2)}, u32[]{:S(2)}) collective-permute-start(bf16[3,32,640]{2,1,0:T(8,128)(2,1)S(1)} %get-tuple-element.70), channel_id=1, source_target_pairs={{16,0},{32,16},{48,32},{64,48},{80,64},{96,80},{112,96},{0,112},{1... | collective-permute-start | bytes 368648 | tf_op jit(solution)/shard_map/ppermute | solution.py:545
  24.0 8.2 %collective-permute-start.5 = (bf16[2,3,32,640]{3,2,1,0:T(8,128)(2,1)S(1)}, bf16[2,3,32,640]{3,2,1,0:T(8,128)(2,1)S(1)}, u32[]{:S(2)}, u32[]{:S(2)}) collective-permute-start(bf16[2,3,32,640]{3,2,1,0:T(8,128)(2,1)S(1)} %get-tuple-element.34), channel_id=1, source_target_pairs={{112,0},{0,16},{16,32},{32,48},{48,64},{64,80},{80,96},{96,112},{1... | collective-permute-start | bytes 737288 | tf_op jit(solution)/shard_map/ppermute | solution.py:545
  24.1 8.1 %collective-permute-start.7 = (bf16[2,3,32,640]{3,2,1,0:T(8,128)(2,1)S(1)}, bf16[2,3,32,640]{3,2,1,0:T(8,128)(2,1)S(1)}, u32[]{:S(2)}, u32[]{:S(2)}) collective-permute-start(bf16[2,3,32,640]{3,2,1,0:T(8,128)(2,1)S(1)} %get-tuple-element.35), channel_id=1, source_target_pairs={{16,0},{32,16},{48,32},{64,48},{80,64},{96,80},{112,96},{0,112},{1... | collective-permute-start | bytes 737288 | tf_op jit(solution)/shard_map/ppermute | solution.py:545
  32.2 6.8 %copy-start.9 = (bf16[128,64]{0,1:T(8,128)(2,1)S(1)}, bf16[128,64]{0,1:T(8,128)(2,1)}, u32[]{:S(2)}) copy-start(bf16[128,64]{0,1:T(8,128)(2,1)} %param.23) | copy-start | bytes 49156
  36.2 18.1 %copy-start = (bf16[640,576]{1,0:T(8,128)(2,1)S(1)}, bf16[640,576]{1,0:T(8,128)(2,1)}, u32[]{:S(2)}) copy-start(bf16[640,576]{1,0:T(8,128)(2,1)} %get-tuple-element.43.order) | copy-start | bytes 2211844
  36.2 5.3 %collective-permute-start.8 = (bf16[2,32,512]{2,1,0:T(8,128)(2,1)S(1)}, bf16[2,32,512]{2,1,0:T(8,128)(2,1)S(1)}, u32[]{:S(2)}, u32[]{:S(2)}) collective-permute-start(bf16[2,32,512]{2,1,0:T(8,128)(2,1)S(1)} %bitcast.52), channel_id=1, source_target_pairs={{3,0},{0,1},{1,2},{2,3},{7,4},{4,5},{5,6},{6,7},{11,8},{8,9},{9,10... | collective-permute-start | bytes 196616 | tf_op jit(solution)/shard_map/ppermute | solution.py:545
  37.5 4.0 %collective-permute-start.9 = (bf16[2,32,512]{2,1,0:T(8,128)(2,1)S(1)}, bf16[2,32,512]{2,1,0:T(8,128)(2,1)S(1)}, u32[]{:S(2)}, u32[]{:S(2)}) collective-permute-start(bf16[2,32,512]{2,1,0:T(8,128)(2,1)S(1)} %bitcast.53), channel_id=1, source_target_pairs={{1,0},{2,1},{3,2},{0,3},{5,4},{6,5},{7,6},{4,7},{9,8},{10,9},{11,1... | collective-permute-start | bytes 196616 | tf_op jit(solution)/shard_map/ppermute | solution.py:545
  41.5 12.4 %collective-permute-start.11 = (bf16[2,3,32,512]{3,2,0,1:T(8,128)(2,1)S(1)}, bf16[2,3,32,512]{3,2,0,1:T(8,128)(2,1)S(1)}, u32[]{:S(2)}, u32[]{:S(2)}) collective-permute-start(bf16[2,3,32,512]{3,2,0,1:T(8,128)(2,1)S(1)} %pad_maximum_fusion.3), channel_id=1, source_target_pairs={{12,0},{0,4},{4,8},{8,12},{13,1},{1,5},{5,9},{9,13},{14,2},{2,6},{... | collective-permute-start | bytes 589832 | tf_op jit(solution)/shard_map/ppermute | solution.py:545
  47.6 6.6 %collective-permute-start.12 = (bf16[2,3,32,512]{3,2,0,1:T(8,128)(2,1)S(1)}, bf16[2,3,32,512]{3,2,0,1:T(8,128)(2,1)S(1)}, u32[]{:S(2)}, u32[]{:S(2)}) collective-permute-start(bf16[2,3,32,512]{3,2,0,1:T(8,128)(2,1)S(1)} %pad_maximum_fusion.3), channel_id=1, source_target_pairs={{4,0},{8,4},{12,8},{0,12},{5,1},{9,5},{13,9},{1,13},{6,2},{10,6},{... | collective-permute-start | bytes 589832 | tf_op jit(solution)/shard_map/ppermute | solution.py:545
  47.6 15.1 %copy-start.8 = (f32[12,72,640]{2,1,0:T(8,128)S(1)}, f32[12,72,640]{2,1,0:T(8,128)}, u32[]{:S(2)}) copy-start(f32[12,72,640]{2,1,0:T(8,128)} %get-tuple-element.54.refs_10_) | copy-start | bytes 6635524
  47.7 18.4 %collective-permute-start.10 = (bf16[3,32,512]{2,1,0:T(8,128)(2,1)S(1)}, bf16[3,32,512]{2,1,0:T(8,128)(2,1)S(1)}, u32[]{:S(2)}, u32[]{:S(2)}) collective-permute-start(bf16[3,32,512]{2,1,0:T(8,128)(2,1)S(1)} %get-tuple-element.77), channel_id=1, source_target_pairs={{112,0},{0,16},{16,32},{32,48},{48,64},{64,80},{80,96},{96,112},{1... | collective-permute-start | bytes 294920 | tf_op jit(solution)/shard_map/ppermute | solution.py:545
  47.7 18.3 %collective-permute-start.14 = (bf16[3,32,512]{2,1,0:T(8,128)(2,1)S(1)}, bf16[3,32,512]{2,1,0:T(8,128)(2,1)S(1)}, u32[]{:S(2)}, u32[]{:S(2)}) collective-permute-start(bf16[3,32,512]{2,1,0:T(8,128)(2,1)S(1)} %get-tuple-element.76), channel_id=1, source_target_pairs={{16,0},{32,16},{48,32},{64,48},{80,64},{96,80},{112,96},{0,112},{1... | collective-permute-start | bytes 294920 | tf_op jit(solution)/shard_map/ppermute | solution.py:545
  55.3 10.7 %collective-permute-start.13 = (bf16[2,3,32,512]{3,2,0,1:T(8,128)(2,1)S(1)}, bf16[2,3,32,512]{3,2,0,1:T(8,128)(2,1)S(1)}, u32[]{:S(2)}, u32[]{:S(2)}) collective-permute-start(bf16[2,3,32,512]{3,2,0,1:T(8,128)(2,1)S(1)} %pad_maximum_fusion.4), channel_id=1, source_target_pairs={{112,0},{0,16},{16,32},{32,48},{48,64},{64,80},{80,96},{96,112},{1... | collective-permute-start | bytes 589832 | tf_op jit(solution)/shard_map/ppermute | solution.py:545
  55.4 10.6 %collective-permute-start.15 = (bf16[2,3,32,512]{3,2,0,1:T(8,128)(2,1)S(1)}, bf16[2,3,32,512]{3,2,0,1:T(8,128)(2,1)S(1)}, u32[]{:S(2)}, u32[]{:S(2)}) collective-permute-start(bf16[2,3,32,512]{3,2,0,1:T(8,128)(2,1)S(1)} %pad_maximum_fusion.5), channel_id=1, source_target_pairs={{16,0},{32,16},{48,32},{64,48},{80,64},{96,80},{112,96},{0,112},{1... | collective-permute-start | bytes 589832 | tf_op jit(solution)/shard_map/ppermute | solution.py:545
  62.7 3.4 %copy-start.6 = (f32[64]{0:T(128)S(1)}, f32[64]{0:T(128)}, u32[]{:S(2)}) copy-start(f32[64]{0:T(128)} %param.24) | copy-start | bytes 772
  62.7 3.4 %copy-start.7 = (bf16[2,384,288]{2,1,0:T(8,128)(2,1)S(1)}, bf16[2,384,288]{2,1,0:T(8,128)(2,1)}, u32[]{:S(2)}) copy-start(bf16[2,384,288]{2,1,0:T(8,128)(2,1)} %get-tuple-element.56.refs_15_) | copy-start | bytes 1327108
